TPU v7x, 512 devices: a whole 4x4x16 slice. The times are simulated.
512 devices in a mesh: frame: 32 (over z, core), head: 16 (over x, y).
Axes of the slice: x: 4, y: 4, z: 16, core: 2. Of those that a mesh axis runs over, the one named last changes fastest.
Arguments:
- queries: bfloat16 [16384, 4096], P('frame', 'head'), may hold values from -6 to 6
- key_rows: bfloat16 [16384, 4096], P('frame', 'head'), may hold values from -6 to 6
- values: bfloat16 [16384, 4096], P('frame', 'head'), may hold values from -6 to 6
- gate_init: float32 [32, 128, 128], P('head'), may hold values from -0.5 to 0.5
- up_init: float32 [32, 128, 128], P('head'), may hold values from -0.5 to 0.5
- down_init: float32 [32, 128, 128], P('head'), may hold values from -0.5 to 0.5
- step_size: float32 [32], P('head'), may hold values from 0.1 to 1
- head_scale: float32 [32], P('head'), may hold values from 0.25 to 4
- out_gain: float32 [4096], P('head'), may hold values from 0.5 to 1.5
Outputs:
- layer_out: bfloat16 [16384, 4096], P('frame', 'head')
All inputs are finite; a program needn't handle non-finite values.
Results may differ from a plain program's by a relative error of at most 0.012.
The roundings to bfloat16 on the way count: a program that leaves them out, or rounds other values in their place, can miss the bound.
Values may be sent and summed in bfloat16 or wider, within the bound.
No kernel may reach another device: no remote copies, remote signals or barrier semaphores. Data moves between devices by JAX's collectives and lax.ppermute only.
A program may use at most 64 MiB of HBM per device.

v0:
```python
import math

import jax
import jax.numpy as jnp
from jax import lax
from jax.sharding import PartitionSpec as P

NS_ITERS = 5
GROUPS = 2


quintic_terms = (3.4445, -4.775, 2.0315)
highest = lax.Precision.HIGHEST


def from_behind(block, axis, distance):
    devices = range(lax.axis_size(axis))
    route = [(i - distance, i) for i in devices if i - distance in devices]
    return lax.ppermute(block, axis, route)


def rms_scale(rows_in, epsilon):
    mean_square = jnp.mean(rows_in * rows_in, axis=-1, keepdims=True)
    return rows_in * lax.rsqrt(mean_square + epsilon)


def newton_schulz(gradient):
    flipped = gradient.shape[1] > gradient.shape[2]
    matrix = gradient
    frobenius = jnp.sqrt(jnp.sum(matrix * matrix, axis=(1, 2), keepdims=True))
    matrix = matrix / (frobenius + 1e-07)
    for repeat_no in range(NS_ITERS):
        square = jnp.einsum("hij,hkj->hik", matrix, matrix, precision=highest)
        quartic = jnp.einsum("hij,hjk->hik", square, square, precision=highest)
        mixing = quintic_terms[1] * square + quintic_terms[2] * quartic
        matrix = quintic_terms[0] * matrix + jnp.einsum(
            "hij,hjk->hik", mixing, matrix, precision=highest
        )
    return matrix


def column_norms(weight):
    return jnp.sqrt(jnp.sum(weight * weight, axis=1, keepdims=True))


def fast_grads(weights, key_part, value_part):
    gate_w, up_w, down_w = weights
    key_f = key_part.astype(jnp.float32)
    value_f = value_part.astype(jnp.float32)
    gate = jnp.einsum("nhd,hdf->nhf", key_f, gate_w, precision=highest)
    upward = jnp.einsum("nhd,hdf->nhf", key_f, up_w, precision=highest)
    sigma = jax.nn.sigmoid(gate)
    active = gate * sigma
    hidden = active * upward
    back_hidden = -jnp.einsum("nhd,hfd->nhf", value_f, down_w, precision=highest)
    grad_down = -jnp.einsum("nhf,nhd->hfd", hidden, value_f, precision=highest)
    back_gate = back_hidden * upward * sigma * (1.0 + gate * (1.0 - sigma))
    back_up = back_hidden * active
    grad_gate = jnp.einsum("nhd,nhf->hdf", key_f, back_gate, precision=highest)
    grad_up = jnp.einsum("nhd,nhf->hdf", key_f, back_up, precision=highest)
    return (grad_gate, grad_up, grad_down)


def summed(gradients):
    return lax.psum((gradients[0], gradients[1], gradients[2]), "frame")


def orthogonal(gradients):
    return tuple((newton_schulz(gradient) for gradient in gradients))


def renewed(weights, gradients, step_size, targets):
    result = []
    for weight, ortho, target in zip(weights, orthogonal(gradients), targets):
        moved = weight - step_size[:, None, None] * ortho
        length = jnp.sqrt(jnp.sum(moved * moved, axis=1, keepdims=True))
        result.append(moved * (target / (length + 1e-06)))
    return tuple(result)


def fast_apply(weights, query_part, head_scale):
    gate_w, up_w, down_w = weights
    query_f = query_part.astype(jnp.float32)
    gate = jnp.einsum("nhd,hdf->nhf", query_f, gate_w, precision=highest)
    upward = jnp.einsum("nhd,hdf->nhf", query_f, up_w, precision=highest)
    hidden = jax.nn.silu(gate) * upward
    output = jnp.einsum("nhf,hfd->nhd", hidden, down_w, precision=highest)
    return (output * head_scale[None, :, None]).astype(jnp.bfloat16)


def attend(queries, keys_here, values_here, keys_prev, values_prev, is_first, heads_dev, head_dim):
    frame_len = queries.shape[0]
    score_scale = 1.0 / math.sqrt(head_dim)
    rows_per = frame_len
    while rows_per > 1024 and rows_per % 2 == 0:
        rows_per = rows_per // 2
    blocks = frame_len // rows_per
    column = lax.broadcasted_iota(jnp.int32, (1, 2 * frame_len), 1)
    masked = jnp.logical_and(is_first, column < frame_len)
    outputs = []
    for head_no in range(heads_dev):
        lower = head_no * head_dim
        upper = lower + head_dim
        key_all = jnp.concatenate([keys_prev[:, lower:upper], keys_here[:, lower:upper]], axis=0)
        value_all = jnp.concatenate(
            [values_prev[:, lower:upper], values_here[:, lower:upper]], axis=0
        )
        query_blocks = queries[:, lower:upper].reshape(blocks, rows_per, head_dim)

        def one_block(query_part):
            scores = (
                jnp.einsum("qd,kd->qk", query_part, key_all, preferred_element_type=jnp.float32)
                * score_scale
            )
            scores = jnp.where(masked, -1e30, scores)
            probs = jax.nn.softmax(scores, axis=-1).astype(jnp.bfloat16)
            mixed = jnp.dot(probs, value_all, preferred_element_type=jnp.float32)
            return rms_scale(mixed, 1e-06).astype(jnp.bfloat16)

        outputs.append(lax.map(one_block, query_blocks).reshape(frame_len, head_dim))
    return jnp.concatenate(outputs, axis=1)


def shards(
    queries, key_rows, values, gate_init, up_init, down_init, step_size, head_scale, out_gain
):
    frame_len, width = queries.shape
    heads_dev = gate_init.shape[0]
    head_dim = gate_init.shape[1]
    keys_prev, values_prev = from_behind((key_rows, values), "frame", 1)
    position = lax.axis_index("frame")
    attended = attend(
        queries, key_rows, values, keys_prev, values_prev, position == 0, heads_dev, head_dim
    )
    query_norm = rms_scale(
        queries.astype(jnp.float32).reshape(frame_len, heads_dev, head_dim), 1e-06
    ).astype(jnp.bfloat16)
    frames_count = lax.axis_size("frame")
    half = frames_count // GROUPS
    weights = (gate_init, up_init, down_init)
    targets = tuple((column_norms(weight) for weight in weights))
    depth = frame_len // frames_count
    dealt = (
        lax.all_to_all(
            attended.reshape(depth, frames_count, width),
            "frame",
            split_axis=1,
            concat_axis=1,
            tiled=True,
        ),
        lax.all_to_all(
            query_norm.reshape(depth, frames_count, width),
            "frame",
            split_axis=1,
            concat_axis=1,
            tiled=True,
        ),
        lax.all_to_all(
            values.reshape(depth, frames_count, width),
            "frame",
            split_axis=1,
            concat_axis=1,
            tiled=True,
        ),
    )
    pieces = []
    for segment in range(GROUPS):
        lower = segment * half
        upper = lower + half
        picked = [
            member[:, lower:upper].reshape(depth * half, heads_dev, head_dim) for member in dealt
        ]
        weights = renewed(
            weights, summed(fast_grads(weights, picked[0], picked[2])), step_size, targets
        )
        pieces.append(fast_apply(weights, picked[1], head_scale).reshape(depth, half, width))
    assembled = jnp.concatenate(pieces, axis=1)
    fast_out = lax.all_to_all(assembled, "frame", split_axis=1, concat_axis=1, tiled=True).reshape(
        frame_len, width
    )
    combined = attended.astype(jnp.float32) + fast_out.astype(jnp.float32)
    local_sum = jnp.sum(combined * combined, axis=1)
    total = lax.psum(local_sum, "head")
    features = width * lax.axis_size("head")
    scaled = combined * lax.rsqrt(total / features + 1e-05)[:, None] * out_gain[None, :]
    return scaled.astype(jnp.bfloat16)


def solution(mesh):
    in_specs = (
        P("frame", "head"),
        P("frame", "head"),
        P("frame", "head"),
        P("head", None, None),
        P("head", None, None),
        P("head", None, None),
        P("head"),
        P("head"),
        P("head"),
    )
    out_specs = P("frame", "head")
    return jax.shard_map(shards, mesh=mesh, in_specs=in_specs, out_specs=out_specs, check_vma=False)
```

profile of v0, /device:TPU:1, one launch (start us, length us, event | category | flops | bytes accessed | tf_op | source)
XLA Modules:
  0.0 607.0 jit_solution(17275909676013510593)
XLA Ops:
  6.5 4.9 collective-permute-start
  11.5 1.9 collective-permute-start.1
  13.4 1.8 copy.306
  15.2 14.8 %all-to-all-start.1 = ((bf16[16,32,256]{2,0,1:T(8,128)(2,1)}), bf16[16,32,256]{2,0,1:T(8,128)(2,1)S(1)}, u32[]{:S(2)}, u32[]{:S(2)}) async-start(bf16[16,32,256]{2,0,1:T(8,128)(2,1)} %copy.306), calls=%async_computation.1 | async-start | bytes 524288 | tf_op jit(solution)/shard_map/all_to_all | solution.py:158
  30.0 1.0 fusion.156
  31.0 1.0 convert_multiply_fusion
  32.3 0.6 reduce_sum.205
  33.0 0.6 mul.610
  33.6 0.4 mul.611
  34.1 0.4 fusion.59
  34.6 0.7 fusion.1
  35.3 0.9 fusion.3
  36.2 1.0 multiply_reduce_fusion.1
  37.3 1.0 multiply_reduce_fusion.2
  38.4 0.7 copy_dynamic-update-slice_fusion.1
  39.3 0.7 copy_dynamic-update-slice_fusion
  40.0 12.0 %all-to-all-done.1 = bf16[16,32,256]{2,0,1:T(8,128)(2,1)S(1)} async-done(((bf16[16,32,256]{2,0,1:T(8,128)(2,1)}), bf16[16,32,256]{2,0,1:T(8,128)(2,1)S(1)}, u32[]{:S(2)}, u32[]{:S(2)}) %all-to-all-start.1) | async-done | bytes 262176 | tf_op jit(solution)/shard_map/all_to_all | solution.py:158
  52.0 4.5 all-to-all-start
  56.6 0.8 copy.315
  58.0 20.6 %all-to-all-done = bf16[16,32,256]{2,0,1:T(8,128)(2,1)S(1)} async-done(((bf16[16,32,256]{2,0,1:T(8,128)(2,1)}), bf16[16,32,256]{2,0,1:T(8,128)(2,1)S(1)}, u32[]{:S(2)}, u32[]{:S(2)}) %all-to-all-start) | async-done | bytes 262176 | tf_op jit(solution)/shard_map/all_to_all | solution.py:144
  78.6 4.7 all-to-all-start.2
  84.2 1.0 fusion.84
  85.2 1.1 convolution_negate_fusion.3
  86.3 1.0 fusion.86
  87.6 17.7 %all-to-all-done.2 = bf16[16,32,256]{2,0,1:T(8,128)(2,1)S(1)} async-done(((bf16[16,32,256]{2,0,1:T(8,128)(2,1)}), bf16[16,32,256]{2,0,1:T(8,128)(2,1)S(1)}, u32[]{:S(2)}, u32[]{:S(2)}) %all-to-all-start.2) | async-done | bytes 262176 | tf_op jit(solution)/shard_map/all_to_all | solution.py:151
  105.8 183.2 %all-reduce.7.cloned.1.call-done = (f32[2,128,128]{2,1,0:T(8,128)}, f32[2,128,128]{2,1,0:T(8,128)}, f32[2,128,128]{2,1,0:T(8,128)}) async-done(((f32[2,128,128]{2,1,0:T(8,128)}, f32[2,128,128]{2,1,0:T(8,128)}, f32[2,128,128]{2,1,0:T(8,128)}), (f32[2,128,128]{2,1,0:T(8,128)}, f32[2,128,128]{2,1,0:T(8,128)}, f32[2,128,128]{2,1,0:T(8,128)})) %all-reduce.7.cloned.1.call-update) | async-done | bytes 393232 | tf_op jit(solution)/shard_map/psum | solution.py:65
  289.0 1.1 multiply_reduce_fusion.11
  290.1 1.5 fusion.130
  291.8 1.3 convolution_add_fusion.24
  293.1 0.4 fusion.161
  294.1 0.4 fusion.162
  296.0 0.4 fusion.164
  296.7 0.5 fusion.131
  297.8 0.4 fusion.165
  298.7 0.4 fusion.166
  299.7 0.4 fusion.167
  300.6 0.4 fusion.168
  302.0 0.5 fusion.129
  303.1 0.4 fusion.157
  304.1 0.4 fusion.158
  305.0 0.4 fusion.159
  306.0 0.4 fusion.160
  307.7 1.1 convolution_negate_fusion.2
  309.0 1.0 fusion.73
  310.1 1.1 fusion.75
  311.7 0.4 fusion.11
  312.6 199.6 %all-reduce.5.cloned.1.call-done = (f32[2,128,128]{2,1,0:T(8,128)}, f32[2,128,128]{2,1,0:T(8,128)}, f32[2,128,128]{2,1,0:T(8,128)}) async-done(((f32[2,128,128]{2,1,0:T(8,128)}, f32[2,128,128]{2,1,0:T(8,128)}, f32[2,128,128]{2,1,0:T(8,128)}), (f32[2,128,128]{2,1,0:T(8,128)}, f32[2,128,128]{2,1,0:T(8,128)}, f32[2,128,128]{2,1,0:T(8,128)})) %all-reduce.5.cloned.1.call-update) | async-done | bytes 393232 | tf_op jit(solution)/shard_map/psum | solution.py:65
  512.2 1.0 multiply_reduce_fusion.8
  513.2 1.5 fusion.132
  514.9 1.3 convolution_add_fusion.14
  516.3 0.4 fusion.169
  519.1 0.4 fusion.172
  520.2 0.5 fusion.134
  521.3 0.4 fusion.177
  522.3 0.4 fusion.178
  524.2 0.4 fusion.180
  525.3 0.5 fusion.133
  526.4 0.4 fusion.173
  528.3 0.4 fusion.175
  530.8 0.4 fusion.10
  531.7 33.2 %all_to_all.20 = bf16[16,32,256]{2,0,1:T(8,128)(2,1)S(1)} all-to-all(bf16[16,32,256]{2,0,1:T(8,128)(2,1)S(1)} %copy.349), channel_id=1, replica_groups=mesh['frame'=32,'head'=16] {'frame'}, dimensions={1} | all-to-all | bytes 524288 | tf_op jit(solution)/shard_map/all_to_all | solution.py:178
  564.8 1.1 multiply_reduce_fusion
  566.1 33.1 %psum.55 = f32[512]{0:T(512)S(1)} all-reduce(f32[512]{0:T(512)S(1)} %reduce_sum.216), channel_id=1, replica_groups=mesh['frame'=32,'head'=16] {'head'}, use_global_device_ids=true, to_apply=%region_29.30 | all-reduce | flops 512 | bytes 4096 | tf_op jit(solution)/shard_map/psum | solution.py:183
  599.3 0.8 fusion.58
  (160 shorter events, 24.8 us)
Async XLA Ops:
  6.5 27.6 %collective-permute-start = (bf16[512,256]{1,0:T(8,128)(2,1)}, bf16[512,256]{1,0:T(8,128)(2,1)S(1)}, u32[]{:S(2)}, u32[]{:S(2)}) collective-permute-start(bf16[512,256]{1,0:T(8,128)(2,1)} %param.10), channel_id=1, source_target_pairs={{0,16},{16,32},{32,48},{48,64},{64,80},{80,96},{96,112},{112,128},... | collective-permute-start | bytes 786440 | tf_op jit(solution)/shard_map/ppermute | solution.py:19
  11.5 24.7 %collective-permute-start.1 = (bf16[512,256]{1,0:T(8,128)(2,1)}, bf16[512,256]{1,0:T(8,128)(2,1)S(1)}, u32[]{:S(2)}, u32[]{:S(2)}) collective-permute-start(bf16[512,256]{1,0:T(8,128)(2,1)} %param.11), channel_id=1, source_target_pairs={{0,16},{16,32},{32,48},{48,64},{64,80},{80,96},{96,112},{112,128},... | collective-permute-start | bytes 786440 | tf_op jit(solution)/shard_map/ppermute | solution.py:19
  15.2 36.8 %all-to-all-start.1 = ((bf16[16,32,256]{2,0,1:T(8,128)(2,1)}), bf16[16,32,256]{2,0,1:T(8,128)(2,1)S(1)}, u32[]{:S(2)}, u32[]{:S(2)}) async-start(bf16[16,32,256]{2,0,1:T(8,128)(2,1)} %copy.306), calls=%async_computation.1 | async-start | bytes 524288 | tf_op jit(solution)/shard_map/all_to_all | solution.py:158
  32.0 2.0 copy-start.4
  32.3 1.8 copy-start
  38.3 19.2 %copy-start.1 = (f32[2,128,128]{2,1,0:T(8,128)S(1)}, f32[2,128,128]{2,1,0:T(8,128)}, u32[]{:S(2)}) copy-start(f32[2,128,128]{2,1,0:T(8,128)} %param.12) | copy-start | bytes 393220
  38.3 19.3 %copy-start.2 = (f32[2,128,128]{2,1,0:T(8,128)S(1)}, f32[2,128,128]{2,1,0:T(8,128)}, u32[]{:S(2)}) copy-start(f32[2,128,128]{2,1,0:T(8,128)} %param.13) | copy-start | bytes 393220
  38.3 19.3 %copy-start.3 = (f32[2,128,128]{2,1,0:T(8,128)S(1)}, f32[2,128,128]{2,1,0:T(8,128)}, u32[]{:S(2)}) copy-start(f32[2,128,128]{2,1,0:T(8,128)} %param.14) | copy-start | bytes 393220
  52.0 26.5 %all-to-all-start = ((bf16[16,32,256]{2,0,1:T(8,128)(2,1)}), bf16[16,32,256]{2,0,1:T(8,128)(2,1)S(1)}, u32[]{:S(2)}, u32[]{:S(2)}) async-start(bf16[16,32,256]{2,0,1:T(8,128)(2,1)} %copy_dynamic-update-slice_fusion), calls=%async_computation | async-start | bytes 524288 | tf_op jit(solution)/shard_map/all_to_all | solution.py:144
  78.6 26.7 %all-to-all-start.2 = ((bf16[16,32,256]{2,0,1:T(8,128)(2,1)}), bf16[16,32,256]{2,0,1:T(8,128)(2,1)S(1)}, u32[]{:S(2)}, u32[]{:S(2)}) async-start(bf16[16,32,256]{2,0,1:T(8,128)(2,1)} %copy.315), calls=%async_computation.2 | async-start | bytes 524288 | tf_op jit(solution)/shard_map/all_to_all | solution.py:151
  83.2 205.7 %all-reduce.7.cloned.1.call-start = ((), (), s32[]{:S(2)}) async-start(), calls=%async_computation.5 | async-start | bytes 786432 | tf_op jit(solution)/shard_map/psum | solution.py:65
  87.4 424.8 %all-reduce.5.cloned.1.call-start = ((), (), s32[]{:S(2)}) async-start(), calls=%async_computation.4 | async-start | bytes 786432 | tf_op jit(solution)/shard_map/psum | solution.py:65
  293.1 3.5 copy-start.7
  297.8 3.5 copy-start.9
  298.7 3.2 copy-start.5
  310.1 1.6 copy-start.10
  516.9 3.2 copy-start.8
  522.0 3.2 copy-start.6
  530.8 68.5 %copy-start.11 = (f32[256]{0:T(256)S(1)}, f32[256]{0:T(256)}, u32[]{:S(2)}) copy-start(f32[256]{0:T(256)} %param.17) | copy-start | bytes 3076
Sparse Core Ops, SparseCore 0:
  87.5 201.4 all-reduce.6
  311.8 200.3 all-reduce.4
where the time goes:
time: 612 us; the launch traced here: 607 us
  waiting for transfers between devices  433 us (71%)
  blocking collectives  66.2 us (11%)
  matrix products  46 us (8%)
  starting transfers between devices  31.1 us (5%)
  between operations  14.7 us (2%)
  local copies, waits for them, and re-layouts  8.25 us (1%)
  other arithmetic  7.57 us (1%)
    psum x2, waiting for transfers between devices, summed(): return lax.psum((gradients[0], gradients[1], gradients[2]), 'frame')  383 us
    all_to_all x1, blocking collectives, shards(): lax.all_to_all(assembled, 'frame', split_axis=1, concat_axis=1, tiled=True)  33.2 us
    psum x1, blocking collectives, shards(): total = lax.psum(local_sum, 'head')  33.1 us
    all_to_all x1, waiting for transfers between devices, shards(): lax.all_to_all(attended.reshape(depth, frames_count, width), 'frame', spl...  20.6 us
    all_to_all x1, waiting for transfers between devices, shards(): lax.all_to_all(query_norm.reshape(depth, frames_count, width), 'frame', s...  17.7 us
    all_to_all x1, starting transfers between devices, shards(): lax.all_to_all(values.reshape(depth, frames_count, width), 'frame', split...  14.8 us
    dot_general x30, matrix products, newton_schulz(): square = jnp.einsum('hij,hkj->hik', matrix, matrix, precision=highest)  14 us
  transfers between devices with their start and end apart: 7, of which 5 were waited for; matrix products, arithmetic and copies ran while one was open for 3% of the time, Pallas kernels for 0%

commit v1 on v0

v1 whole, which is shorter than its diff:
```python
import math

import jax
import jax.numpy as jnp
from jax import lax
from jax.experimental import pallas as pl
from jax.experimental.pallas import tpu as pltpu
from jax.sharding import PartitionSpec as P

NS_ITERS = 5
quintic_terms = (3.4445, -4.775, 2.0315)
f32, bf16 = jnp.float32, jnp.bfloat16
WIRE = f32

inside = (((1,), (0,)), ((), ()))
across = (((1,), (1,)), ((), ()))


def dot(a, b, dims):
    return lax.dot_general(a, b, dims, preferred_element_type=f32)


def parts_of(matrix):
    high = matrix.astype(bf16)
    low = (matrix - high.astype(f32)).astype(bf16)
    return high, low


def rows2(high, low):
    return jnp.concatenate([jnp.concatenate([high, high], 1), jnp.concatenate([low, low], 1)], 0)


def cols2(high, low):
    both = jnp.concatenate([high, low], 1)
    return jnp.concatenate([both, both], 0)


def folded(wide):
    half = wide.shape[1] // 2
    return wide[:, :half] + wide[:, half:]


def newton_schulz(gradients):
    matrices = []
    for gradient in gradients:
        total = jnp.sum(jnp.sum(gradient * gradient, axis=1, keepdims=True), axis=0, keepdims=True)
        matrices.append(gradient / (jnp.sqrt(total) + 1e-07))
    for _ in range(NS_ITERS):
        split = [parts_of(matrix) for matrix in matrices]
        squares = [
            folded(dot(jnp.concatenate(pair, 1), rows2(*pair), across)) for pair in split
        ]
        halves = [parts_of(square) for square in squares]
        quartics = [
            folded(dot(jnp.concatenate(pair, 1), cols2(*pair), inside)) for pair in halves
        ]
        mixings = [
            parts_of(quintic_terms[1] * square + quintic_terms[2] * quartic)
            for square, quartic in zip(squares, quartics)
        ]
        products = [
            folded(dot(jnp.concatenate(pair, 1), cols2(*other), inside))
            for pair, other in zip(mixings, split)
        ]
        matrices = [
            quintic_terms[0] * matrix + product for matrix, product in zip(matrices, products)
        ]
    return matrices


def renewed(weights, gradients, initial, steps):
    result = []
    for no, (weight, ortho, first) in enumerate(zip(weights, newton_schulz(gradients), initial)):
        axis = 1 if no % 3 == 2 else 0
        moved = weight - steps[no // 3] * ortho
        target = jnp.sqrt(jnp.sum(first * first, axis=axis, keepdims=True))
        length = jnp.sqrt(jnp.sum(moved * moved, axis=axis, keepdims=True))
        result.append(moved * (target / (length + 1e-06)))
    return result


def gate_and_up(rows, gate_w, up_w):
    gate_parts, up_parts = parts_of(gate_w), parts_of(up_w)
    stacked = jnp.concatenate(
        [jnp.concatenate([gate_parts[i], up_parts[i]], 1) for i in range(2)], 0
    )
    both = dot(jnp.concatenate([rows, rows], 1), stacked, inside)
    dim = gate_w.shape[1]
    return both[:, :dim], both[:, dim:]


def fast_grads(weights, key, value):
    gate_w, up_w, down_t = weights
    gate, upward = gate_and_up(key, gate_w, up_w)
    sigma = 1.0 / (1.0 + jnp.exp(-gate))
    active = gate * sigma
    hidden = active * upward
    back = dot(jnp.concatenate([value, value], 1), jnp.concatenate(parts_of(down_t), 0), inside)
    back_gate = back * upward * sigma * (1.0 + gate * (1.0 - sigma))
    back_up = back * active
    gate_parts, up_parts, hidden_parts = parts_of(back_gate), parts_of(back_up), parts_of(hidden)
    key_t, value_t = key.T, value.T
    dim = key.shape[1]
    both = dot(key_t, jnp.concatenate([gate_parts[0], up_parts[0]], 1), inside)
    both = both + dot(key_t, jnp.concatenate([gate_parts[1], up_parts[1]], 1), inside)
    down = folded(dot(value_t, jnp.concatenate(hidden_parts, 1), inside))
    return -both[:, :dim], -both[:, dim:], -down


def initial_of(gate_ref, up_ref, down_ref):
    weights = []
    for head_no in range(gate_ref.shape[0]):
        weights += [gate_ref[head_no], up_ref[head_no], down_ref[head_no].T]
    return weights


def store_matrices(ref, first, matrices):
    for no, matrix in enumerate(matrices):
        rows = matrix.shape[0]
        ref[(first + no) * rows : (first + no + 1) * rows, :] = matrix.astype(ref.dtype)


def load_matrices(ref, dim):
    return [
        ref[no * dim : (no + 1) * dim, :].astype(f32) for no in range(ref.shape[0] // dim)
    ]


def attend_kernel(
    flags, q_ref, kp_ref, k_ref, vp_ref, v_ref, gate_ref, up_ref, down_ref, att_ref, grad_ref
):
    heads, dim = gate_ref.shape[0], gate_ref.shape[1]
    frame_len = q_ref.shape[0]
    rows = 128
    scale = math.log2(math.e) / math.sqrt(dim)
    bias = jnp.where(flags[0] == 0, -1e30, 0.0).astype(f32)
    weights = initial_of(gate_ref, up_ref, down_ref)
    for head_no in range(heads):
        cols = slice(head_no * dim, (head_no + 1) * dim)
        for block in range(frame_len // rows):
            here = slice(block * rows, (block + 1) * rows)
            query = q_ref[here, cols]
            before = dot(query, kp_ref[:, cols], across) + bias
            within = dot(query, k_ref[:, cols], across)
            top = jnp.maximum(
                jnp.max(before, axis=1, keepdims=True), jnp.max(within, axis=1, keepdims=True)
            )
            before = jnp.exp2((before - top) * scale)
            within = jnp.exp2((within - top) * scale)
            total = jnp.sum(before, axis=1, keepdims=True) + jnp.sum(within, axis=1, keepdims=True)
            share = 1.0 / total
            mixed = dot((before * share).astype(bf16), vp_ref[:, cols], inside)
            mixed = mixed + dot((within * share).astype(bf16), v_ref[:, cols], inside)
            square = jnp.mean(mixed * mixed, axis=1, keepdims=True)
            att_ref[here, cols] = (mixed * lax.rsqrt(square + 1e-06)).astype(bf16)
        grads = fast_grads(
            weights[3 * head_no : 3 * head_no + 3], att_ref[:, cols], v_ref[:, cols]
        )
        store_matrices(grad_ref, 3 * head_no, grads)


def second_kernel(
    step_ref, total_ref, att_ref, v_ref, gate_ref, up_ref, down_ref, weight_ref, grad_ref
):
    heads, dim = gate_ref.shape[0], gate_ref.shape[1]
    initial = initial_of(gate_ref, up_ref, down_ref)
    steps = [step_ref[head_no] for head_no in range(heads)]
    weights = renewed(initial, load_matrices(total_ref, dim), initial, steps)
    store_matrices(weight_ref, 0, weights)
    for head_no in range(heads):
        cols = slice(head_no * dim, (head_no + 1) * dim)
        grads = fast_grads(
            weights[3 * head_no : 3 * head_no + 3], att_ref[:, cols], v_ref[:, cols]
        )
        store_matrices(grad_ref, 3 * head_no, grads)


def apply_kernel(
    flags,
    step_ref,
    scale_ref,
    total_ref,
    weight_ref,
    att_ref,
    q_ref,
    gate_ref,
    up_ref,
    down_ref,
    comb_ref,
    square_ref,
):
    heads, dim = gate_ref.shape[0], gate_ref.shape[1]
    initial = initial_of(gate_ref, up_ref, down_ref)
    steps = [step_ref[head_no] for head_no in range(heads)]
    earlier = load_matrices(weight_ref, dim)
    weights = renewed(earlier, load_matrices(total_ref, dim), initial, steps)
    late = flags[1] != 0
    weights = [jnp.where(late, new, old) for new, old in zip(weights, earlier)]
    for head_no in range(heads):
        cols = slice(head_no * dim, (head_no + 1) * dim)
        gate_w, up_w, down_t = weights[3 * head_no : 3 * head_no + 3]
        query = q_ref[:, cols].astype(f32)
        square = jnp.mean(query * query, axis=1, keepdims=True)
        query = (query * lax.rsqrt(square + 1e-06)).astype(bf16)
        gate, upward = gate_and_up(query, gate_w, up_w)
        hidden = gate / (1.0 + jnp.exp(-gate)) * upward
        output = folded(
            dot(jnp.concatenate(parts_of(hidden), 1), rows2(*parts_of(down_t)), across)
        )
        fast_out = (output * scale_ref[head_no]).astype(bf16)
        comb_ref[:, cols] = att_ref[:, cols].astype(f32) + fast_out.astype(f32)
    combined = comb_ref[...]
    square = combined * combined
    ones = jnp.ones((8, square.shape[1]), bf16)
    high, low = parts_of(square)
    square_ref[...] = dot(ones, high, across) + dot(ones, low, across)


def final_kernel(square_ref, comb_ref, gain_ref, out_ref, *, features):
    ones = jnp.ones((square_ref.shape[0], 128), bf16)
    squares = square_ref[...]
    high, low = parts_of(squares)
    first = (((0,), (0,)), ((), ()))
    total = dot(high, ones, first) + dot(low, ones, first)
    scale = lax.rsqrt(total / features + 1e-05)
    for no in range(comb_ref.shape[1] // 128):
        cols = slice(no * 128, (no + 1) * 128)
        out_ref[:, cols] = (comb_ref[:, cols] * scale * gain_ref[:, cols]).astype(bf16)


def call(kernel, outs, *args, smem=0, flops=0):
    spec = pl.BlockSpec(memory_space=pltpu.VMEM)
    scalar = pl.BlockSpec(memory_space=pltpu.SMEM)
    shapes = [jax.ShapeDtypeStruct(*out) for out in outs]
    return pl.pallas_call(
        kernel,
        out_shape=shapes,
        in_specs=[scalar] * smem + [spec] * (len(args) - smem),
        out_specs=[spec] * len(shapes),
        compiler_params=pltpu.CompilerParams(vmem_limit_bytes=40 * 2**20),
    )(*args)


def exchange(array, groups):
    return lax.all_to_all(
        array, "frame", split_axis=0, concat_axis=0, tiled=True, axis_index_groups=groups
    )


def shards(
    queries, key_rows, values, gate_init, up_init, down_init, step_size, head_scale, out_gain
):
    frame_len, width = queries.shape
    heads, dim = gate_init.shape[0], gate_init.shape[1]
    frames = lax.axis_size("frame")
    position = lax.axis_index("frame")
    near = frames // 4
    near_groups = [list(range(near * i, near * i + near)) for i in range(4)]
    far_groups = [list(range(i, frames, near)) for i in range(near)]
    rows = 3 * heads * dim
    piece = rows // near
    flags = jnp.stack([position, position // (frames // 2)]).astype(jnp.int32)

    route = [(i, i + 1) for i in range(frames - 1)]
    keys_prev = lax.ppermute(key_rows, "frame", route)
    values_prev = lax.ppermute(values, "frame", route)
    attended, grads = call(
        attend_kernel,
        [((frame_len, width), bf16), ((rows, dim), WIRE)],
        flags,
        queries,
        keys_prev,
        key_rows,
        values_prev,
        values,
        gate_init,
        up_init,
        down_init,
        smem=1,
    )

    def near_sum(grads):
        return jnp.sum(exchange(grads, near_groups).reshape(near, piece, dim).astype(f32), axis=0)

    def spread(part):
        part = part.astype(WIRE)
        return exchange(
            jnp.broadcast_to(part[None], (near, piece, dim)).reshape(rows, dim), near_groups
        )

    part = near_sum(grads).astype(WIRE)
    parts = exchange(
        jnp.broadcast_to(part[None], (4, piece, dim)).reshape(4 * piece, dim), far_groups
    ).reshape(4, piece, dim)
    total = spread(parts[0].astype(f32) + parts[1].astype(f32))
    weights, grads = call(
        second_kernel,
        [((rows, dim), f32), ((rows, dim), WIRE)],
        step_size,
        total,
        attended,
        values,
        gate_init,
        up_init,
        down_init,
        smem=1,
    )
    part = near_sum(grads).astype(WIRE)
    other = lax.ppermute(part, "frame", [(i, i ^ near) for i in range(frames)])
    total = spread(part.astype(f32) + other.astype(f32))
    combined, square = call(
        apply_kernel,
        [((frame_len, width), f32), ((8, frame_len), f32)],
        flags,
        step_size,
        head_scale,
        total,
        weights,
        attended,
        queries,
        gate_init,
        up_init,
        down_init,
        smem=3,
    )
    columns = lax.axis_size("head")
    squares = lax.all_to_all(
        jnp.broadcast_to(square[:1], (columns, frame_len)),
        "head",
        split_axis=0,
        concat_axis=0,
        tiled=True,
    )
    (out,) = call(
        lambda *refs: final_kernel(*refs, features=width * columns),
        [((frame_len, width), bf16)],
        squares,
        combined,
        out_gain[None, :],
    )
    return out


def solution(mesh):
    in_specs = (
        P("frame", "head"),
        P("frame", "head"),
        P("frame", "head"),
        P("head", None, None),
        P("head", None, None),
        P("head", None, None),
        P("head"),
        P("head"),
        P("head"),
    )
    out_specs = P("frame", "head")
    return jax.shard_map(shards, mesh=mesh, in_specs=in_specs, out_specs=out_specs, check_vma=False)
```

time: 612 us -> 154 us (0.25)
  waiting for transfers between devices: 433 us -> 13.5 us
  matrix products: 46 us -> 0 us
  blocking collectives: 66.2 us -> 107 us
  starting transfers between devices: 31.1 us -> 9.81 us
  Pallas kernels: 0 us -> 15.7 us
  between operations: 14.7 us -> 0.15 us
  other arithmetic: 7.57 us -> 0.14 us
    psum x2 -> x0, waiting for transfers between devices: 383 us -> none  [summed(): return lax.psum((gradients[0], gradients[1], gradients[2]), 'frame')]
    all_to_all x1 -> x6, blocking collectives: 33.2 us -> 107 us  [the longest x5 93.7 us: exchange(): lax.all_to_all(array, 'frame', split_axis=0, concat_axis=0, tiled=True, a...]
    all_to_all x3 -> x0, waiting for transfers between devices: 50.3 us -> none  [the longest x1 20.6 us: shards(): lax.all_to_all(attended.reshape(depth, frames_count, width), 'frame', spl...]
    dot_general x112 -> x0, matrix products: 46 us -> none  [the longest x30 14 us: newton_schulz(): square = jnp.einsum('hij,hkj->hik', matrix, matrix, precision=highest)]
    psum x1 -> x0, blocking collectives: 33.1 us -> none  [shards(): total = lax.psum(local_sum, 'head')]
    all_to_all x3 -> x0, starting transfers between devices: 24 us -> none  [the longest x1 14.8 us: shards(): lax.all_to_all(values.reshape(depth, frames_count, width), 'frame', split...]
    pallas_call x0 -> x4, Pallas kernels: none -> 15.7 us  [call(): pl.pallas_call(kernel, out_shape=shapes, in_specs=[scalar] * smem + [spec...]
    ppermute x2 -> x3, waiting for transfers between devices: 0.01 us -> 13.5 us  [the longest x1 9.11 us: shards(): other = lax.ppermute(part, 'frame', [(i, i ^ near) for i in range(frames)])]
  transfers between devices with their start and end apart: 7 -> 3, of which waited for: 5 -> 3; matrix products, arithmetic and copies ran while one was open for 3% -> 0% of each run, Pallas kernels for 0% -> 0%
where the time goes in v1:
time: 154 us
  blocking collectives  107 us (69%)
  Pallas kernels  15.7 us (10%)
  waiting for transfers between devices  13.5 us (9%)
  starting transfers between devices  9.81 us (6%)
  local copies, waits for them, and re-layouts  7.69 us (5%)
    all_to_all x5, blocking collectives, exchange(): lax.all_to_all(array, 'frame', split_axis=0, concat_axis=0, tiled=True, a...  93.7 us
    pallas_call x4, Pallas kernels, call(): pl.pallas_call(kernel, out_shape=shapes, in_specs=[scalar] * smem + [spec...  15.7 us
    all_to_all x1, blocking collectives, shards(): lax.all_to_all(jnp.broadcast_to(square[:1], (columns, frame_len)), 'head'...  13 us
    ppermute x1, waiting for transfers between devices, shards(): other = lax.ppermute(part, 'frame', [(i, i ^ near) for i in range(frames)])  9.11 us
    unnamed x29, local copies, waits for them, and re-layouts  7.56 us
    ppermute x1, starting transfers between devices, shards(): keys_prev = lax.ppermute(key_rows, 'frame', route)  4.93 us
  transfers between devices with their start and end apart: 3, of which 3 were waited for; matrix products, arithmetic and copies ran while one was open for 0% of the time, Pallas kernels for 0%

profile of v1, /device:TPU:1, one launch (start us, length us, event | category | flops | bytes accessed | tf_op | source)
XLA Modules:
  0.0 153.7 jit_solution(17629417038439384823)
XLA Ops:
  0.0 4.9 %collective-permute-start = (bf16[512,256]{1,0:T(8,128)(2,1)}, bf16[512,256]{1,0:T(8,128)(2,1)S(1)}, u32[]{:S(2)}, u32[]{:S(2)}) collective-permute-start(bf16[512,256]{1,0:T(8,128)(2,1)} %k_ref.1), channel_id=1, source_target_pairs={{0,16},{16,32},{32,48},{48,64},{64,80},{80,96},{96,112},{112,128},... | collective-permute-start | bytes 786440 | tf_op jit(solution)/shard_map/ppermute | solution.py:265
  4.9 1.9 %collective-permute-start.1 = (bf16[512,256]{1,0:T(8,128)(2,1)}, bf16[512,256]{1,0:T(8,128)(2,1)S(1)}, u32[]{:S(2)}, u32[]{:S(2)}) collective-permute-start(bf16[512,256]{1,0:T(8,128)(2,1)} %v_ref.3), channel_id=1, source_target_pairs={{0,16},{16,32},{32,48},{48,64},{64,80},{80,96},{96,112},{112,128},... | collective-permute-start | bytes 786440 | tf_op jit(solution)/shard_map/ppermute | solution.py:266
  6.9 0.1 pad_add_fusion.flags
  7.0 2.4 %collective-permute-done.kp_ref = bf16[512,256]{1,0:T(8,128)(2,1)S(1)} collective-permute-done((bf16[512,256]{1,0:T(8,128)(2,1)}, bf16[512,256]{1,0:T(8,128)(2,1)S(1)}, u32[]{:S(2)}, u32[]{:S(2)}) %collective-permute-start) | collective-permute-done | bytes 262176 | tf_op jit(solution)/shard_map/ppermute | solution.py:265
  9.4 2.0 %collective-permute-done.1.vp_ref = bf16[512,256]{1,0:T(8,128)(2,1)S(1)} collective-permute-done((bf16[512,256]{1,0:T(8,128)(2,1)}, bf16[512,256]{1,0:T(8,128)(2,1)S(1)}, u32[]{:S(2)}, u32[]{:S(2)}) %collective-permute-start.1) | collective-permute-done | bytes 262176 | tf_op jit(solution)/shard_map/ppermute | solution.py:266
  11.4 0.0 copy-start
  11.4 0.9 copy-done
  12.3 0.0 copy-start.2
  12.3 0.9 copy-done.2
  13.2 0.0 copy-start.4
  13.2 0.9 copy-done.4
  14.1 0.0 copy-start.6
  14.1 0.9 copy-done.6
  15.0 0.0 copy-start.8
  15.0 0.9 copy-done.8
  16.0 0.0 copy-start.10
  16.0 0.9 copy-done.10
  16.9 5.3 %shard_map.91 = (bf16[512,256]{1,0:T(8,128)(2,1)S(1)}, f32[768,128]{1,0:T(8,128)S(1)}) custom-call(s32[2]{0:T(128)S(1)} %pad_add_fusion.flags, bf16[512,256]{1,0:T(8,128)(2,1)S(1)} %copy-done.8, bf16[512,256]{1,0:T(8,128)(2,1)S(1)} %collective-permute-done.kp_ref, bf16[512,256]{1,0:T(8,128)(2,1)S(1)} %copy-done.10, ...), custom_call_target="tpu_custom_call" | custom-call | tf_op jit(solution)/shard_map/pallas_call | solution.py:235
  22.2 18.7 %all_to_all.48 = f32[8,96,128]{2,1,0:T(8,128)S(1)} all-to-all(f32[8,96,128]{2,1,0:T(8,128)S(1)} %bitcast.15), channel_id=1, replica_groups={{0,16,32,48,64,80,96,112},{128,144,160,176,192,208,224,240},{256,272,28..., dimensions={0} | all-to-all | bytes 786432 | tf_op jit(solution)/shard_map/all_to_all | solution.py:245
  41.0 25.0 %all_to_all.49 = f32[4,96,128]{2,1,0:T(8,128)S(1)} all-to-all(f32[4,96,128]{2,1,0:T(8,128)S(1)} %broadcast_in_dim.12), channel_id=1, replica_groups={{0,128,256,384},{16,144,272,400},{32,160,288,416},{48,176,304,432},{64,..., dimensions={0} | all-to-all | bytes 393216 | tf_op jit(solution)/shard_map/all_to_all | solution.py:245
  66.0 0.0 copy-start.1
  66.0 0.0 copy-start.3
  66.0 0.0 copy-start.5
  66.0 0.0 copy-start.7
  66.1 20.2 %all_to_all.50 = f32[8,96,128]{2,1,0:T(8,128)S(1)} all-to-all(f32[8,96,128]{2,1,0:T(8,128)S(1)} %broadcast_in_dim.14), channel_id=1, replica_groups={{0,16,32,48,64,80,96,112},{128,144,160,176,192,208,224,240},{256,272,28..., dimensions={0} | all-to-all | bytes 786432 | tf_op jit(solution)/shard_map/all_to_all | solution.py:245
  86.3 0.0 copy-start.11
  86.3 0.0 copy-done.1
  86.3 0.0 copy-done.3
  86.3 0.0 copy-done.5
  86.3 0.0 copy-done.7
  86.3 0.6 copy-done.11
  87.0 4.7 %shard_map.92 = (f32[768,128]{1,0:T(8,128)S(1)}, f32[768,128]{1,0:T(8,128)S(1)}) custom-call(f32[2]{0:T(128)S(1)} %copy-done.11, f32[768,128]{1,0:T(8,128)S(1)} %bitcast.14, bf16[512,256]{1,0:T(8,128)(2,1)S(1)} %get-tuple-element.12.att_ref, bf16[512,256]{1,0:T(8,128)(2,1)S(1)} %copy-done.7, f32[2,128,128]{2,1,0:T(8,128)S(1)} %copy-done.1, ...), custom_call_target="tpu_custom_call" | custom-call | tf_op jit(solution)/shard_map/pallas_call | solution.py:235
  91.7 14.9 %all_to_all.51 = f32[8,96,128]{2,1,0:T(8,128)S(1)} all-to-all(f32[8,96,128]{2,1,0:T(8,128)S(1)} %bitcast.16), channel_id=1, replica_groups={{0,16,32,48,64,80,96,112},{128,144,160,176,192,208,224,240},{256,272,28..., dimensions={0} | all-to-all | bytes 786432 | tf_op jit(solution)/shard_map/all_to_all | solution.py:245
  106.6 3.0 %collective-permute-start.2 = (f32[96,128]{1,0:T(8,128)S(1)}, f32[96,128]{1,0:T(8,128)S(1)}, u32[]{:S(2)}, u32[]{:S(2)}) collective-permute-start(f32[96,128]{1,0:T(8,128)S(1)} %reduce_sum.19), channel_id=1, source_target_pairs={{0,128},{16,144},{32,160},{48,176},{64,192},{80,208},{96,224},{112... | collective-permute-start | bytes 147464 | tf_op jit(solution)/shard_map/ppermute | solution.py:309
  109.6 9.1 %collective-permute-done.2 = f32[96,128]{1,0:T(8,128)S(1)} collective-permute-done((f32[96,128]{1,0:T(8,128)S(1)}, f32[96,128]{1,0:T(8,128)S(1)}, u32[]{:S(2)}, u32[]{:S(2)}) %collective-permute-start.2) | collective-permute-done | bytes 49184 | tf_op jit(solution)/shard_map/ppermute | solution.py:309
  118.7 0.0 copy-start.9
  118.8 14.8 %all_to_all.52 = f32[8,96,128]{2,1,0:T(8,128)S(1)} all-to-all(f32[8,96,128]{2,1,0:T(8,128)S(1)} %broadcast_in_dim.15), channel_id=1, replica_groups={{0,16,32,48,64,80,96,112},{128,144,160,176,192,208,224,240},{256,272,28..., dimensions={0} | all-to-all | bytes 786432 | tf_op jit(solution)/shard_map/all_to_all | solution.py:245
  133.5 0.0 copy-start.13
  133.5 0.0 copy-done.9
  133.5 0.7 copy-done.13
  134.2 4.8 %shard_map.93 = (f32[512,256]{1,0:T(8,128)S(1)}, f32[8,512]{1,0:T(8,128)S(1)}) custom-call(s32[2]{0:T(128)S(1)} %pad_add_fusion.flags, f32[2]{0:T(128)S(1)} %copy-done.11, f32[2]{0:T(128)S(1)} %copy-done.13, f32[768,128]{1,0:T(8,128)S(1)} %bitcast.13, f32[768,128]{1,0:T(8,128)S(1)} %get-tuple-element.14.weight_ref, ...), custom_call_target="tpu_custom_call" | custom-call | tf_op jit(solution)/shard_map/pallas_call | solution.py:235
  138.9 0.1 broadcast_in_dim.32
  139.0 13.0 %all_to_all.53 = f32[16,1,512]{2,1,0:T(1,128)S(1)} all-to-all(f32[16,1,512]{2,1,0:T(1,128)S(1)} %broadcast_in_dim.32), channel_id=1, replica_groups=mesh['frame'=32,'head'=16] {'head'}, dimensions={0} | all-to-all | bytes 65536 | tf_op jit(solution)/shard_map/all_to_all | solution.py:327
  152.0 0.0 copy-start.12
  152.0 0.7 copy-done.12
  152.7 1.0 shard_map.94
  (9 shorter events, 0.1 us)
Async XLA Ops:
  0.0 9.4 %collective-permute-start = (bf16[512,256]{1,0:T(8,128)(2,1)}, bf16[512,256]{1,0:T(8,128)(2,1)S(1)}, u32[]{:S(2)}, u32[]{:S(2)}) collective-permute-start(bf16[512,256]{1,0:T(8,128)(2,1)} %k_ref.1), channel_id=1, source_target_pairs={{0,16},{16,32},{32,48},{48,64},{64,80},{80,96},{96,112},{112,128},... | collective-permute-start | bytes 786440 | tf_op jit(solution)/shard_map/ppermute | solution.py:265
  4.9 6.4 %collective-permute-start.1 = (bf16[512,256]{1,0:T(8,128)(2,1)}, bf16[512,256]{1,0:T(8,128)(2,1)S(1)}, u32[]{:S(2)}, u32[]{:S(2)}) collective-permute-start(bf16[512,256]{1,0:T(8,128)(2,1)} %v_ref.3), channel_id=1, source_target_pairs={{0,16},{16,32},{32,48},{48,64},{64,80},{80,96},{96,112},{112,128},... | collective-permute-start | bytes 786440 | tf_op jit(solution)/shard_map/ppermute | solution.py:266
  11.4 0.9 copy-start
  12.3 0.9 copy-start.2
  13.2 0.9 copy-start.4
  14.1 0.9 copy-start.6
  15.0 0.9 copy-start.8
  16.0 0.9 copy-start.10
  66.0 20.3 %copy-start.1 = (f32[2,128,128]{2,1,0:T(8,128)S(1)}, f32[2,128,128]{2,1,0:T(8,128)}, u32[]{:S(2)}) copy-start(f32[2,128,128]{2,1,0:T(8,128)} %gate_ref.5) | copy-start | bytes 393220
  66.0 20.3 %copy-start.3 = (f32[2,128,128]{2,1,0:T(8,128)S(1)}, f32[2,128,128]{2,1,0:T(8,128)}, u32[]{:S(2)}) copy-start(f32[2,128,128]{2,1,0:T(8,128)} %up_ref.5) | copy-start | bytes 393220
  66.0 20.3 %copy-start.5 = (f32[2,128,128]{2,1,0:T(8,128)S(1)}, f32[2,128,128]{2,1,0:T(8,128)}, u32[]{:S(2)}) copy-start(f32[2,128,128]{2,1,0:T(8,128)} %down_ref.5) | copy-start | bytes 393220
  66.0 20.3 %copy-start.7 = (bf16[512,256]{1,0:T(8,128)(2,1)S(1)}, bf16[512,256]{1,0:T(8,128)(2,1)}, u32[]{:S(2)}) copy-start(bf16[512,256]{1,0:T(8,128)(2,1)} %v_ref.3) | copy-start | bytes 786436
  86.3 0.7 copy-start.11
  106.6 12.1 %collective-permute-start.2 = (f32[96,128]{1,0:T(8,128)S(1)}, f32[96,128]{1,0:T(8,128)S(1)}, u32[]{:S(2)}, u32[]{:S(2)}) collective-permute-start(f32[96,128]{1,0:T(8,128)S(1)} %reduce_sum.19), channel_id=1, source_target_pairs={{0,128},{16,144},{32,160},{48,176},{64,192},{80,208},{96,224},{112... | collective-permute-start | bytes 147464 | tf_op jit(solution)/shard_map/ppermute | solution.py:309
  118.7 14.8 %copy-start.9 = (bf16[512,256]{1,0:T(8,128)(2,1)S(1)}, bf16[512,256]{1,0:T(8,128)(2,1)}, u32[]{:S(2)}) copy-start(bf16[512,256]{1,0:T(8,128)(2,1)} %q_ref.3) | copy-start | bytes 786436
  133.5 0.7 copy-start.13
  152.0 0.7 copy-start.12

commit v2 on v1

--- a/solution.py
+++ b/solution.py
@@ -11,6 +11,7 @@
 quintic_terms = (3.4445, -4.775, 2.0315)
 f32, bf16 = jnp.float32, jnp.bfloat16
 WIRE = f32
+ROWS = 128
 
 inside = (((1,), (0,)), ((), ()))
 across = (((1,), (1,)), ((), ()))
@@ -107,10 +108,13 @@
     return -both[:, :dim], -both[:, dim:], -down
 
 
-def initial_of(gate_ref, up_ref, down_ref):
+def initial_of(weights_ref):
+    heads = weights_ref.shape[0] // 3
+    dim = weights_ref.shape[1]
     weights = []
-    for head_no in range(gate_ref.shape[0]):
-        weights += [gate_ref[head_no], up_ref[head_no], down_ref[head_no].T]
+    for head_no in range(heads):
+        weights += [weights_ref[head_no], weights_ref[heads + head_no]]
+        weights.append(weights_ref[2 * heads + head_no].T)
     return weights
 
 
@@ -126,75 +130,82 @@
     ]
 
 
+def within_kernel(q_ref, kv_ref, prob_ref, stat_ref):
+    frame_len, width = q_ref.shape
+    dim = 128
+    heads = width // dim
+    scale = math.log2(math.e) / math.sqrt(dim)
+    for head_no in range(heads):
+        cols = slice(head_no * dim, (head_no + 1) * dim)
+        for block in range(frame_len // ROWS):
+            here = slice(block * ROWS, (block + 1) * ROWS)
+            place = slice(head_no * frame_len + block * ROWS, head_no * frame_len + (block + 1) * ROWS)
+            within = dot(q_ref[here, cols], kv_ref[0:frame_len, cols], across)
+            top = jnp.max(within, axis=1, keepdims=True)
+            within = jnp.exp2((within - top) * scale)
+            total = jnp.sum(within, axis=1, keepdims=True)
+            prob_ref[place, :] = within
+            stat_ref[place, 0:128] = jnp.broadcast_to(top, (ROWS, 128))
+            stat_ref[place, 128:256] = jnp.broadcast_to(total, (ROWS, 128))
+
+
 def attend_kernel(
-    flags, q_ref, kp_ref, k_ref, vp_ref, v_ref, gate_ref, up_ref, down_ref, att_ref, grad_ref
+    scalars, q_ref, past_ref, kv_ref, weights_ref, prob_ref, stat_ref, att_ref, grad_ref
 ):
-    heads, dim = gate_ref.shape[0], gate_ref.shape[1]
+    dim = weights_ref.shape[1]
+    heads = weights_ref.shape[0] // 3
     frame_len = q_ref.shape[0]
-    rows = 128
     scale = math.log2(math.e) / math.sqrt(dim)
-    bias = jnp.where(flags[0] == 0, -1e30, 0.0).astype(f32)
-    weights = initial_of(gate_ref, up_ref, down_ref)
+    bias = jnp.where(scalars[0] == 0, -1e30, 0.0).astype(f32)
+    weights = initial_of(weights_ref)
     for head_no in range(heads):
         cols = slice(head_no * dim, (head_no + 1) * dim)
-        for block in range(frame_len // rows):
-            here = slice(block * rows, (block + 1) * rows)
-            query = q_ref[here, cols]
-            before = dot(query, kp_ref[:, cols], across) + bias
-            within = dot(query, k_ref[:, cols], across)
-            top = jnp.maximum(
-                jnp.max(before, axis=1, keepdims=True), jnp.max(within, axis=1, keepdims=True)
-            )
+        for block in range(frame_len // ROWS):
+            here = slice(block * ROWS, (block + 1) * ROWS)
+            place = slice(head_no * frame_len + block * ROWS, head_no * frame_len + (block + 1) * ROWS)
+            before = dot(q_ref[here, cols], past_ref[0:frame_len, cols], across) + bias
+            top_within = stat_ref[place, 0:1]
+            top = jnp.maximum(jnp.max(before, axis=1, keepdims=True), top_within)
             before = jnp.exp2((before - top) * scale)
-            within = jnp.exp2((within - top) * scale)
-            total = jnp.sum(before, axis=1, keepdims=True) + jnp.sum(within, axis=1, keepdims=True)
+            shrink = jnp.exp2((top_within - top) * scale)
+            total = jnp.sum(before, axis=1, keepdims=True) + stat_ref[place, 128:129] * shrink
             share = 1.0 / total
-            mixed = dot((before * share).astype(bf16), vp_ref[:, cols], inside)
-            mixed = mixed + dot((within * share).astype(bf16), v_ref[:, cols], inside)
+            mixed = dot((before * share).astype(bf16), past_ref[frame_len:, cols], inside)
+            within = (prob_ref[place, :] * (shrink * share)).astype(bf16)
+            mixed = mixed + dot(within, kv_ref[frame_len:, cols], inside)
             square = jnp.mean(mixed * mixed, axis=1, keepdims=True)
             att_ref[here, cols] = (mixed * lax.rsqrt(square + 1e-06)).astype(bf16)
         grads = fast_grads(
-            weights[3 * head_no : 3 * head_no + 3], att_ref[:, cols], v_ref[:, cols]
+            weights[3 * head_no : 3 * head_no + 3], att_ref[:, cols], kv_ref[frame_len:, cols]
         )
         store_matrices(grad_ref, 3 * head_no, grads)
 
 
-def second_kernel(
-    step_ref, total_ref, att_ref, v_ref, gate_ref, up_ref, down_ref, weight_ref, grad_ref
-):
-    heads, dim = gate_ref.shape[0], gate_ref.shape[1]
-    initial = initial_of(gate_ref, up_ref, down_ref)
-    steps = [step_ref[head_no] for head_no in range(heads)]
+def second_kernel(scalars, total_ref, att_ref, kv_ref, weights_ref, weight_ref, grad_ref):
+    dim = weights_ref.shape[1]
+    heads = weights_ref.shape[0] // 3
+    initial = initial_of(weights_ref)
+    steps = [scalars[2 + head_no] for head_no in range(heads)]
     weights = renewed(initial, load_matrices(total_ref, dim), initial, steps)
     store_matrices(weight_ref, 0, weights)
     for head_no in range(heads):
         cols = slice(head_no * dim, (head_no + 1) * dim)
         grads = fast_grads(
-            weights[3 * head_no : 3 * head_no + 3], att_ref[:, cols], v_ref[:, cols]
+            weights[3 * head_no : 3 * head_no + 3], att_ref[:, cols], kv_ref[att_ref.shape[0] :, cols]
         )
         store_matrices(grad_ref, 3 * head_no, grads)
 
 
 def apply_kernel(
-    flags,
-    step_ref,
-    scale_ref,
-    total_ref,
-    weight_ref,
-    att_ref,
-    q_ref,
-    gate_ref,
-    up_ref,
-    down_ref,
-    comb_ref,
-    square_ref,
+    scalars, total_ref, weight_ref, att_ref, q_ref, weights_ref, comb_ref, square_ref
 ):
-    heads, dim = gate_ref.shape[0], gate_ref.shape[1]
-    initial = initial_of(gate_ref, up_ref, down_ref)
-    steps = [step_ref[head_no] for head_no in range(heads)]
+    dim = weights_ref.shape[1]
+    heads = weights_ref.shape[0] // 3
+    initial = initial_of(weights_ref)
+    steps = [scalars[2 + head_no] for head_no in range(heads)]
     earlier = load_matrices(weight_ref, dim)
     weights = renewed(earlier, load_matrices(total_ref, dim), initial, steps)
-    late = flags[1] != 0
+    late = scalars[1] != 0
     weights = [jnp.where(late, new, old) for new, old in zip(weights, earlier)]
     for head_no in range(heads):
         cols = slice(head_no * dim, (head_no + 1) * dim)
@@ -207,7 +218,7 @@
         output = folded(
             dot(jnp.concatenate(parts_of(hidden), 1), rows2(*parts_of(down_t)), across)
         )
-        fast_out = (output * scale_ref[head_no]).astype(bf16)
+        fast_out = (output * scalars[2 + heads + head_no]).astype(bf16)
         comb_ref[:, cols] = att_ref[:, cols].astype(f32) + fast_out.astype(f32)
     combined = comb_ref[...]
     square = combined * combined
@@ -228,16 +239,19 @@
         out_ref[:, cols] = (comb_ref[:, cols] * scale * gain_ref[:, cols]).astype(bf16)
 
 
-def call(kernel, outs, *args, smem=0, flops=0):
+def call(kernel, outs, *args, scalars=0, hbm=0, scratch=(), flops=0):
     spec = pl.BlockSpec(memory_space=pltpu.VMEM)
-    scalar = pl.BlockSpec(memory_space=pltpu.SMEM)
+    first = [pl.BlockSpec(memory_space=pltpu.SMEM)] * scalars
+    first += [pl.BlockSpec(memory_space=pltpu.HBM)] * hbm
     shapes = [jax.ShapeDtypeStruct(*out) for out in outs]
     return pl.pallas_call(
         kernel,
         out_shape=shapes,
-        in_specs=[scalar] * smem + [spec] * (len(args) - smem),
+        in_specs=first + [spec] * (len(args) - len(first)),
         out_specs=[spec] * len(shapes),
+        scratch_shapes=scratch,
         compiler_params=pltpu.CompilerParams(vmem_limit_bytes=40 * 2**20),
+        cost_estimate=pl.CostEstimate(flops=flops, bytes_accessed=2**21, transcendentals=0),
     )(*args)
 
 
@@ -259,24 +273,32 @@
     far_groups = [list(range(i, frames, near)) for i in range(near)]
     rows = 3 * heads * dim
     piece = rows // near
-    flags = jnp.stack([position, position // (frames // 2)]).astype(jnp.int32)
+    flags = jnp.stack([position, position // (frames // 2)]).astype(f32)
+    scalars = jnp.concatenate([flags, step_size, head_scale])
 
     route = [(i, i + 1) for i in range(frames - 1)]
-    keys_prev = lax.ppermute(key_rows, "frame", route)
-    values_prev = lax.ppermute(values, "frame", route)
+    here = jnp.concatenate([key_rows, values], axis=0)
+    past = lax.ppermute(here, "frame", route)
+    all_weights = jnp.concatenate([gate_init, up_init, down_init], axis=0)
+    probs, stats = call(
+        within_kernel,
+        [((heads * frame_len, frame_len), f32), ((heads * frame_len, 256), f32)],
+        queries,
+        here,
+        flops=2 * 10**9,
+    )
     attended, grads = call(
         attend_kernel,
         [((frame_len, width), bf16), ((rows, dim), WIRE)],
-        flags,
+        scalars,
         queries,
-        keys_prev,
-        key_rows,
-        values_prev,
-        values,
-        gate_init,
-        up_init,
-        down_init,
-        smem=1,
+        past,
+        here,
+        all_weights,
+        probs,
+        stats,
+        scalars=1,
+        flops=3 * 10**9,
     )
 
     def near_sum(grads):
@@ -296,14 +318,13 @@
     weights, grads = call(
         second_kernel,
         [((rows, dim), f32), ((rows, dim), WIRE)],
-        step_size,
+        scalars,
         total,
         attended,
-        values,
-        gate_init,
-        up_init,
-        down_init,
-        smem=1,
+        here,
+        all_weights,
+        scalars=1,
+        flops=4 * 10**9,
     )
     part = near_sum(grads).astype(WIRE)
     other = lax.ppermute(part, "frame", [(i, i ^ near) for i in range(frames)])
@@ -311,17 +332,14 @@
     combined, square = call(
         apply_kernel,
         [((frame_len, width), f32), ((8, frame_len), f32)],
-        flags,
-        step_size,
-        head_scale,
+        scalars,
         total,
         weights,
         attended,
         queries,
-        gate_init,
-        up_init,
-        down_init,
-        smem=3,
+        all_weights,
+        scalars=1,
+        flops=4 * 10**9,
     )
     columns = lax.axis_size("head")
     squares = lax.all_to_all(

time: 154 us -> 149 us (0.968)
  waiting for transfers between devices: 13.5 us -> 10 us
  local copies, waits for them, and re-layouts: 7.69 us -> 5.77 us
  starting transfers between devices: 9.81 us -> 7.9 us
    unnamed x29 -> x10, local copies, waits for them, and re-layouts: 7.56 us -> 3.76 us
    ppermute x2 -> x1, waiting for transfers between devices: 4.4 us -> 0.89 us  [shards(): past = lax.ppermute(here, 'frame', route)]
    ppermute x2 -> x1, starting transfers between devices: 6.85 us -> 4.94 us  [shards(): past = lax.ppermute(here, 'frame', route)]
    concatenate x0 -> x2, local copies, waits for them, and re-layouts: none -> 1.89 us  [the longest x1 0.97 us: shards(): here = jnp.concatenate([key_rows, values], axis=0)]
    pallas_call x4 -> x5, Pallas kernels: 15.7 us -> 17.1 us  [call(): pl.pallas_call(kernel, out_shape=shapes, in_specs=first + [spec] * (len(a...]
  transfers between devices with their start and end apart: 3 -> 2, of which waited for: 3 -> 2; matrix products, arithmetic and copies ran while one was open for 0% -> 2% of each run, Pallas kernels for 0% -> 0%
where the time goes in v2:
time: 149 us; the launch traced here: 148 us
  blocking collectives  107 us (72%)
  Pallas kernels  17.1 us (11%)
  waiting for transfers between devices  10 us (7%)
  starting transfers between devices  7.9 us (5%)
  local copies, waits for them, and re-layouts  5.77 us (4%)
    all_to_all x5, blocking collectives, exchange(): lax.all_to_all(array, 'frame', split_axis=0, concat_axis=0, tiled=True, a...  93.6 us
    pallas_call x5, Pallas kernels, call(): pl.pallas_call(kernel, out_shape=shapes, in_specs=first + [spec] * (len(a...  17.1 us
    all_to_all x1, blocking collectives, shards(): lax.all_to_all(jnp.broadcast_to(square[:1], (columns, frame_len)), 'head'...  13 us
    ppermute x1, waiting for transfers between devices, shards(): other = lax.ppermute(part, 'frame', [(i, i ^ near) for i in range(frames)])  9.1 us
    ppermute x1, starting transfers between devices, shards(): past = lax.ppermute(here, 'frame', route)  4.94 us
    unnamed x10, local copies, waits for them, and re-layouts  3.76 us
  transfers between devices with their start and end apart: 2, of which 2 were waited for; matrix products, arithmetic and copies ran while one was open for 2% of the time, Pallas kernels for 0%

profile of v2, /device:TPU:1, one launch (start us, length us, event | category | flops | bytes accessed | tf_op | source)
XLA Modules:
  0.0 148.4 jit_solution(12641270434434912874)
XLA Ops:
  0.0 1.0 constant_dynamic-update-slice_fusion.1
  1.0 1.0 constant_dynamic-update-slice_fusion.kv_ref
  1.9 4.9 %collective-permute-start = (bf16[1024,256]{1,0:T(8,128)(2,1)S(1)}, bf16[1024,256]{1,0:T(8,128)(2,1)S(1)}, u32[]{:S(2)}, u32[]{:S(2)}) collective-permute-start(bf16[1024,256]{1,0:T(8,128)(2,1)S(1)} %constant_dynamic-update-slice_fusion.kv_ref), channel_id=1, source_target_pairs={{0,16},{16,32},{32,48},{48,64},{64,80},{80,96},{96,112},{112,128},... | collective-permute-start | bytes 1572872 | tf_op jit(solution)/shard_map/ppermute | solution.py:281
  6.9 0.9 constant_dynamic-update-slice_fusion.4
  7.8 0.1 add_convert_fusion
  7.9 0.7 pad_maximum_fusion.scalars
  8.7 0.9 constant_dynamic-update-slice_fusion.3
  9.6 0.9 constant_dynamic-update-slice_fusion.2.weights_ref
  10.5 0.0 copy-start.1
  10.5 0.9 copy-done.1
  11.4 0.6 shard_map.91
  12.1 0.9 collective-permute-done.past_ref
  13.0 5.9 %shard_map.92 = (bf16[512,256]{1,0:T(8,128)(2,1)S(1)}, f32[768,128]{1,0:T(8,128)S(1)}) custom-call(f32[6]{0:T(128)S(1)} %pad_maximum_fusion.scalars, bf16[512,256]{1,0:T(8,128)(2,1)S(1)} %copy-done.1, bf16[1024,256]{1,0:T(8,128)(2,1)S(1)} %collective-permute-done.past_ref, bf16[1024,256]{1,0:T(8,128)(2,1)S(1)} %constant_dynamic-update-slice_fusion.kv_ref, ...), custom_call_target="tpu_custom_call" | custom-call | flops 3000000000 | bytes 2097152 | tf_op jit(solution)/shard_map/pallas_call | solution.py:247
  18.9 18.7 %all_to_all.48 = f32[8,96,128]{2,1,0:T(8,128)S(1)} all-to-all(f32[8,96,128]{2,1,0:T(8,128)S(1)} %bitcast.14), channel_id=1, replica_groups={{0,16,32,48,64,80,96,112},{128,144,160,176,192,208,224,240},{256,272,28..., dimensions={0} | all-to-all | bytes 786432 | tf_op jit(solution)/shard_map/all_to_all | solution.py:259
  37.7 25.1 %all_to_all.49 = f32[4,96,128]{2,1,0:T(8,128)S(1)} all-to-all(f32[4,96,128]{2,1,0:T(8,128)S(1)} %broadcast_in_dim.12), channel_id=1, replica_groups={{0,128,256,384},{16,144,272,400},{32,160,288,416},{48,176,304,432},{64,..., dimensions={0} | all-to-all | bytes 393216 | tf_op jit(solution)/shard_map/all_to_all | solution.py:259
  62.8 20.1 %all_to_all.50 = f32[8,96,128]{2,1,0:T(8,128)S(1)} all-to-all(f32[8,96,128]{2,1,0:T(8,128)S(1)} %broadcast_in_dim.14), channel_id=1, replica_groups={{0,16,32,48,64,80,96,112},{128,144,160,176,192,208,224,240},{256,272,28..., dimensions={0} | all-to-all | bytes 786432 | tf_op jit(solution)/shard_map/all_to_all | solution.py:259
  83.0 4.7 %shard_map.93 = (f32[768,128]{1,0:T(8,128)S(1)}, f32[768,128]{1,0:T(8,128)S(1)}) custom-call(f32[6]{0:T(128)S(1)} %pad_maximum_fusion.scalars, f32[768,128]{1,0:T(8,128)S(1)} %bitcast.15, bf16[512,256]{1,0:T(8,128)(2,1)S(1)} %get-tuple-element.16.att_ref, bf16[1024,256]{1,0:T(8,128)(2,1)S(1)} %constant_dynamic-update-slice_fusion.kv_ref, ...), custom_call_target="tpu_custom_call" | custom-call | flops 4000000000 | bytes 2097152 | tf_op jit(solution)/shard_map/pallas_call | solution.py:247
  87.7 0.0 copy-start.2
  87.7 15.1 %all_to_all.51 = f32[8,96,128]{2,1,0:T(8,128)S(1)} all-to-all(f32[8,96,128]{2,1,0:T(8,128)S(1)} %bitcast.16), channel_id=1, replica_groups={{0,16,32,48,64,80,96,112},{128,144,160,176,192,208,224,240},{256,272,28..., dimensions={0} | all-to-all | bytes 786432 | tf_op jit(solution)/shard_map/all_to_all | solution.py:259
  102.8 3.0 %collective-permute-start.1 = (f32[96,128]{1,0:T(8,128)S(1)}, f32[96,128]{1,0:T(8,128)S(1)}, u32[]{:S(2)}, u32[]{:S(2)}) collective-permute-start(f32[96,128]{1,0:T(8,128)S(1)} %reduce_sum.19), channel_id=1, source_target_pairs={{0,128},{16,144},{32,160},{48,176},{64,192},{80,208},{96,224},{112... | collective-permute-start | bytes 147464 | tf_op jit(solution)/shard_map/ppermute | solution.py:330
  105.8 9.1 %collective-permute-done.1 = f32[96,128]{1,0:T(8,128)S(1)} collective-permute-done((f32[96,128]{1,0:T(8,128)S(1)}, f32[96,128]{1,0:T(8,128)S(1)}, u32[]{:S(2)}, u32[]{:S(2)}) %collective-permute-start.1) | collective-permute-done | bytes 49184 | tf_op jit(solution)/shard_map/ppermute | solution.py:330
  114.9 14.6 %all_to_all.52 = f32[8,96,128]{2,1,0:T(8,128)S(1)} all-to-all(f32[8,96,128]{2,1,0:T(8,128)S(1)} %broadcast_in_dim.15), channel_id=1, replica_groups={{0,16,32,48,64,80,96,112},{128,144,160,176,192,208,224,240},{256,272,28..., dimensions={0} | all-to-all | bytes 786432 | tf_op jit(solution)/shard_map/all_to_all | solution.py:259
  129.5 0.0 copy-done.2
  129.5 0.0 copy-start
  129.5 4.8 %shard_map.94 = (f32[512,256]{1,0:T(8,128)S(1)}, f32[8,512]{1,0:T(8,128)S(1)}) custom-call(f32[6]{0:T(128)S(1)} %pad_maximum_fusion.scalars, f32[768,128]{1,0:T(8,128)S(1)} %bitcast.13, f32[768,128]{1,0:T(8,128)S(1)} %get-tuple-element.18.weight_ref, bf16[512,256]{1,0:T(8,128)(2,1)S(1)} %get-tuple-element.16.att_ref, bf16[512,256]{1,0:T(8,128)(2,1)S(1)} %copy-done.2, ...), custom_call_target="tpu_custom_call" | custom-call | flops 4000000000 | bytes 2097152 | tf_op jit(solution)/shard_map/pallas_call | solution.py:247
  134.3 0.1 broadcast_in_dim.32
  134.4 13.0 %all_to_all.53 = f32[16,1,512]{2,1,0:T(1,128)S(1)} all-to-all(f32[16,1,512]{2,1,0:T(1,128)S(1)} %broadcast_in_dim.32), channel_id=1, replica_groups=mesh['frame'=32,'head'=16] {'head'}, dimensions={0} | all-to-all | bytes 65536 | tf_op jit(solution)/shard_map/all_to_all | solution.py:345
  147.4 0.0 copy-done
  147.4 1.0 shard_map.95
  (9 shorter events, 0.1 us)
Async XLA Ops:
  1.9 11.0 %collective-permute-start = (bf16[1024,256]{1,0:T(8,128)(2,1)S(1)}, bf16[1024,256]{1,0:T(8,128)(2,1)S(1)}, u32[]{:S(2)}, u32[]{:S(2)}) collective-permute-start(bf16[1024,256]{1,0:T(8,128)(2,1)S(1)} %constant_dynamic-update-slice_fusion.kv_ref), channel_id=1, source_target_pairs={{0,16},{16,32},{32,48},{48,64},{64,80},{80,96},{96,112},{112,128},... | collective-permute-start | bytes 1572872 | tf_op jit(solution)/shard_map/ppermute | solution.py:281
  10.5 1.0 copy-start.1
  87.7 41.8 %copy-start.2 = (bf16[512,256]{1,0:T(8,128)(2,1)S(1)}, bf16[512,256]{1,0:T(8,128)(2,1)}, u32[]{:S(2)}) copy-start(bf16[512,256]{1,0:T(8,128)(2,1)} %q_ref.5) | copy-start | bytes 786436
  102.8 12.1 %collective-permute-start.1 = (f32[96,128]{1,0:T(8,128)S(1)}, f32[96,128]{1,0:T(8,128)S(1)}, u32[]{:S(2)}, u32[]{:S(2)}) collective-permute-start(f32[96,128]{1,0:T(8,128)S(1)} %reduce_sum.19), channel_id=1, source_target_pairs={{0,128},{16,144},{32,160},{48,176},{64,192},{80,208},{96,224},{112... | collective-permute-start | bytes 147464 | tf_op jit(solution)/shard_map/ppermute | solution.py:330
  129.5 17.9 %copy-start = (f32[256]{0:T(256)S(1)}, f32[256]{0:T(256)}, u32[]{:S(2)}) copy-start(f32[256]{0:T(256)} %param.17) | copy-start | bytes 3076

commit v3 on v2

--- a/solution.py
+++ b/solution.py
@@ -10,7 +10,8 @@
 NS_ITERS = 5
 quintic_terms = (3.4445, -4.775, 2.0315)
 f32, bf16 = jnp.float32, jnp.bfloat16
-WIRE = f32
+f16 = jnp.float16
+TOP = 12.0
 ROWS = 128
 
 inside = (((1,), (0,)), ((), ()))
@@ -124,10 +125,60 @@
         ref[(first + no) * rows : (first + no + 1) * rows, :] = matrix.astype(ref.dtype)
 
 
+def store_scaled(ref, matrices):
+    dim = matrices[0].shape[0]
+    piece = ref.shape[1] - 8
+    unit = math.gcd(piece, dim)
+    peak = matrices[0]
+    for matrix in matrices[1:]:
+        peak = jnp.maximum(jnp.abs(peak), jnp.abs(matrix))
+    peak = jnp.max(jnp.max(jnp.abs(peak), axis=1, keepdims=True), axis=0, keepdims=True)
+    exponent = jnp.floor(jnp.log2(jnp.maximum(peak, 1e-30)))
+    factor = jnp.exp2(TOP - exponent)
+    for no, matrix in enumerate(matrices):
+        for step in range(dim // unit):
+            row = no * dim + step * unit
+            place = slice(row % piece, row % piece + unit)
+            ref[row // piece, place, :] = matrix[step * unit : (step + 1) * unit, :] * factor
+    for no in range(ref.shape[0]):
+        ref[no, piece:, :] = jnp.broadcast_to(exponent, (8, dim))
+
+
 def load_matrices(ref, dim):
     return [
         ref[no * dim : (no + 1) * dim, :].astype(f32) for no in range(ref.shape[0] // dim)
     ]
+
+
+def combine_kernel(*refs):
+    parts, out_ref = refs[:-1], refs[-1]
+    piece = out_ref.shape[0] - 8
+    terms = [(ref, no) for ref in parts for no in range(ref.shape[0])]
+    exponents = [ref[no, piece : piece + 1, :] for ref, no in terms]
+    exponent = exponents[0]
+    for other in exponents[1:]:
+        exponent = jnp.maximum(exponent, other)
+    exponent = exponent + float(math.ceil(math.log2(len(terms))))
+    total = None
+    for (ref, no), own in zip(terms, exponents):
+        term = ref[no, :piece, :] * jnp.exp2(own - exponent)
+        total = term if total is None else total + term
+    out_ref[:piece, :] = total
+    out_ref[piece:, :] = jnp.broadcast_to(exponent, (8, total.shape[1]))
+
+
+def load_scaled(ref):
+    piece, dim = ref.shape[1] - 8, ref.shape[2]
+    unit = math.gcd(piece, dim)
+    factors = [jnp.exp2(ref[no, piece : piece + 1, :] - TOP) for no in range(ref.shape[0])]
+    matrices = []
+    for first in range(0, ref.shape[0] * piece, dim):
+        chunks = []
+        for row in range(first, first + dim, unit):
+            place = slice(row % piece, row % piece + unit)
+            chunks.append(ref[row // piece, place, :] * factors[row // piece])
+        matrices.append(jnp.concatenate(chunks, axis=0))
+    return matrices
 
 
 def within_kernel(q_ref, kv_ref, prob_ref, stat_ref):
@@ -158,6 +209,7 @@
     scale = math.log2(math.e) / math.sqrt(dim)
     bias = jnp.where(scalars[0] == 0, -1e30, 0.0).astype(f32)
     weights = initial_of(weights_ref)
+    grads = []
     for head_no in range(heads):
         cols = slice(head_no * dim, (head_no + 1) * dim)
         for block in range(frame_len // ROWS):
@@ -175,10 +227,10 @@
             mixed = mixed + dot(within, kv_ref[frame_len:, cols], inside)
             square = jnp.mean(mixed * mixed, axis=1, keepdims=True)
             att_ref[here, cols] = (mixed * lax.rsqrt(square + 1e-06)).astype(bf16)
-        grads = fast_grads(
+        grads += fast_grads(
             weights[3 * head_no : 3 * head_no + 3], att_ref[:, cols], kv_ref[frame_len:, cols]
         )
-        store_matrices(grad_ref, 3 * head_no, grads)
+    store_scaled(grad_ref, grads)
 
 
 def second_kernel(scalars, total_ref, att_ref, kv_ref, weights_ref, weight_ref, grad_ref):
@@ -186,14 +238,17 @@
     heads = weights_ref.shape[0] // 3
     initial = initial_of(weights_ref)
     steps = [scalars[2 + head_no] for head_no in range(heads)]
-    weights = renewed(initial, load_matrices(total_ref, dim), initial, steps)
+    weights = renewed(initial, load_scaled(total_ref), initial, steps)
     store_matrices(weight_ref, 0, weights)
+    grads = []
     for head_no in range(heads):
         cols = slice(head_no * dim, (head_no + 1) * dim)
-        grads = fast_grads(
-            weights[3 * head_no : 3 * head_no + 3], att_ref[:, cols], kv_ref[att_ref.shape[0] :, cols]
+        grads += fast_grads(
+            weights[3 * head_no : 3 * head_no + 3],
+            att_ref[:, cols],
+            kv_ref[att_ref.shape[0] :, cols],
         )
-        store_matrices(grad_ref, 3 * head_no, grads)
+    store_scaled(grad_ref, grads)
 
 
 def apply_kernel(
@@ -204,7 +259,7 @@
     initial = initial_of(weights_ref)
     steps = [scalars[2 + head_no] for head_no in range(heads)]
     earlier = load_matrices(weight_ref, dim)
-    weights = renewed(earlier, load_matrices(total_ref, dim), initial, steps)
+    weights = renewed(earlier, load_scaled(total_ref), initial, steps)
     late = scalars[1] != 0
     weights = [jnp.where(late, new, old) for new, old in zip(weights, earlier)]
     for head_no in range(heads):
@@ -289,7 +344,7 @@
     )
     attended, grads = call(
         attend_kernel,
-        [((frame_len, width), bf16), ((rows, dim), WIRE)],
+        [((frame_len, width), bf16), ((near, piece + 8, dim), f32)],
         scalars,
         queries,
         past,
@@ -301,23 +356,21 @@
         flops=3 * 10**9,
     )
 
-    def near_sum(grads):
-        return jnp.sum(exchange(grads, near_groups).reshape(near, piece, dim).astype(f32), axis=0)
-
-    def spread(part):
-        part = part.astype(WIRE)
-        return exchange(
-            jnp.broadcast_to(part[None], (near, piece, dim)).reshape(rows, dim), near_groups
-        )
-
-    part = near_sum(grads).astype(WIRE)
-    parts = exchange(
-        jnp.broadcast_to(part[None], (4, piece, dim)).reshape(4 * piece, dim), far_groups
-    ).reshape(4, piece, dim)
-    total = spread(parts[0].astype(f32) + parts[1].astype(f32))
+    def combined_of(*parts):
+        return call(combine_kernel, [((piece + 8, dim), f32)], *parts)[0]
+
+    def wired(part, copies, groups):
+        part = part.astype(f16)
+        if copies:
+            part = jnp.broadcast_to(part[None], (copies,) + part.shape)
+        return exchange(part, groups).astype(f32)
+
+    part = combined_of(wired(grads, 0, near_groups))
+    part = combined_of(wired(part, 4, far_groups)[:2])
+    total = wired(part, near, near_groups)
     weights, grads = call(
         second_kernel,
-        [((rows, dim), f32), ((rows, dim), WIRE)],
+        [((rows, dim), f32), ((near, piece + 8, dim), f32)],
         scalars,
         total,
         attended,
@@ -326,9 +379,10 @@
         scalars=1,
         flops=4 * 10**9,
     )
-    part = near_sum(grads).astype(WIRE)
+    part = combined_of(wired(grads, 0, near_groups))
     other = lax.ppermute(part, "frame", [(i, i ^ near) for i in range(frames)])
-    total = spread(part.astype(f32) + other.astype(f32))
+    part = combined_of(part[None], other[None])
+    total = wired(part, near, near_groups)
     combined, square = call(
         apply_kernel,
         [((frame_len, width), f32), ((8, frame_len), f32)],

time: 149 us -> 130 us (0.87)
  blocking collectives: 107 us -> 86 us
  waiting for transfers between devices: 10 us -> 11.5 us
    all_to_all x5, blocking collectives: 93.6 us -> 72.9 us  [exchange(): lax.all_to_all(array, 'frame', split_axis=0, concat_axis=0, tiled=True, a...]
    pallas_call x5 -> x9, Pallas kernels: 17.1 us -> 17.5 us  [call(): pl.pallas_call(kernel, out_shape=shapes, in_specs=first + [spec] * (len(a...]
  transfers between devices with their start and end apart: 2 -> 2, of which waited for: 2 -> 2; matrix products, arithmetic and copies ran while one was open for 2% -> 3% of each run, Pallas kernels for 0% -> 1%
where the time goes in v3:
time: 130 us; the launch traced here: 129 us
  blocking collectives  86 us (66%)
  Pallas kernels  17.5 us (13%)
  waiting for transfers between devices  11.5 us (9%)
  starting transfers between devices  6.87 us (5%)
  local copies, waits for them, and re-layouts  5.79 us (4%)
    all_to_all x5, blocking collectives, exchange(): lax.all_to_all(array, 'frame', split_axis=0, concat_axis=0, tiled=True, a...  72.9 us
    pallas_call x9, Pallas kernels, call(): pl.pallas_call(kernel, out_shape=shapes, in_specs=first + [spec] * (len(a...  17.5 us
    all_to_all x1, blocking collectives, shards(): lax.all_to_all(jnp.broadcast_to(square[:1], (columns, frame_len)), 'head'...  13 us
    ppermute x1, waiting for transfers between devices, shards(): other = lax.ppermute(part, 'frame', [(i, i ^ near) for i in range(frames)])  10.6 us
    ppermute x1, starting transfers between devices, shards(): past = lax.ppermute(here, 'frame', route)  4.94 us
    unnamed x10, local copies, waits for them, and re-layouts  3.76 us
  transfers between devices with their start and end apart: 2, of which 2 were waited for; matrix products, arithmetic and copies ran while one was open for 3% of the time, Pallas kernels for 1%

profile of v3, /device:TPU:1, one launch (start us, length us, event | category | flops | bytes accessed | tf_op | source)
XLA Modules:
  0.0 128.9 jit_solution(4642128084087756541)
XLA Ops:
  0.0 1.0 constant_dynamic-update-slice_fusion.1
  1.0 1.0 constant_dynamic-update-slice_fusion.kv_ref
  1.9 4.9 %collective-permute-start = (bf16[1024,256]{1,0:T(8,128)(2,1)S(1)}, bf16[1024,256]{1,0:T(8,128)(2,1)S(1)}, u32[]{:S(2)}, u32[]{:S(2)}) collective-permute-start(bf16[1024,256]{1,0:T(8,128)(2,1)S(1)} %constant_dynamic-update-slice_fusion.kv_ref), channel_id=1, source_target_pairs={{0,16},{16,32},{32,48},{48,64},{64,80},{80,96},{96,112},{112,128},... | collective-permute-start | bytes 1572872 | tf_op jit(solution)/shard_map/ppermute | solution.py:336
  6.9 0.9 constant_dynamic-update-slice_fusion.4
  7.8 0.1 add_convert_fusion
  7.9 0.7 pad_maximum_fusion.scalars
  8.7 0.9 constant_dynamic-update-slice_fusion.3
  9.6 0.9 constant_dynamic-update-slice_fusion.2.weights_ref
  10.5 0.0 copy-start.1
  10.5 0.9 copy-done.1
  11.4 0.6 shard_map.91
  12.1 0.9 collective-permute-done.past_ref
  13.0 6.1 %shard_map.92 = (bf16[512,256]{1,0:T(8,128)(2,1)S(1)}, f32[8,104,128]{2,1,0:T(8,128)S(1)}) custom-call(f32[6]{0:T(128)S(1)} %pad_maximum_fusion.scalars, bf16[512,256]{1,0:T(8,128)(2,1)S(1)} %copy-done.1, bf16[1024,256]{1,0:T(8,128)(2,1)S(1)} %collective-permute-done.past_ref, bf16[1024,256]{1,0:T(8,128)(2,1)S(1)} %constant_dynamic-update-slice_fusion.kv_ref, ...), custom_call_target="tpu_custom_call" | custom-call | flops 3000000000 | bytes 2097152 | tf_op jit(solution)/shard_map/pallas_call | solution.py:302
  19.1 13.7 %all_to_all.33 = f16[8,104,128]{2,1,0:T(8,128)(2,1)S(1)} all-to-all(f16[8,104,128]{2,1,0:T(8,128)(2,1)S(1)} %convert_element_type.32), channel_id=1, replica_groups={{0,16,32,48,64,80,96,112},{128,144,160,176,192,208,224,240},{256,272,28..., dimensions={0} | all-to-all | bytes 425984 | tf_op jit(solution)/shard_map/all_to_all | solution.py:314
  33.0 24.2 %all_to_all.34 = f16[4,104,128]{2,1,0:T(8,128)(2,1)S(1)} all-to-all(f16[4,104,128]{2,1,0:T(8,128)(2,1)S(1)} %broadcast_in_dim.14), channel_id=1, replica_groups={{0,128,256,384},{16,144,272,400},{32,160,288,416},{48,176,304,432},{64,..., dimensions={0} | all-to-all | bytes 212992 | tf_op jit(solution)/shard_map/all_to_all | solution.py:314
  57.3 13.7 %all_to_all.35 = f16[8,104,128]{2,1,0:T(8,128)(2,1)S(1)} all-to-all(f16[8,104,128]{2,1,0:T(8,128)(2,1)S(1)} %broadcast_in_dim.15), channel_id=1, replica_groups={{0,16,32,48,64,80,96,112},{128,144,160,176,192,208,224,240},{256,272,28..., dimensions={0} | all-to-all | bytes 425984 | tf_op jit(solution)/shard_map/all_to_all | solution.py:314
  71.0 4.9 %shard_map.95 = (f32[768,128]{1,0:T(8,128)S(1)}, f32[8,104,128]{2,1,0:T(8,128)S(1)}) custom-call(f32[6]{0:T(128)S(1)} %pad_maximum_fusion.scalars, f32[8,104,128]{2,1,0:T(8,128)S(1)} %convert_element_type.36.total_ref, bf16[512,256]{1,0:T(8,128)(2,1)S(1)} %get-tuple-element.16.att_ref, bf16[1024,256]{1,0:T(8,128)(2,1)S(1)} %constant_dynamic-update-slice_fusion.kv_ref, ...), custom_call_target="tpu_custom_call" | custom-call | flops 4000000000 | bytes 2097152 | tf_op jit(solution)/shard_map/pallas_call | solution.py:302
  75.9 0.0 copy-start.2
  76.0 11.2 %all_to_all.36 = f16[8,104,128]{2,1,0:T(8,128)(2,1)S(1)} all-to-all(f16[8,104,128]{2,1,0:T(8,128)(2,1)S(1)} %convert_element_type.37), channel_id=1, replica_groups={{0,16,32,48,64,80,96,112},{128,144,160,176,192,208,224,240},{256,272,28..., dimensions={0} | all-to-all | bytes 425984 | tf_op jit(solution)/shard_map/all_to_all | solution.py:314
  87.3 1.9 %collective-permute-start.1 = (f32[104,128]{1,0:T(8,128)S(1)}, f32[104,128]{1,0:T(8,128)S(1)}, u32[]{:S(2)}, u32[]{:S(2)}) collective-permute-start(f32[104,128]{1,0:T(8,128)S(1)} %shard_map.96), channel_id=1, source_target_pairs={{0,128},{16,144},{32,160},{48,176},{64,192},{80,208},{96,224},{112... | collective-permute-start | bytes 159752 | tf_op jit(solution)/shard_map/ppermute | solution.py:383
  89.2 10.6 %collective-permute-done.1 = f32[104,128]{1,0:T(8,128)S(1)} collective-permute-done((f32[104,128]{1,0:T(8,128)S(1)}, f32[104,128]{1,0:T(8,128)S(1)}, u32[]{:S(2)}, u32[]{:S(2)}) %collective-permute-start.1) | collective-permute-done | bytes 53280 | tf_op jit(solution)/shard_map/ppermute | solution.py:383
  99.8 10.1 %all_to_all.37 = f16[8,104,128]{2,1,0:T(8,128)(2,1)S(1)} all-to-all(f16[8,104,128]{2,1,0:T(8,128)(2,1)S(1)} %broadcast_in_dim.36), channel_id=1, replica_groups={{0,16,32,48,64,80,96,112},{128,144,160,176,192,208,224,240},{256,272,28..., dimensions={0} | all-to-all | bytes 425984 | tf_op jit(solution)/shard_map/all_to_all | solution.py:314
  110.0 0.0 copy-done.2
  110.0 0.0 copy-start
  110.0 4.8 %shard_map.98 = (f32[512,256]{1,0:T(8,128)S(1)}, f32[8,512]{1,0:T(8,128)S(1)}) custom-call(f32[6]{0:T(128)S(1)} %pad_maximum_fusion.scalars, f32[8,104,128]{2,1,0:T(8,128)S(1)} %convert_element_type.40.total_ref, f32[768,128]{1,0:T(8,128)S(1)} %get-tuple-element.18.weight_ref, bf16[512,256]{1,0:T(8,128)(2,1)S(1)} %get-tuple-element.16.att_ref, ...), custom_call_target="tpu_custom_call" | custom-call | flops 4000000000 | bytes 2097152 | tf_op jit(solution)/shard_map/pallas_call | solution.py:302
  114.8 0.1 broadcast_in_dim.37
  114.8 13.0 %all_to_all.38 = f32[16,1,512]{2,1,0:T(1,128)S(1)} all-to-all(f32[16,1,512]{2,1,0:T(1,128)S(1)} %broadcast_in_dim.37), channel_id=1, replica_groups=mesh['frame'=32,'head'=16] {'head'}, dimensions={0} | all-to-all | bytes 65536 | tf_op jit(solution)/shard_map/all_to_all | solution.py:399
  127.9 0.0 copy-done
  127.9 1.0 shard_map.99
  (19 shorter events, 0.4 us)
Async XLA Ops:
  1.9 11.0 %collective-permute-start = (bf16[1024,256]{1,0:T(8,128)(2,1)S(1)}, bf16[1024,256]{1,0:T(8,128)(2,1)S(1)}, u32[]{:S(2)}, u32[]{:S(2)}) collective-permute-start(bf16[1024,256]{1,0:T(8,128)(2,1)S(1)} %constant_dynamic-update-slice_fusion.kv_ref), channel_id=1, source_target_pairs={{0,16},{16,32},{32,48},{48,64},{64,80},{80,96},{96,112},{112,128},... | collective-permute-start | bytes 1572872 | tf_op jit(solution)/shard_map/ppermute | solution.py:336
  10.5 1.0 copy-start.1
  75.9 34.0 %copy-start.2 = (bf16[512,256]{1,0:T(8,128)(2,1)S(1)}, bf16[512,256]{1,0:T(8,128)(2,1)}, u32[]{:S(2)}) copy-start(bf16[512,256]{1,0:T(8,128)(2,1)} %q_ref.5) | copy-start | bytes 786436
  87.3 12.5 %collective-permute-start.1 = (f32[104,128]{1,0:T(8,128)S(1)}, f32[104,128]{1,0:T(8,128)S(1)}, u32[]{:S(2)}, u32[]{:S(2)}) collective-permute-start(f32[104,128]{1,0:T(8,128)S(1)} %shard_map.96), channel_id=1, source_target_pairs={{0,128},{16,144},{32,160},{48,176},{64,192},{80,208},{96,224},{112... | collective-permute-start | bytes 159752 | tf_op jit(solution)/shard_map/ppermute | solution.py:383
  110.0 17.9 %copy-start = (f32[256]{0:T(256)S(1)}, f32[256]{0:T(256)}, u32[]{:S(2)}) copy-start(f32[256]{0:T(256)} %param.17) | copy-start | bytes 3076

commit v4 on v3

--- a/solution.py
+++ b/solution.py
@@ -12,7 +12,6 @@
 f32, bf16 = jnp.float32, jnp.bfloat16
 f16 = jnp.float16
 TOP = 12.0
-ROWS = 128
 
 inside = (((1,), (0,)), ((), ()))
 across = (((1,), (1,)), ((), ()))
@@ -28,18 +27,14 @@
     return high, low
 
 
-def rows2(high, low):
-    return jnp.concatenate([jnp.concatenate([high, high], 1), jnp.concatenate([low, low], 1)], 0)
-
-
-def cols2(high, low):
-    both = jnp.concatenate([high, low], 1)
-    return jnp.concatenate([both, both], 0)
-
-
 def folded(wide):
     half = wide.shape[1] // 2
     return wide[:, :half] + wide[:, half:]
+
+
+def product(left, right, dims):
+    both = jnp.concatenate(right, 0 if dims == across else 1)
+    return folded(dot(left[0], both, dims)) + dot(left[1], right[0], dims)
 
 
 def newton_schulz(gradients):
@@ -49,21 +44,14 @@
         matrices.append(gradient / (jnp.sqrt(total) + 1e-07))
     for _ in range(NS_ITERS):
         split = [parts_of(matrix) for matrix in matrices]
-        squares = [
-            folded(dot(jnp.concatenate(pair, 1), rows2(*pair), across)) for pair in split
-        ]
+        squares = [product(pair, pair, across) for pair in split]
         halves = [parts_of(square) for square in squares]
-        quartics = [
-            folded(dot(jnp.concatenate(pair, 1), cols2(*pair), inside)) for pair in halves
-        ]
+        quartics = [product(pair, pair, inside) for pair in halves]
         mixings = [
             parts_of(quintic_terms[1] * square + quintic_terms[2] * quartic)
             for square, quartic in zip(squares, quartics)
         ]
-        products = [
-            folded(dot(jnp.concatenate(pair, 1), cols2(*other), inside))
-            for pair, other in zip(mixings, split)
-        ]
+        products = [product(pair, other, inside) for pair, other in zip(mixings, split)]
         matrices = [
             quintic_terms[0] * matrix + product for matrix, product in zip(matrices, products)
         ]
@@ -91,7 +79,7 @@
     return both[:, :dim], both[:, dim:]
 
 
-def fast_grads(weights, key, value):
+def fast_grads(weights, key, value, key_t, value_t):
     gate_w, up_w, down_t = weights
     gate, upward = gate_and_up(key, gate_w, up_w)
     sigma = 1.0 / (1.0 + jnp.exp(-gate))
@@ -101,7 +89,6 @@
     back_gate = back * upward * sigma * (1.0 + gate * (1.0 - sigma))
     back_up = back * active
     gate_parts, up_parts, hidden_parts = parts_of(back_gate), parts_of(back_up), parts_of(hidden)
-    key_t, value_t = key.T, value.T
     dim = key.shape[1]
     both = dot(key_t, jnp.concatenate([gate_parts[0], up_parts[0]], 1), inside)
     both = both + dot(key_t, jnp.concatenate([gate_parts[1], up_parts[1]], 1), inside)
@@ -110,13 +97,7 @@
 
 
 def initial_of(weights_ref):
-    heads = weights_ref.shape[0] // 3
-    dim = weights_ref.shape[1]
-    weights = []
-    for head_no in range(heads):
-        weights += [weights_ref[head_no], weights_ref[heads + head_no]]
-        weights.append(weights_ref[2 * heads + head_no].T)
-    return weights
+    return [weights_ref[no] for no in range(weights_ref.shape[0])]
 
 
 def store_matrices(ref, first, matrices):
@@ -181,61 +162,113 @@
     return matrices
 
 
-def within_kernel(q_ref, kv_ref, prob_ref, stat_ref):
-    frame_len, width = q_ref.shape
-    dim = 128
-    heads = width // dim
-    scale = math.log2(math.e) / math.sqrt(dim)
-    for head_no in range(heads):
-        cols = slice(head_no * dim, (head_no + 1) * dim)
-        for block in range(frame_len // ROWS):
-            here = slice(block * ROWS, (block + 1) * ROWS)
-            place = slice(head_no * frame_len + block * ROWS, head_no * frame_len + (block + 1) * ROWS)
-            within = dot(q_ref[here, cols], kv_ref[0:frame_len, cols], across)
-            top = jnp.max(within, axis=1, keepdims=True)
-            within = jnp.exp2((within - top) * scale)
-            total = jnp.sum(within, axis=1, keepdims=True)
-            prob_ref[place, :] = within
-            stat_ref[place, 0:128] = jnp.broadcast_to(top, (ROWS, 128))
-            stat_ref[place, 128:256] = jnp.broadcast_to(total, (ROWS, 128))
+def exponentials(scores, top, dim):
+    return jnp.exp2((scores - top) * (math.log2(math.e) / math.sqrt(dim)))
+
+
+def within_kernel(
+    q_hbm,
+    k_hbm,
+    v_hbm,
+    gate_hbm,
+    up_hbm,
+    down_hbm,
+    q_ref,
+    v_ref,
+    norm_ref,
+    turned_ref,
+    weights_ref,
+    prob_ref,
+    stat_ref,
+    k_ref,
+    raw_ref,
+    sems,
+):
+    heads, dim = gate_hbm.shape[0], gate_hbm.shape[1]
+    frame_len = q_hbm.shape[0]
+    pairs = [(q_hbm, q_ref), (k_hbm, k_ref), (v_hbm, v_ref)]
+    pairs += [
+        (source, raw_ref.at[no * heads : (no + 1) * heads])
+        for no, source in enumerate([gate_hbm, up_hbm, down_hbm])
+    ]
+    copies = [
+        pltpu.make_async_copy(source, target, sems.at[no])
+        for no, (source, target) in enumerate(pairs)
+    ]
+    for copy in copies:
+        copy.start()
+    copies[0].wait()
+    copies[1].wait()
+    for head_no in range(heads):
+        cols = slice(head_no * dim, (head_no + 1) * dim)
+        scores = dot(k_ref[:, cols], q_ref[:, cols], across)
+        top = jnp.max(scores, axis=0, keepdims=True)
+        scores = exponentials(scores, top, dim)
+        prob_ref[head_no] = scores
+        stat_ref[head_no, 0:1, :] = top
+        stat_ref[head_no, 1:2, :] = jnp.sum(scores, axis=0, keepdims=True)
+        query = q_ref[:, cols].astype(f32)
+        square = jnp.mean(query * query, axis=1, keepdims=True)
+        norm_ref[:, cols] = (query * lax.rsqrt(square + 1e-06)).astype(bf16)
+    for copy in copies[2:]:
+        copy.wait()
+    for head_no in range(heads):
+        cols = slice(head_no * dim, (head_no + 1) * dim)
+        turned_ref[head_no] = v_ref[:, cols].T
+        weights_ref[3 * head_no] = raw_ref[head_no]
+        weights_ref[3 * head_no + 1] = raw_ref[heads + head_no]
+        weights_ref[3 * head_no + 2] = raw_ref[2 * heads + head_no].T
+
+
+def probs_kernel(scalars, q_ref, past_ref, prob_ref, stat_ref, turned_ref, share_ref, mixed_ref):
+    heads, dim, frame_len = turned_ref.shape
+    bias = jnp.where(scalars[0] == 0, -1e30, 0.0).astype(f32)
+    for head_no in range(heads):
+        cols = slice(head_no * dim, (head_no + 1) * dim)
+        before = dot(past_ref[:, cols], q_ref[:, cols], across) + bias
+        near_top = stat_ref[head_no, 0:1, :]
+        top = jnp.maximum(jnp.max(before, axis=0, keepdims=True), near_top)
+        before = exponentials(before, top, dim)
+        shrink = exponentials(near_top, top, dim)
+        total = jnp.sum(before, axis=0, keepdims=True) + stat_ref[head_no, 1:2, :] * shrink
+        share = 1.0 / total
+        share_ref[head_no] = (before * share).astype(bf16)
+        within = (prob_ref[head_no] * (shrink * share)).astype(bf16)
+        mixed_ref[head_no] = dot(turned_ref[head_no], within, inside)
 
 
 def attend_kernel(
-    scalars, q_ref, past_ref, kv_ref, weights_ref, prob_ref, stat_ref, att_ref, grad_ref
+    share_ref, mixed_ref, past_ref, v_ref, turned_ref, weights_ref, att_ref, att_t_ref, grad_ref
 ):
-    dim = weights_ref.shape[1]
-    heads = weights_ref.shape[0] // 3
-    frame_len = q_ref.shape[0]
-    scale = math.log2(math.e) / math.sqrt(dim)
-    bias = jnp.where(scalars[0] == 0, -1e30, 0.0).astype(f32)
+    heads, dim, frame_len = turned_ref.shape
     weights = initial_of(weights_ref)
     grads = []
     for head_no in range(heads):
         cols = slice(head_no * dim, (head_no + 1) * dim)
-        for block in range(frame_len // ROWS):
-            here = slice(block * ROWS, (block + 1) * ROWS)
-            place = slice(head_no * frame_len + block * ROWS, head_no * frame_len + (block + 1) * ROWS)
-            before = dot(q_ref[here, cols], past_ref[0:frame_len, cols], across) + bias
-            top_within = stat_ref[place, 0:1]
-            top = jnp.maximum(jnp.max(before, axis=1, keepdims=True), top_within)
-            before = jnp.exp2((before - top) * scale)
-            shrink = jnp.exp2((top_within - top) * scale)
-            total = jnp.sum(before, axis=1, keepdims=True) + stat_ref[place, 128:129] * shrink
-            share = 1.0 / total
-            mixed = dot((before * share).astype(bf16), past_ref[frame_len:, cols], inside)
-            within = (prob_ref[place, :] * (shrink * share)).astype(bf16)
-            mixed = mixed + dot(within, kv_ref[frame_len:, cols], inside)
-            square = jnp.mean(mixed * mixed, axis=1, keepdims=True)
-            att_ref[here, cols] = (mixed * lax.rsqrt(square + 1e-06)).astype(bf16)
+        mixed = mixed_ref[head_no] + dot(past_ref[:, cols].T, share_ref[head_no], inside)
+        square = jnp.mean(mixed * mixed, axis=0, keepdims=True)
+        att_t = (mixed * lax.rsqrt(square + 1e-06)).astype(bf16)
+        att = att_t.T
+        att_t_ref[head_no] = att_t
+        att_ref[:, cols] = att
         grads += fast_grads(
-            weights[3 * head_no : 3 * head_no + 3], att_ref[:, cols], kv_ref[frame_len:, cols]
+            weights[3 * head_no : 3 * head_no + 3], att, v_ref[:, cols], att_t, turned_ref[head_no]
         )
     store_scaled(grad_ref, grads)
 
 
-def second_kernel(scalars, total_ref, att_ref, kv_ref, weights_ref, weight_ref, grad_ref):
-    dim = weights_ref.shape[1]
-    heads = weights_ref.shape[0] // 3
+def second_kernel(
+    scalars,
+    total_ref,
+    att_ref,
+    att_t_ref,
+    v_ref,
+    turned_ref,
+    weights_ref,
+    weight_ref,
+    grad_ref,
+):
+    heads, dim, frame_len = turned_ref.shape
     initial = initial_of(weights_ref)
     steps = [scalars[2 + head_no] for head_no in range(heads)]
     weights = renewed(initial, load_scaled(total_ref), initial, steps)
@@ -246,13 +279,15 @@
         grads += fast_grads(
             weights[3 * head_no : 3 * head_no + 3],
             att_ref[:, cols],
-            kv_ref[att_ref.shape[0] :, cols],
+            v_ref[:, cols],
+            att_t_ref[head_no],
+            turned_ref[head_no],
         )
     store_scaled(grad_ref, grads)
 
 
 def apply_kernel(
-    scalars, total_ref, weight_ref, att_ref, q_ref, weights_ref, comb_ref, square_ref
+    scalars, total_ref, weight_ref, att_ref, norm_ref, weights_ref, comb_ref, square_ref
 ):
     dim = weights_ref.shape[1]
     heads = weights_ref.shape[0] // 3
@@ -265,14 +300,9 @@
     for head_no in range(heads):
         cols = slice(head_no * dim, (head_no + 1) * dim)
         gate_w, up_w, down_t = weights[3 * head_no : 3 * head_no + 3]
-        query = q_ref[:, cols].astype(f32)
-        square = jnp.mean(query * query, axis=1, keepdims=True)
-        query = (query * lax.rsqrt(square + 1e-06)).astype(bf16)
-        gate, upward = gate_and_up(query, gate_w, up_w)
+        gate, upward = gate_and_up(norm_ref[:, cols], gate_w, up_w)
         hidden = gate / (1.0 + jnp.exp(-gate)) * upward
-        output = folded(
-            dot(jnp.concatenate(parts_of(hidden), 1), rows2(*parts_of(down_t)), across)
-        )
+        output = product(parts_of(hidden), parts_of(down_t), across)
         fast_out = (output * scalars[2 + heads + head_no]).astype(bf16)
         comb_ref[:, cols] = att_ref[:, cols].astype(f32) + fast_out.astype(f32)
     combined = comb_ref[...]
@@ -299,6 +329,10 @@
     first = [pl.BlockSpec(memory_space=pltpu.SMEM)] * scalars
     first += [pl.BlockSpec(memory_space=pltpu.HBM)] * hbm
     shapes = [jax.ShapeDtypeStruct(*out) for out in outs]
+    args = [
+        pltpu.with_memory_space_constraint(arg, pltpu.HBM) if scalars <= no < scalars + hbm else arg
+        for no, arg in enumerate(args)
+    ]
     return pl.pallas_call(
         kernel,
         out_shape=shapes,
@@ -332,27 +366,55 @@
     scalars = jnp.concatenate([flags, step_size, head_scale])
 
     route = [(i, i + 1) for i in range(frames - 1)]
-    here = jnp.concatenate([key_rows, values], axis=0)
-    past = lax.ppermute(here, "frame", route)
-    all_weights = jnp.concatenate([gate_init, up_init, down_init], axis=0)
-    probs, stats = call(
+    keys_prev = lax.ppermute(key_rows, "frame", route)
+    values_prev = lax.ppermute(values, "frame", route)
+    turned = (heads, dim, frame_len)
+    queries_v, values_v, norms, values_t, weights_v, probs, stats = call(
         within_kernel,
-        [((heads * frame_len, frame_len), f32), ((heads * frame_len, 256), f32)],
+        [
+            ((frame_len, width), bf16),
+            ((frame_len, width), bf16),
+            ((frame_len, width), bf16),
+            (turned, bf16),
+            ((3 * heads, dim, dim), f32),
+            ((heads, frame_len, frame_len), f32),
+            ((heads, 8, frame_len), f32),
+        ],
         queries,
-        here,
+        key_rows,
+        values,
+        gate_init,
+        up_init,
+        down_init,
+        hbm=6,
+        scratch=[
+            pltpu.VMEM((frame_len, width), bf16),
+            pltpu.VMEM((3 * heads, dim, dim), f32),
+            pltpu.SemaphoreType.DMA((6,)),
+        ],
         flops=2 * 10**9,
     )
-    attended, grads = call(
-        attend_kernel,
-        [((frame_len, width), bf16), ((near, piece + 8, dim), f32)],
+    shares, mixed = call(
+        probs_kernel,
+        [((heads, frame_len, frame_len), bf16), (turned, f32)],
         scalars,
-        queries,
-        past,
-        here,
-        all_weights,
+        queries_v,
+        keys_prev,
         probs,
         stats,
+        values_t,
         scalars=1,
+        flops=2 * 10**9,
+    )
+    attended, attended_t, grads = call(
+        attend_kernel,
+        [((frame_len, width), bf16), (turned, bf16), ((near, piece + 8, dim), f32)],
+        shares,
+        mixed,
+        values_prev,
+        values_v,
+        values_t,
+        weights_v,
         flops=3 * 10**9,
     )
 
@@ -374,8 +436,10 @@
         scalars,
         total,
         attended,
-        here,
-        all_weights,
+        attended_t,
+        values_v,
+        values_t,
+        weights_v,
         scalars=1,
         flops=4 * 10**9,
     )
@@ -390,8 +454,8 @@
         total,
         weights,
         attended,
-        queries,
-        all_weights,
+        norms,
+        weights_v,
         scalars=1,
         flops=4 * 10**9,
     )

time: 130 us -> 123 us (0.946)
  local copies, waits for them, and re-layouts: 5.79 us -> 0.16 us
  starting transfers between devices: 6.87 us -> 8.78 us
  Pallas kernels: 17.5 us -> 16.1 us
    unnamed x10 -> x7, local copies, waits for them, and re-layouts: 3.76 us -> 0.02 us
    ppermute x1 -> x2, starting transfers between devices: 4.94 us -> 6.85 us  [the longest x1 4.93 us: shards(): keys_prev = lax.ppermute(key_rows, 'frame', route)]
    concatenate x2 -> x0, local copies, waits for them, and re-layouts: 1.89 us -> none  [the longest x1 0.97 us: shards(): here = jnp.concatenate([key_rows, values], axis=0)]
    pallas_call x9 -> x10, Pallas kernels: 17.5 us -> 16.1 us  [call(): pl.pallas_call(kernel, out_shape=shapes, in_specs=first + [spec] * (len(a...]
  transfers between devices with their start and end apart: 2 -> 3, of which waited for: 2 -> 2; matrix products, arithmetic and copies ran while one was open for 3% -> 0% of each run, Pallas kernels for 1% -> 3%
where the time goes in v4:
time: 123 us; the launch traced here: 122 us
  blocking collectives  85.7 us (70%)
  Pallas kernels  16.1 us (13%)
  waiting for transfers between devices  10.7 us (9%)
  starting transfers between devices  8.78 us (7%)
    all_to_all x5, blocking collectives, exchange(): lax.all_to_all(array, 'frame', split_axis=0, concat_axis=0, tiled=True, a...  72.6 us
    pallas_call x10, Pallas kernels, call(): pl.pallas_call(kernel, out_shape=shapes, in_specs=first + [spec] * (len(a...  16.1 us
    all_to_all x1, blocking collectives, shards(): lax.all_to_all(jnp.broadcast_to(square[:1], (columns, frame_len)), 'head'...  13 us
    ppermute x1, waiting for transfers between devices, shards(): other = lax.ppermute(part, 'frame', [(i, i ^ near) for i in range(frames)])  10.6 us
    ppermute x1, starting transfers between devices, shards(): keys_prev = lax.ppermute(key_rows, 'frame', route)  4.93 us
  transfers between devices with their start and end apart: 3, of which 2 were waited for; matrix products, arithmetic and copies ran while one was open for 0% of the time, Pallas kernels for 3%

profile of v4, /device:TPU:1, one launch (start us, length us, event | category | flops | bytes accessed | tf_op | source)
XLA Modules:
  0.0 122.0 jit_solution(7687596432626468212)
XLA Ops:
  0.0 4.9 %collective-permute-start = (bf16[512,256]{1,0:T(8,128)(2,1)}, bf16[512,256]{1,0:T(8,128)(2,1)S(1)}, u32[]{:S(2)}, u32[]{:S(2)}) collective-permute-start(bf16[512,256]{1,0:T(8,128)(2,1)} %k_hbm.1), channel_id=1, source_target_pairs={{0,16},{16,32},{32,48},{48,64},{64,80},{80,96},{96,112},{112,128},... | collective-permute-start | bytes 786440 | tf_op jit(solution)/shard_map/ppermute | solution.py:369
  4.9 1.9 %collective-permute-start.1 = (bf16[512,256]{1,0:T(8,128)(2,1)}, bf16[512,256]{1,0:T(8,128)(2,1)S(1)}, u32[]{:S(2)}, u32[]{:S(2)}) collective-permute-start(bf16[512,256]{1,0:T(8,128)(2,1)} %v_hbm.1), channel_id=1, source_target_pairs={{0,16},{16,32},{32,48},{48,64},{64,80},{80,96},{96,112},{112,128},... | collective-permute-start | bytes 786440 | tf_op jit(solution)/shard_map/ppermute | solution.py:370
  6.9 0.1 add_convert_fusion
  7.0 0.0 copy-start.1
  7.0 0.0 copy-start.2
  7.0 2.2 %shard_map.91 = (bf16[512,256]{1,0:T(8,128)(2,1)S(1)}, bf16[512,256]{1,0:T(8,128)(2,1)S(1)}, bf16[512,256]{1,0:T(8,128)(2,1)S(1)}, bf16[2,128,512]{2,1,0:T(8,128...) custom-call(bf16[512,256]{1,0:T(8,128)(2,1)} %q_hbm.1, ...), custom_call_target="tpu_custom_call" | custom-call | flops 2000000000 | bytes 2097152 | tf_op jit(solution)/shard_map/pallas_call | solution.py:336
  9.2 0.0 copy-done.1
  9.2 0.0 copy-done.2
  9.2 0.1 pad_maximum_fusion.scalars
  9.3 0.1 collective-permute-done.past_ref
  9.4 2.0 %shard_map.92 = (bf16[2,512,512]{2,1,0:T(8,128)(2,1)S(1)}, f32[2,128,512]{2,1,0:T(8,128)S(1)}) custom-call(f32[6]{0:T(128)S(1)} %pad_maximum_fusion.scalars, bf16[512,256]{1,0:T(8,128)(2,1)S(1)} %get-tuple-element.21.q_ref, bf16[512,256]{1,0:T(8,128)(2,1)S(1)} %collective-permute-done.past_ref, f32[2,512,512]{2,1,0:T(8,128)S(1)} %get-tuple-element.22.prob_ref, ...), custom_call_target="tpu_custom_call" | custom-call | flops 2000000000 | bytes 2097152 | tf_op jit(solution)/shard_map/pallas_call | solution.py:336
  11.4 0.0 collective-permute-done.1.past_ref
  11.4 1.7 %shard_map.93 = (bf16[512,256]{1,0:T(8,128)(2,1)S(1)}, bf16[2,128,512]{2,1,0:T(8,128)(2,1)S(1)}, f32[8,104,128]{2,1,0:T(8,128)S(1)}) custom-call(bf16[2,512,512]{2,1,0:T(8,128)(2,1)S(1)} %get-tuple-element.25.share_ref, f32[2,128,512]{2,1,0:T(8,128)S(1)} %get-tuple-element.26.mixed_ref, bf16[512,256]{1,0:T(8,128)(2,1)S(1)} %collective-permute-done.1.past_ref, ...), custom_call_target="tpu_custom_call" | custom-call | flops 3000000000 | bytes 2097152 | tf_op jit(solution)/shard_map/pallas_call | solution.py:336
  13.2 14.1 %all_to_all.33 = f16[8,104,128]{2,1,0:T(8,128)(2,1)S(1)} all-to-all(f16[8,104,128]{2,1,0:T(8,128)(2,1)S(1)} %convert_element_type.32), channel_id=1, replica_groups={{0,16,32,48,64,80,96,112},{128,144,160,176,192,208,224,240},{256,272,28..., dimensions={0} | all-to-all | bytes 425984 | tf_op jit(solution)/shard_map/all_to_all | solution.py:348
  27.4 23.7 %all_to_all.34 = f16[4,104,128]{2,1,0:T(8,128)(2,1)S(1)} all-to-all(f16[4,104,128]{2,1,0:T(8,128)(2,1)S(1)} %broadcast_in_dim.14), channel_id=1, replica_groups={{0,128,256,384},{16,144,272,400},{32,160,288,416},{48,176,304,432},{64,..., dimensions={0} | all-to-all | bytes 212992 | tf_op jit(solution)/shard_map/all_to_all | solution.py:348
  51.2 13.7 %all_to_all.35 = f16[8,104,128]{2,1,0:T(8,128)(2,1)S(1)} all-to-all(f16[8,104,128]{2,1,0:T(8,128)(2,1)S(1)} %broadcast_in_dim.15), channel_id=1, replica_groups={{0,16,32,48,64,80,96,112},{128,144,160,176,192,208,224,240},{256,272,28..., dimensions={0} | all-to-all | bytes 425984 | tf_op jit(solution)/shard_map/all_to_all | solution.py:348
  64.9 4.7 %shard_map.96 = (f32[768,128]{1,0:T(8,128)S(1)}, f32[8,104,128]{2,1,0:T(8,128)S(1)}) custom-call(f32[6]{0:T(128)S(1)} %pad_maximum_fusion.scalars, f32[8,104,128]{2,1,0:T(8,128)S(1)} %convert_element_type.36.total_ref, bf16[512,256]{1,0:T(8,128)(2,1)S(1)} %get-tuple-element.30.att_ref, bf16[2,128,512]{2,1,0:T(8,128)(2,1)S(1)} %get-tuple-element.31.att_t_ref, ...), custom_call_target="tpu_custom_call" | custom-call | flops 4000000000 | bytes 2097152 | tf_op jit(solution)/shard_map/pallas_call | solution.py:336
  69.6 11.1 %all_to_all.36 = f16[8,104,128]{2,1,0:T(8,128)(2,1)S(1)} all-to-all(f16[8,104,128]{2,1,0:T(8,128)(2,1)S(1)} %convert_element_type.37), channel_id=1, replica_groups={{0,16,32,48,64,80,96,112},{128,144,160,176,192,208,224,240},{256,272,28..., dimensions={0} | all-to-all | bytes 425984 | tf_op jit(solution)/shard_map/all_to_all | solution.py:348
  80.8 1.9 %collective-permute-start.2 = (f32[104,128]{1,0:T(8,128)S(1)}, f32[104,128]{1,0:T(8,128)S(1)}, u32[]{:S(2)}, u32[]{:S(2)}) collective-permute-start(f32[104,128]{1,0:T(8,128)S(1)} %shard_map.97), channel_id=1, source_target_pairs={{0,128},{16,144},{32,160},{48,176},{64,192},{80,208},{96,224},{112... | collective-permute-start | bytes 159752 | tf_op jit(solution)/shard_map/ppermute | solution.py:447
  82.8 10.6 %collective-permute-done.2 = f32[104,128]{1,0:T(8,128)S(1)} collective-permute-done((f32[104,128]{1,0:T(8,128)S(1)}, f32[104,128]{1,0:T(8,128)S(1)}, u32[]{:S(2)}, u32[]{:S(2)}) %collective-permute-start.2) | collective-permute-done | bytes 53280 | tf_op jit(solution)/shard_map/ppermute | solution.py:447
  93.4 10.1 %all_to_all.37 = f16[8,104,128]{2,1,0:T(8,128)(2,1)S(1)} all-to-all(f16[8,104,128]{2,1,0:T(8,128)(2,1)S(1)} %broadcast_in_dim.36), channel_id=1, replica_groups={{0,16,32,48,64,80,96,112},{128,144,160,176,192,208,224,240},{256,272,28..., dimensions={0} | all-to-all | bytes 425984 | tf_op jit(solution)/shard_map/all_to_all | solution.py:348
  103.5 0.0 copy-start
  103.5 4.4 %shard_map.99 = (f32[512,256]{1,0:T(8,128)S(1)}, f32[8,512]{1,0:T(8,128)S(1)}) custom-call(f32[6]{0:T(128)S(1)} %pad_maximum_fusion.scalars, f32[8,104,128]{2,1,0:T(8,128)S(1)} %convert_element_type.40.total_ref, f32[768,128]{1,0:T(8,128)S(1)} %get-tuple-element.33.weight_ref, bf16[512,256]{1,0:T(8,128)(2,1)S(1)} %get-tuple-element.30.att_ref, ...), custom_call_target="tpu_custom_call" | custom-call | flops 4000000000 | bytes 2097152 | tf_op jit(solution)/shard_map/pallas_call | solution.py:336
  107.9 0.1 broadcast_in_dim.37
  108.0 13.0 %all_to_all.38 = f32[16,1,512]{2,1,0:T(1,128)S(1)} all-to-all(f32[16,1,512]{2,1,0:T(1,128)S(1)} %broadcast_in_dim.37), channel_id=1, replica_groups=mesh['frame'=32,'head'=16] {'head'}, dimensions={0} | all-to-all | bytes 65536 | tf_op jit(solution)/shard_map/all_to_all | solution.py:463
  121.0 0.0 copy-done
  121.0 1.0 shard_map.100
  (19 shorter events, 0.4 us)
Async XLA Ops:
  0.0 9.4 %collective-permute-start = (bf16[512,256]{1,0:T(8,128)(2,1)}, bf16[512,256]{1,0:T(8,128)(2,1)S(1)}, u32[]{:S(2)}, u32[]{:S(2)}) collective-permute-start(bf16[512,256]{1,0:T(8,128)(2,1)} %k_hbm.1), channel_id=1, source_target_pairs={{0,16},{16,32},{32,48},{48,64},{64,80},{80,96},{96,112},{112,128},... | collective-permute-start | bytes 786440 | tf_op jit(solution)/shard_map/ppermute | solution.py:369
  4.9 6.5 %collective-permute-start.1 = (bf16[512,256]{1,0:T(8,128)(2,1)}, bf16[512,256]{1,0:T(8,128)(2,1)S(1)}, u32[]{:S(2)}, u32[]{:S(2)}) collective-permute-start(bf16[512,256]{1,0:T(8,128)(2,1)} %v_hbm.1), channel_id=1, source_target_pairs={{0,16},{16,32},{32,48},{48,64},{64,80},{80,96},{96,112},{112,128},... | collective-permute-start | bytes 786440 | tf_op jit(solution)/shard_map/ppermute | solution.py:370
  7.0 2.3 %copy-start.1 = (f32[2]{0:T(128)S(1)}, f32[2]{0:T(128)}, u32[]{:S(2)}) copy-start(f32[2]{0:T(128)} %param.16) | copy-start | bytes 28
  7.0 2.3 %copy-start.2 = (f32[2]{0:T(128)S(1)}, f32[2]{0:T(128)}, u32[]{:S(2)}) copy-start(f32[2]{0:T(128)} %param.15) | copy-start | bytes 28
  80.8 12.5 %collective-permute-start.2 = (f32[104,128]{1,0:T(8,128)S(1)}, f32[104,128]{1,0:T(8,128)S(1)}, u32[]{:S(2)}, u32[]{:S(2)}) collective-permute-start(f32[104,128]{1,0:T(8,128)S(1)} %shard_map.97), channel_id=1, source_target_pairs={{0,128},{16,144},{32,160},{48,176},{64,192},{80,208},{96,224},{112... | collective-permute-start | bytes 159752 | tf_op jit(solution)/shard_map/ppermute | solution.py:447
  103.5 17.5 %copy-start = (f32[256]{0:T(256)S(1)}, f32[256]{0:T(256)}, u32[]{:S(2)}) copy-start(f32[256]{0:T(256)} %param.17) | copy-start | bytes 3076

commit v5 on v4

--- a/solution.py
+++ b/solution.py
@@ -286,17 +286,24 @@
     store_scaled(grad_ref, grads)
 
 
-def apply_kernel(
-    scalars, total_ref, weight_ref, att_ref, norm_ref, weights_ref, comb_ref, square_ref
+def late_kernel(
+    scalars, weight_ref, att_ref, norm_ref, total_ref, weights_ref, comb_ref, square_ref
 ):
     dim = weights_ref.shape[1]
     heads = weights_ref.shape[0] // 3
     initial = initial_of(weights_ref)
     steps = [scalars[2 + head_no] for head_no in range(heads)]
-    earlier = load_matrices(weight_ref, dim)
-    weights = renewed(earlier, load_scaled(total_ref), initial, steps)
-    late = scalars[1] != 0
-    weights = [jnp.where(late, new, old) for new, old in zip(weights, earlier)]
+    weights = renewed(load_matrices(weight_ref, dim), load_scaled(total_ref), initial, steps)
+    apply_weights(weights, scalars, att_ref, norm_ref, comb_ref, square_ref)
+
+
+def early_kernel(scalars, weight_ref, att_ref, norm_ref, comb_ref, square_ref):
+    weights = load_matrices(weight_ref, weight_ref.shape[1])
+    apply_weights(weights, scalars, att_ref, norm_ref, comb_ref, square_ref)
+
+
+def apply_weights(weights, scalars, att_ref, norm_ref, comb_ref, square_ref):
+    heads, dim = len(weights) // 3, weights[0].shape[0]
     for head_no in range(heads):
         cols = slice(head_no * dim, (head_no + 1) * dim)
         gate_w, up_w, down_t = weights[3 * head_no : 3 * head_no + 3]
@@ -362,7 +369,7 @@
     far_groups = [list(range(i, frames, near)) for i in range(near)]
     rows = 3 * heads * dim
     piece = rows // near
-    flags = jnp.stack([position, position // (frames // 2)]).astype(f32)
+    flags = jnp.stack([position, position]).astype(f32)
     scalars = jnp.concatenate([flags, step_size, head_scale])
 
     route = [(i, i + 1) for i in range(frames - 1)]
@@ -427,7 +434,13 @@
             part = jnp.broadcast_to(part[None], (copies,) + part.shape)
         return exchange(part, groups).astype(f32)
 
-    part = combined_of(wired(grads, 0, near_groups))
+    late = position >= frames // 2
+    part = lax.cond(
+        late,
+        lambda grads: jnp.zeros((piece + 8, dim), f32),
+        lambda grads: combined_of(wired(grads, 0, near_groups)),
+        grads,
+    )
     part = combined_of(wired(part, 4, far_groups)[:2])
     total = wired(part, near, near_groups)
     weights, grads = call(
@@ -443,21 +456,48 @@
         scalars=1,
         flops=4 * 10**9,
     )
-    part = combined_of(wired(grads, 0, near_groups))
-    other = lax.ppermute(part, "frame", [(i, i ^ near) for i in range(frames)])
-    part = combined_of(part[None], other[None])
-    total = wired(part, near, near_groups)
-    combined, square = call(
-        apply_kernel,
-        [((frame_len, width), f32), ((8, frame_len), f32)],
+    results = [((frame_len, width), f32), ((8, frame_len), f32)]
+
+    def with_second_sum(scalars, weights, attended, norms, grads, weights_v):
+        part = combined_of(wired(grads, 0, near_groups))
+        other = lax.ppermute(part, "frame", [(i, i ^ near) for i in range(frames)])
+        part = combined_of(part[None], other[None])
+        total = wired(part, near, near_groups)
+        return call(
+            late_kernel,
+            results,
+            scalars,
+            weights,
+            attended,
+            norms,
+            total,
+            weights_v,
+            scalars=1,
+            flops=4 * 10**9,
+        )
+
+    def with_first_sum(scalars, weights, attended, norms, grads, weights_v):
+        return call(
+            early_kernel,
+            results,
+            scalars,
+            weights,
+            attended,
+            norms,
+            scalars=1,
+            flops=10**9,
+        )
+
+    combined, square = lax.cond(
+        late,
+        with_second_sum,
+        with_first_sum,
         scalars,
-        total,
         weights,
         attended,
         norms,
+        grads,
         weights_v,
-        scalars=1,
-        flops=4 * 10**9,
     )
     columns = lax.axis_size("head")
     squares = lax.all_to_all(

time: 123 us -> 110 us (0.89)
  the two profiles are of different devices: /device:TPU:1 before, /device:TPU:384 now
where the time goes in v5:
time: 110 us
  blocking collectives  75.6 us (69%)
  Pallas kernels  16.1 us (15%)
  starting transfers between devices  9.2 us (8%)
  waiting for transfers between devices  8.18 us (7%)
    all_to_all x4, blocking collectives, exchange(): lax.all_to_all(array, 'frame', split_axis=0, concat_axis=0, tiled=True, a...  61.1 us
    pallas_call x9, Pallas kernels, call(): pl.pallas_call(kernel, out_shape=shapes, in_specs=first + [spec] * (len(a...  16.1 us
    all_to_all x1, blocking collectives, shards(): lax.all_to_all(jnp.broadcast_to(square[:1], (columns, frame_len)), 'head'...  14.5 us
    ppermute x1, waiting for transfers between devices, with_second_sum(): other = lax.ppermute(part, 'frame', [(i, i ^ near) for i in range(frames)])  5.67 us
    ppermute x1, starting transfers between devices, with_second_sum(): other = lax.ppermute(part, 'frame', [(i, i ^ near) for i in range(frames)])  4.26 us
    ppermute x1, starting transfers between devices, shards(): values_prev = lax.ppermute(values, 'frame', route)  3.03 us
  transfers between devices with their start and end apart: 3, of which 3 were waited for; matrix products, arithmetic and copies ran while one was open for 0% of the time, Pallas kernels for 4%

profile of v5, /device:TPU:384, one launch (start us, length us, event | category | flops | bytes accessed | tf_op | source)
XLA Modules:
  0.0 109.9 jit_solution(1694655482762834668)
XLA Ops:
  0.0 1.9 %collective-permute-start.1 = (bf16[512,256]{1,0:T(8,128)(2,1)}, bf16[512,256]{1,0:T(8,128)(2,1)S(1)}, u32[]{:S(2)}, u32[]{:S(2)}) collective-permute-start(bf16[512,256]{1,0:T(8,128)(2,1)} %k_hbm.1), channel_id=1, source_target_pairs={{0,16},{16,32},{32,48},{48,64},{64,80},{80,96},{96,112},{112,128},... | collective-permute-start | bytes 786440 | tf_op jit(solution)/shard_map/ppermute | solution.py:376
  1.9 3.0 %collective-permute-start.2 = (bf16[512,256]{1,0:T(8,128)(2,1)}, bf16[512,256]{1,0:T(8,128)(2,1)S(1)}, u32[]{:S(2)}, u32[]{:S(2)}) collective-permute-start(bf16[512,256]{1,0:T(8,128)(2,1)} %v_hbm.1), channel_id=1, source_target_pairs={{0,16},{16,32},{32,48},{48,64},{64,80},{80,96},{96,112},{112,128},... | collective-permute-start | bytes 786440 | tf_op jit(solution)/shard_map/ppermute | solution.py:377
  5.0 0.1 add_convert_fusion
  5.0 0.0 copy-start.1
  5.0 0.0 copy-start.2
  5.0 2.2 %shard_map.91 = (bf16[512,256]{1,0:T(8,128)(2,1)S(1)}, bf16[512,256]{1,0:T(8,128)(2,1)S(1)}, bf16[512,256]{1,0:T(8,128)(2,1)S(1)}, bf16[2,128,512]{2,1,0:T(8,128...) custom-call(bf16[512,256]{1,0:T(8,128)(2,1)} %q_hbm.1, ...), custom_call_target="tpu_custom_call" | custom-call | flops 2000000000 | bytes 2097152 | tf_op jit(solution)/shard_map/pallas_call | solution.py:343
  7.3 0.0 copy-done.1
  7.3 0.0 copy-done.2
  7.3 0.1 pad_maximum_fusion.scalars
  7.4 1.7 %collective-permute-done.1.past_ref = bf16[512,256]{1,0:T(8,128)(2,1)S(1)} collective-permute-done((bf16[512,256]{1,0:T(8,128)(2,1)}, bf16[512,256]{1,0:T(8,128)(2,1)S(1)}, u32[]{:S(2)}, u32[]{:S(2)}) %collective-permute-start.1) | collective-permute-done | bytes 262176 | tf_op jit(solution)/shard_map/ppermute | solution.py:376
  9.1 2.0 %shard_map.92 = (bf16[2,512,512]{2,1,0:T(8,128)(2,1)S(1)}, f32[2,128,512]{2,1,0:T(8,128)S(1)}) custom-call(f32[6]{0:T(128)S(1)} %pad_maximum_fusion.scalars, bf16[512,256]{1,0:T(8,128)(2,1)S(1)} %get-tuple-element.55.q_ref, bf16[512,256]{1,0:T(8,128)(2,1)S(1)} %collective-permute-done.1.past_ref, f32[2,512,512]{2,1,0:T(8,128)S(1)} %get-tuple-element.56.prob_ref, ...), custom_call_target="tpu_custom_call" | custom-call | flops 2000000000 | bytes 2097152 | tf_op jit(solution)/shard_map/pallas_call | solution.py:343
  11.1 0.8 collective-permute-done.2.past_ref
  11.9 1.7 %shard_map.93 = (bf16[512,256]{1,0:T(8,128)(2,1)S(1)}, bf16[2,128,512]{2,1,0:T(8,128)(2,1)S(1)}, f32[8,104,128]{2,1,0:T(8,128)S(1)}) custom-call(bf16[2,512,512]{2,1,0:T(8,128)(2,1)S(1)} %get-tuple-element.59.share_ref, f32[2,128,512]{2,1,0:T(8,128)S(1)} %get-tuple-element.60.mixed_ref, bf16[512,256]{1,0:T(8,128)(2,1)S(1)} %collective-permute-done.2.past_ref, ...), custom_call_target="tpu_custom_call" | custom-call | flops 3000000000 | bytes 2097152 | tf_op jit(solution)/shard_map/pallas_call | solution.py:343
  13.7 25.3 %all_to_all.33 = f16[4,104,128]{2,1,0:T(8,128)(2,1)S(1)} all-to-all(f16[4,104,128]{2,1,0:T(8,128)(2,1)S(1)} %broadcast_in_dim.20), channel_id=1, replica_groups={{0,128,256,384},{16,144,272,400},{32,160,288,416},{48,176,304,432},{64,..., dimensions={0} | all-to-all | bytes 212992 | tf_op jit(solution)/shard_map/all_to_all | solution.py:355
  39.1 11.3 %all_to_all.34 = f16[8,104,128]{2,1,0:T(8,128)(2,1)S(1)} all-to-all(f16[8,104,128]{2,1,0:T(8,128)(2,1)S(1)} %broadcast_in_dim.21), channel_id=1, replica_groups={{0,16,32,48,64,80,96,112},{128,144,160,176,192,208,224,240},{256,272,28..., dimensions={0} | all-to-all | bytes 425984 | tf_op jit(solution)/shard_map/all_to_all | solution.py:355
  50.4 4.7 %shard_map.95 = (f32[768,128]{1,0:T(8,128)S(1)}, f32[8,104,128]{2,1,0:T(8,128)S(1)}) custom-call(f32[6]{0:T(128)S(1)} %pad_maximum_fusion.scalars, f32[8,104,128]{2,1,0:T(8,128)S(1)} %convert_element_type.39.total_ref, bf16[512,256]{1,0:T(8,128)(2,1)S(1)} %get-tuple-element.64.att_ref, bf16[2,128,512]{2,1,0:T(8,128)(2,1)S(1)} %get-tuple-element.65.att_t_ref, ...), custom_call_target="tpu_custom_call" | custom-call | flops 4000000000 | bytes 2097152 | tf_op jit(solution)/shard_map/pallas_call | solution.py:343
  55.0 0.0 copy-start
  55.1 39.3 %conditional.3 = ((f32[512,256]{1,0:T(8,128)S(1)}, f32[8,512]{1,0:T(8,128)S(1)})) conditional(s32[]{:T(128)} %convert_element_type.35, (f32[6]{0:T(128)S(1)}, f32[768,128]{1,0:T(8,128)S(1)}, bf16[512,256]{1,0:T(8,128)(2,1)S(1)}, bf16[512,256]{1,0:T(8,128)(2,1)S(1)}) %tuple.18, (f32[8,104,128]{2,1,0:T(8,128)S(1)}, f32[6]{0:T(128)S(1)}, ...), branch_computations={%region_2.0_spmd, %region_3.0_spmd} | conditional | flops 4000332800 | bytes 9592880 | solution.py:491
  55.1 11.1 %all_to_all.31 = f16[8,104,128]{2,1,0:T(8,128)(2,1)S(1)} all-to-all(f16[8,104,128]{2,1,0:T(8,128)(2,1)S(1)} %convert_element_type.26), channel_id=1, replica_groups={{0,16,32,48,64,80,96,112},{128,144,160,176,192,208,224,240},{256,272,28..., dimensions={0} | all-to-all | bytes 425984 | tf_op jit(solution)/shard_map/cond/branch_1_fun/all_to_all | solution.py:355
  66.3 4.3 %collective-permute-start = (f32[104,128]{1,0:T(8,128)S(1)}, f32[104,128]{1,0:T(8,128)S(1)}, u32[]{:S(2)}, u32[]{:S(2)}) collective-permute-start(f32[104,128]{1,0:T(8,128)S(1)} %branch_1_fun.3), channel_id=1, source_target_pairs={{0,128},{16,144},{32,160},{48,176},{64,192},{80,208},{96,224},{112... | collective-permute-start | bytes 159752 | tf_op jit(solution)/shard_map/cond/branch_1_fun/ppermute | solution.py:463
  70.6 5.7 %collective-permute-done = f32[104,128]{1,0:T(8,128)S(1)} collective-permute-done((f32[104,128]{1,0:T(8,128)S(1)}, f32[104,128]{1,0:T(8,128)S(1)}, u32[]{:S(2)}, u32[]{:S(2)}) %collective-permute-start) | collective-permute-done | bytes 53280 | tf_op jit(solution)/shard_map/cond/branch_1_fun/ppermute | solution.py:463
  76.3 13.5 %all_to_all.32 = f16[8,104,128]{2,1,0:T(8,128)(2,1)S(1)} all-to-all(f16[8,104,128]{2,1,0:T(8,128)(2,1)S(1)} %broadcast_in_dim.2), channel_id=1, replica_groups={{0,16,32,48,64,80,96,112},{128,144,160,176,192,208,224,240},{256,272,28..., dimensions={0} | all-to-all | bytes 425984 | tf_op jit(solution)/shard_map/cond/branch_1_fun/all_to_all | solution.py:355
  89.9 4.4 %branch_1_fun.5 = (f32[512,256]{1,0:T(8,128)S(1)}, f32[8,512]{1,0:T(8,128)S(1)}) custom-call(f32[6]{0:T(128)S(1)} %get-tuple-element.33.scalars, f32[768,128]{1,0:T(8,128)S(1)} %get-tuple-element.34.weight_ref, bf16[512,256]{1,0:T(8,128)(2,1)S(1)} %get-tuple-element.35.att_ref, bf16[512,256]{1,0:T(8,128)(2,1)S(1)} %get-tuple-element.36.norm_ref, ...), custom_call_target="tpu_custom_call" | custom-call | flops 4000000000 | bytes 2097152 | tf_op jit(solution)/shard_map/cond/branch_1_fun/pallas_call | solution.py:343
  94.4 14.5 %all_to_all.35 = f32[16,1,512]{2,1,0:T(1,128)S(1)} all-to-all(f32[16,1,512]{2,1,0:T(1,128)S(1)} %broadcast_in_dim.22), channel_id=1, replica_groups=mesh['frame'=32,'head'=16] {'head'}, dimensions={0} | all-to-all | bytes 65536 | tf_op jit(solution)/shard_map/all_to_all | solution.py:503
  108.9 0.0 copy-done
  108.9 1.0 shard_map.96
  (19 shorter events, 0.4 us)
Async XLA Ops:
  0.0 9.1 %collective-permute-start.1 = (bf16[512,256]{1,0:T(8,128)(2,1)}, bf16[512,256]{1,0:T(8,128)(2,1)S(1)}, u32[]{:S(2)}, u32[]{:S(2)}) collective-permute-start(bf16[512,256]{1,0:T(8,128)(2,1)} %k_hbm.1), channel_id=1, source_target_pairs={{0,16},{16,32},{32,48},{48,64},{64,80},{80,96},{96,112},{112,128},... | collective-permute-start | bytes 786440 | tf_op jit(solution)/shard_map/ppermute | solution.py:376
  1.9 10.0 %collective-permute-start.2 = (bf16[512,256]{1,0:T(8,128)(2,1)}, bf16[512,256]{1,0:T(8,128)(2,1)S(1)}, u32[]{:S(2)}, u32[]{:S(2)}) collective-permute-start(bf16[512,256]{1,0:T(8,128)(2,1)} %v_hbm.1), channel_id=1, source_target_pairs={{0,16},{16,32},{32,48},{48,64},{64,80},{80,96},{96,112},{112,128},... | collective-permute-start | bytes 786440 | tf_op jit(solution)/shard_map/ppermute | solution.py:377
  5.0 2.2 %copy-start.1 = (f32[2]{0:T(128)S(1)}, f32[2]{0:T(128)}, u32[]{:S(2)}) copy-start(f32[2]{0:T(128)} %param.20) | copy-start | bytes 28
  5.0 2.3 %copy-start.2 = (f32[2]{0:T(128)S(1)}, f32[2]{0:T(128)}, u32[]{:S(2)}) copy-start(f32[2]{0:T(128)} %param.19) | copy-start | bytes 28
  55.0 53.8 %copy-start = (f32[256]{0:T(256)S(1)}, f32[256]{0:T(256)}, u32[]{:S(2)}) copy-start(f32[256]{0:T(256)} %param.21) | copy-start | bytes 3076
  66.3 9.9 %collective-permute-start = (f32[104,128]{1,0:T(8,128)S(1)}, f32[104,128]{1,0:T(8,128)S(1)}, u32[]{:S(2)}, u32[]{:S(2)}) collective-permute-start(f32[104,128]{1,0:T(8,128)S(1)} %branch_1_fun.3), channel_id=1, source_target_pairs={{0,128},{16,144},{32,160},{48,176},{64,192},{80,208},{96,224},{112... | collective-permute-start | bytes 159752 | tf_op jit(solution)/shard_map/cond/branch_1_fun/ppermute | solution.py:463

commit v6 on v5

--- a/solution.py
+++ b/solution.py
@@ -357,6 +357,19 @@
     )
 
 
+def sum_groups(frames):
+    cores, chips = 2, frames // 8
+    half = chips // 2
+    turned = [(i + half) % chips for i in range(chips)]
+    orders = [list(range(chips)), turned, turned, list(range(chips))]
+    near_groups = [
+        [(group * chips + chip) * cores + core for chip in order for core in range(cores)]
+        for group, order in enumerate(orders)
+    ]
+    far_groups = [list(members) for members in zip(*near_groups)]
+    return near_groups, far_groups
+
+
 def shards(
     queries, key_rows, values, gate_init, up_init, down_init, step_size, head_scale, out_gain
 ):
@@ -365,8 +378,8 @@
     frames = lax.axis_size("frame")
     position = lax.axis_index("frame")
     near = frames // 4
-    near_groups = [list(range(near * i, near * i + near)) for i in range(4)]
-    far_groups = [list(range(i, frames, near)) for i in range(near)]
+    near_groups, far_groups = sum_groups(frames)
+    plain_groups = [list(range(near * i, near * i + near)) for i in range(4)]
     rows = 3 * heads * dim
     piece = rows // near
     flags = jnp.stack([position, position]).astype(f32)
@@ -459,10 +472,11 @@
     results = [((frame_len, width), f32), ((8, frame_len), f32)]
 
     def with_second_sum(scalars, weights, attended, norms, grads, weights_v):
-        part = combined_of(wired(grads, 0, near_groups))
-        other = lax.ppermute(part, "frame", [(i, i ^ near) for i in range(frames)])
+        part = combined_of(wired(grads, 0, plain_groups))
+        pairs = [(i, i ^ near) for i in range(frames // 2, frames)]
+        other = lax.ppermute(part.astype(f16), "frame", pairs).astype(f32)
         part = combined_of(part[None], other[None])
-        total = wired(part, near, near_groups)
+        total = wired(part, near, plain_groups)
         return call(
             late_kernel,
             results,

time: 110 us -> 107 us (0.973)
  blocking collectives: 75.6 us -> 72.6 us
    all_to_all x4, blocking collectives: 61.1 us -> 58.2 us  [exchange(): lax.all_to_all(array, 'frame', split_axis=0, concat_axis=0, tiled=True, a...]
where the time goes in v6:
time: 107 us
  blocking collectives  72.6 us (68%)
  Pallas kernels  16.1 us (15%)
  waiting for transfers between devices  8.93 us (8%)
  starting transfers between devices  8.16 us (8%)
    all_to_all x4, blocking collectives, exchange(): lax.all_to_all(array, 'frame', split_axis=0, concat_axis=0, tiled=True, a...  58.2 us
    pallas_call x9, Pallas kernels, call(): pl.pallas_call(kernel, out_shape=shapes, in_specs=first + [spec] * (len(a...  16.1 us
    all_to_all x1, blocking collectives, shards(): lax.all_to_all(jnp.broadcast_to(square[:1], (columns, frame_len)), 'head'...  14.5 us
    ppermute x1, waiting for transfers between devices, with_second_sum(): other = lax.ppermute(part.astype(f16), 'frame', pairs).astype(f32)  6.42 us
    ppermute x1, starting transfers between devices, with_second_sum(): other = lax.ppermute(part.astype(f16), 'frame', pairs).astype(f32)  3.22 us
    ppermute x1, starting transfers between devices, shards(): values_prev = lax.ppermute(values, 'frame', route)  3.03 us
  transfers between devices with their start and end apart: 3, of which 3 were waited for; matrix products, arithmetic and copies ran while one was open for 0% of the time, Pallas kernels for 4%

profile of v6, /device:TPU:384, one launch (start us, length us, event | category | flops | bytes accessed | tf_op | source)
XLA Modules:
  0.0 106.7 jit_solution(15972859191489834855)
XLA Ops:
  0.0 1.9 %collective-permute-start.1 = (bf16[512,256]{1,0:T(8,128)(2,1)}, bf16[512,256]{1,0:T(8,128)(2,1)S(1)}, u32[]{:S(2)}, u32[]{:S(2)}) collective-permute-start(bf16[512,256]{1,0:T(8,128)(2,1)} %k_hbm.1), channel_id=1, source_target_pairs={{0,16},{16,32},{32,48},{48,64},{64,80},{80,96},{96,112},{112,128},... | collective-permute-start | bytes 786440 | tf_op jit(solution)/shard_map/ppermute | solution.py:389
  1.9 3.0 %collective-permute-start.2 = (bf16[512,256]{1,0:T(8,128)(2,1)}, bf16[512,256]{1,0:T(8,128)(2,1)S(1)}, u32[]{:S(2)}, u32[]{:S(2)}) collective-permute-start(bf16[512,256]{1,0:T(8,128)(2,1)} %v_hbm.1), channel_id=1, source_target_pairs={{0,16},{16,32},{32,48},{48,64},{64,80},{80,96},{96,112},{112,128},... | collective-permute-start | bytes 786440 | tf_op jit(solution)/shard_map/ppermute | solution.py:390
  5.0 0.1 add_convert_fusion
  5.0 0.0 copy-start.1
  5.0 0.0 copy-start.2
  5.0 2.2 %shard_map.91 = (bf16[512,256]{1,0:T(8,128)(2,1)S(1)}, bf16[512,256]{1,0:T(8,128)(2,1)S(1)}, bf16[512,256]{1,0:T(8,128)(2,1)S(1)}, bf16[2,128,512]{2,1,0:T(8,128...) custom-call(bf16[512,256]{1,0:T(8,128)(2,1)} %q_hbm.1, ...), custom_call_target="tpu_custom_call" | custom-call | flops 2000000000 | bytes 2097152 | tf_op jit(solution)/shard_map/pallas_call | solution.py:343
  7.3 0.0 copy-done.1
  7.3 0.0 copy-done.2
  7.3 0.1 pad_maximum_fusion.scalars
  7.4 1.7 %collective-permute-done.1.past_ref = bf16[512,256]{1,0:T(8,128)(2,1)S(1)} collective-permute-done((bf16[512,256]{1,0:T(8,128)(2,1)}, bf16[512,256]{1,0:T(8,128)(2,1)S(1)}, u32[]{:S(2)}, u32[]{:S(2)}) %collective-permute-start.1) | collective-permute-done | bytes 262176 | tf_op jit(solution)/shard_map/ppermute | solution.py:389
  9.1 2.0 %shard_map.92 = (bf16[2,512,512]{2,1,0:T(8,128)(2,1)S(1)}, f32[2,128,512]{2,1,0:T(8,128)S(1)}) custom-call(f32[6]{0:T(128)S(1)} %pad_maximum_fusion.scalars, bf16[512,256]{1,0:T(8,128)(2,1)S(1)} %get-tuple-element.55.q_ref, bf16[512,256]{1,0:T(8,128)(2,1)S(1)} %collective-permute-done.1.past_ref, f32[2,512,512]{2,1,0:T(8,128)S(1)} %get-tuple-element.56.prob_ref, ...), custom_call_target="tpu_custom_call" | custom-call | flops 2000000000 | bytes 2097152 | tf_op jit(solution)/shard_map/pallas_call | solution.py:343
  11.1 0.8 collective-permute-done.2.past_ref
  11.9 1.7 %shard_map.93 = (bf16[512,256]{1,0:T(8,128)(2,1)S(1)}, bf16[2,128,512]{2,1,0:T(8,128)(2,1)S(1)}, f32[8,104,128]{2,1,0:T(8,128)S(1)}) custom-call(bf16[2,512,512]{2,1,0:T(8,128)(2,1)S(1)} %get-tuple-element.59.share_ref, f32[2,128,512]{2,1,0:T(8,128)S(1)} %get-tuple-element.60.mixed_ref, bf16[512,256]{1,0:T(8,128)(2,1)S(1)} %collective-permute-done.2.past_ref, ...), custom_call_target="tpu_custom_call" | custom-call | flops 3000000000 | bytes 2097152 | tf_op jit(solution)/shard_map/pallas_call | solution.py:343
  13.7 24.1 %all_to_all.33 = f16[4,104,128]{2,1,0:T(8,128)(2,1)S(1)} all-to-all(f16[4,104,128]{2,1,0:T(8,128)(2,1)S(1)} %broadcast_in_dim.22), channel_id=1, replica_groups={{0,192,320,384},{16,208,336,400},{32,224,352,416},{48,240,368,432},{64,..., dimensions={0} | all-to-all | bytes 212992 | tf_op jit(solution)/shard_map/all_to_all | solution.py:355
  37.9 11.8 %all_to_all.34 = f16[8,104,128]{2,1,0:T(8,128)(2,1)S(1)} all-to-all(f16[8,104,128]{2,1,0:T(8,128)(2,1)S(1)} %broadcast_in_dim.23), channel_id=1, replica_groups={{0,16,32,48,64,80,96,112},{192,208,224,240,128,144,160,176},{320,336,35..., dimensions={0} | all-to-all | bytes 425984 | tf_op jit(solution)/shard_map/all_to_all | solution.py:355
  49.7 4.7 %shard_map.95 = (f32[768,128]{1,0:T(8,128)S(1)}, f32[8,104,128]{2,1,0:T(8,128)S(1)}) custom-call(f32[6]{0:T(128)S(1)} %pad_maximum_fusion.scalars, f32[8,104,128]{2,1,0:T(8,128)S(1)} %convert_element_type.43.total_ref, bf16[512,256]{1,0:T(8,128)(2,1)S(1)} %get-tuple-element.64.att_ref, bf16[2,128,512]{2,1,0:T(8,128)(2,1)S(1)} %get-tuple-element.65.att_t_ref, ...), custom_call_target="tpu_custom_call" | custom-call | flops 4000000000 | bytes 2097152 | tf_op jit(solution)/shard_map/pallas_call | solution.py:343
  54.4 0.0 copy-start
  54.4 36.8 %conditional.3 = ((f32[512,256]{1,0:T(8,128)S(1)}, f32[8,512]{1,0:T(8,128)S(1)})) conditional(s32[]{:T(128)} %convert_element_type.39, (f32[6]{0:T(128)S(1)}, f32[768,128]{1,0:T(8,128)S(1)}, bf16[512,256]{1,0:T(8,128)(2,1)S(1)}, bf16[512,256]{1,0:T(8,128)(2,1)S(1)}) %tuple.18, (f32[8,104,128]{2,1,0:T(8,128)S(1)}, f32[6]{0:T(128)S(1)}, ...), branch_computations={%region_2.0_spmd, %region_3.0_spmd} | conditional | flops 4000359424 | bytes 9646128 | solution.py:505
  54.4 11.1 %all_to_all.31 = f16[8,104,128]{2,1,0:T(8,128)(2,1)S(1)} all-to-all(f16[8,104,128]{2,1,0:T(8,128)(2,1)S(1)} %convert_element_type.13), channel_id=1, replica_groups={{0,16,32,48,64,80,96,112},{128,144,160,176,192,208,224,240},{256,272,28..., dimensions={0} | all-to-all | bytes 425984 | tf_op jit(solution)/shard_map/cond/branch_1_fun/all_to_all | solution.py:355
  65.6 3.2 %collective-permute-start = (f16[104,128]{1,0:T(8,128)(2,1)S(1)}, f16[104,128]{1,0:T(8,128)(2,1)S(1)}, u32[]{:S(2)}, u32[]{:S(2)}) collective-permute-start(f16[104,128]{1,0:T(8,128)(2,1)S(1)} %convert_element_type.31), channel_id=1, source_target_pairs={{256,384},{272,400},{288,416},{304,432},{320,448},{336,464},{352,4... | collective-permute-start | bytes 79880 | tf_op jit(solution)/shard_map/cond/branch_1_fun/ppermute | solution.py:477
  68.9 6.4 %collective-permute-done = f16[104,128]{1,0:T(8,128)(2,1)S(1)} collective-permute-done((f16[104,128]{1,0:T(8,128)(2,1)S(1)}, f16[104,128]{1,0:T(8,128)(2,1)S(1)}, u32[]{:S(2)}, u32[]{:S(2)}) %collective-permute-start) | collective-permute-done | bytes 26656 | tf_op jit(solution)/shard_map/cond/branch_1_fun/ppermute | solution.py:477
  75.4 11.3 %all_to_all.32 = f16[8,104,128]{2,1,0:T(8,128)(2,1)S(1)} all-to-all(f16[8,104,128]{2,1,0:T(8,128)(2,1)S(1)} %broadcast_in_dim.5), channel_id=1, replica_groups={{0,16,32,48,64,80,96,112},{128,144,160,176,192,208,224,240},{256,272,28..., dimensions={0} | all-to-all | bytes 425984 | tf_op jit(solution)/shard_map/cond/branch_1_fun/all_to_all | solution.py:355
  86.6 4.4 %branch_1_fun.5 = (f32[512,256]{1,0:T(8,128)S(1)}, f32[8,512]{1,0:T(8,128)S(1)}) custom-call(f32[6]{0:T(128)S(1)} %get-tuple-element.33.scalars, f32[768,128]{1,0:T(8,128)S(1)} %get-tuple-element.34.weight_ref, bf16[512,256]{1,0:T(8,128)(2,1)S(1)} %get-tuple-element.35.att_ref, bf16[512,256]{1,0:T(8,128)(2,1)S(1)} %get-tuple-element.36.norm_ref, ...), custom_call_target="tpu_custom_call" | custom-call | flops 4000000000 | bytes 2097152 | tf_op jit(solution)/shard_map/cond/branch_1_fun/pallas_call | solution.py:343
  91.2 14.5 %all_to_all.35 = f32[16,1,512]{2,1,0:T(1,128)S(1)} all-to-all(f32[16,1,512]{2,1,0:T(1,128)S(1)} %broadcast_in_dim.36), channel_id=1, replica_groups=mesh['frame'=32,'head'=16] {'head'}, dimensions={0} | all-to-all | bytes 65536 | tf_op jit(solution)/shard_map/all_to_all | solution.py:517
  105.7 0.0 copy-done
  105.7 1.0 shard_map.96
  (21 shorter events, 0.4 us)
Async XLA Ops:
  0.0 9.1 %collective-permute-start.1 = (bf16[512,256]{1,0:T(8,128)(2,1)}, bf16[512,256]{1,0:T(8,128)(2,1)S(1)}, u32[]{:S(2)}, u32[]{:S(2)}) collective-permute-start(bf16[512,256]{1,0:T(8,128)(2,1)} %k_hbm.1), channel_id=1, source_target_pairs={{0,16},{16,32},{32,48},{48,64},{64,80},{80,96},{96,112},{112,128},... | collective-permute-start | bytes 786440 | tf_op jit(solution)/shard_map/ppermute | solution.py:389
  1.9 10.0 %collective-permute-start.2 = (bf16[512,256]{1,0:T(8,128)(2,1)}, bf16[512,256]{1,0:T(8,128)(2,1)S(1)}, u32[]{:S(2)}, u32[]{:S(2)}) collective-permute-start(bf16[512,256]{1,0:T(8,128)(2,1)} %v_hbm.1), channel_id=1, source_target_pairs={{0,16},{16,32},{32,48},{48,64},{64,80},{80,96},{96,112},{112,128},... | collective-permute-start | bytes 786440 | tf_op jit(solution)/shard_map/ppermute | solution.py:390
  5.0 2.2 %copy-start.1 = (f32[2]{0:T(128)S(1)}, f32[2]{0:T(128)}, u32[]{:S(2)}) copy-start(f32[2]{0:T(128)} %param.20) | copy-start | bytes 28
  5.0 2.3 %copy-start.2 = (f32[2]{0:T(128)S(1)}, f32[2]{0:T(128)}, u32[]{:S(2)}) copy-start(f32[2]{0:T(128)} %param.19) | copy-start | bytes 28
  54.4 51.3 %copy-start = (f32[256]{0:T(256)S(1)}, f32[256]{0:T(256)}, u32[]{:S(2)}) copy-start(f32[256]{0:T(256)} %param.21) | copy-start | bytes 3076
  65.6 9.7 %collective-permute-start = (f16[104,128]{1,0:T(8,128)(2,1)S(1)}, f16[104,128]{1,0:T(8,128)(2,1)S(1)}, u32[]{:S(2)}, u32[]{:S(2)}) collective-permute-start(f16[104,128]{1,0:T(8,128)(2,1)S(1)} %convert_element_type.31), channel_id=1, source_target_pairs={{256,384},{272,400},{288,416},{304,432},{320,448},{336,464},{352,4... | collective-permute-start | bytes 79880 | tf_op jit(solution)/shard_map/cond/branch_1_fun/ppermute | solution.py:477

commit v7 on v6

--- a/solution.py
+++ b/solution.py
@@ -106,21 +106,25 @@
         ref[(first + no) * rows : (first + no + 1) * rows, :] = matrix.astype(ref.dtype)
 
 
-def store_scaled(ref, matrices):
-    dim = matrices[0].shape[0]
+def store_scaled(ref, per_head):
+    heads, dim = len(per_head), per_head[0][0].shape[0]
     piece = ref.shape[1] - 8
     unit = math.gcd(piece, dim)
+    matrices = [matrix for group in per_head for matrix in group]
     peak = matrices[0]
     for matrix in matrices[1:]:
         peak = jnp.maximum(jnp.abs(peak), jnp.abs(matrix))
     peak = jnp.max(jnp.max(jnp.abs(peak), axis=1, keepdims=True), axis=0, keepdims=True)
     exponent = jnp.floor(jnp.log2(jnp.maximum(peak, 1e-30)))
     factor = jnp.exp2(TOP - exponent)
-    for no, matrix in enumerate(matrices):
-        for step in range(dim // unit):
-            row = no * dim + step * unit
-            place = slice(row % piece, row % piece + unit)
-            ref[row // piece, place, :] = matrix[step * unit : (step + 1) * unit, :] * factor
+    for head_no, group in enumerate(per_head):
+        for no, matrix in enumerate(group):
+            for step in range(dim // unit):
+                row = no * dim + step * unit
+                place = slice(row % piece, row % piece + unit)
+                ref[row // piece * heads + head_no, place, :] = (
+                    matrix[step * unit : (step + 1) * unit, :] * factor
+                )
     for no in range(ref.shape[0]):
         ref[no, piece:, :] = jnp.broadcast_to(exponent, (8, dim))
 
@@ -148,17 +152,18 @@
     out_ref[piece:, :] = jnp.broadcast_to(exponent, (8, total.shape[1]))
 
 
-def load_scaled(ref):
+def load_scaled(ref, heads):
     piece, dim = ref.shape[1] - 8, ref.shape[2]
     unit = math.gcd(piece, dim)
     factors = [jnp.exp2(ref[no, piece : piece + 1, :] - TOP) for no in range(ref.shape[0])]
     matrices = []
-    for first in range(0, ref.shape[0] * piece, dim):
-        chunks = []
-        for row in range(first, first + dim, unit):
-            place = slice(row % piece, row % piece + unit)
-            chunks.append(ref[row // piece, place, :] * factors[row // piece])
-        matrices.append(jnp.concatenate(chunks, axis=0))
+    for head_no in range(heads):
+        for first in range(0, ref.shape[0] // heads * piece, dim):
+            chunks = []
+            for row in range(first, first + dim, unit):
+                no = row // piece * heads + head_no
+                chunks.append(ref[no, row % piece : row % piece + unit, :] * factors[no])
+            matrices.append(jnp.concatenate(chunks, axis=0))
     return matrices
 
 
@@ -251,10 +256,20 @@
         att = att_t.T
         att_t_ref[head_no] = att_t
         att_ref[:, cols] = att
-        grads += fast_grads(
-            weights[3 * head_no : 3 * head_no + 3], att, v_ref[:, cols], att_t, turned_ref[head_no]
+        grads.append(
+            fast_grads(
+                weights[3 * head_no : 3 * head_no + 3],
+                att,
+                v_ref[:, cols],
+                att_t,
+                turned_ref[head_no],
+            )
         )
     store_scaled(grad_ref, grads)
+
+
+def unused_kernel(out_ref):
+    out_ref[:, 0:16, :] = jnp.zeros((out_ref.shape[0], 16, out_ref.shape[2]), out_ref.dtype)
 
 
 def second_kernel(
@@ -264,6 +279,7 @@
     att_t_ref,
     v_ref,
     turned_ref,
+    other_ref,
     weights_ref,
     weight_ref,
     grad_ref,
@@ -271,19 +287,29 @@
     heads, dim, frame_len = turned_ref.shape
     initial = initial_of(weights_ref)
     steps = [scalars[2 + head_no] for head_no in range(heads)]
-    weights = renewed(initial, load_scaled(total_ref), initial, steps)
+    weights = renewed(initial, load_scaled(total_ref, heads), initial, steps)
     store_matrices(weight_ref, 0, weights)
-    grads = []
-    for head_no in range(heads):
-        cols = slice(head_no * dim, (head_no + 1) * dim)
-        grads += fast_grads(
-            weights[3 * head_no : 3 * head_no + 3],
-            att_ref[:, cols],
-            v_ref[:, cols],
-            att_t_ref[head_no],
-            turned_ref[head_no],
-        )
-    store_scaled(grad_ref, grads)
+    first = scalars[1] == 0
+
+    def mine(zero, one):
+        return jnp.where(first, zero, one)
+
+    def rows_of(ref, received):
+        own = mine(ref[:, :dim].astype(f32), ref[:, dim:].astype(f32)).astype(bf16)
+        return jnp.concatenate([own, received], axis=0)
+
+    def columns_of(ref, received):
+        own = mine(ref[0].astype(f32), ref[1].astype(f32)).astype(bf16)
+        return jnp.concatenate([own, received.T], axis=1)
+
+    grads = fast_grads(
+        [mine(weights[no], weights[3 + no]) for no in range(3)],
+        rows_of(att_ref, other_ref[0]),
+        rows_of(v_ref, other_ref[1]),
+        columns_of(att_t_ref, other_ref[0]),
+        columns_of(turned_ref, other_ref[1]),
+    )
+    store_scaled(grad_ref, [grads])
 
 
 def late_kernel(
@@ -293,12 +319,7 @@
     heads = weights_ref.shape[0] // 3
     initial = initial_of(weights_ref)
     steps = [scalars[2 + head_no] for head_no in range(heads)]
-    weights = renewed(load_matrices(weight_ref, dim), load_scaled(total_ref), initial, steps)
-    apply_weights(weights, scalars, att_ref, norm_ref, comb_ref, square_ref)
-
-
-def early_kernel(scalars, weight_ref, att_ref, norm_ref, comb_ref, square_ref):
-    weights = load_matrices(weight_ref, weight_ref.shape[1])
+    weights = renewed(load_matrices(weight_ref, dim), load_scaled(total_ref, heads), initial, steps)
     apply_weights(weights, scalars, att_ref, norm_ref, comb_ref, square_ref)
 
 
@@ -382,7 +403,8 @@
     plain_groups = [list(range(near * i, near * i + near)) for i in range(4)]
     rows = 3 * heads * dim
     piece = rows // near
-    flags = jnp.stack([position, position]).astype(f32)
+    core = position % heads
+    flags = jnp.stack([position, core]).astype(f32)
     scalars = jnp.concatenate([flags, step_size, head_scale])
 
     route = [(i, i + 1) for i in range(frames - 1)]
@@ -448,35 +470,24 @@
         return exchange(part, groups).astype(f32)
 
     late = position >= frames // 2
-    part = lax.cond(
-        late,
-        lambda grads: jnp.zeros((piece + 8, dim), f32),
-        lambda grads: combined_of(wired(grads, 0, near_groups)),
-        grads,
-    )
+    cores = [(i, i ^ 1) for i in range(frames // 2, frames)]
+    same_core = [group[core_no::heads] for group in plain_groups for core_no in range(heads)]
+
+    def swapped(grads, attended, values):
+        both = jnp.stack([attended, values])
+        leaving = jnp.where(core == 0, both[:, :, dim:], both[:, :, :dim])
+        return jnp.zeros((piece + 8, dim), f32), lax.ppermute(leaving, "frame", cores)
+
+    def summed(grads, attended, values):
+        part = combined_of(wired(grads, 0, near_groups))
+        return part, call(unused_kernel, [((2, frame_len, dim), bf16)])[0]
+
+    part, other_frame = lax.cond(late, swapped, summed, grads, attended, values_v)
     part = combined_of(wired(part, 4, far_groups)[:2])
     total = wired(part, near, near_groups)
-    weights, grads = call(
-        second_kernel,
-        [((rows, dim), f32), ((near, piece + 8, dim), f32)],
-        scalars,
-        total,
-        attended,
-        attended_t,
-        values_v,
-        values_t,
-        weights_v,
-        scalars=1,
-        flops=4 * 10**9,
-    )
     results = [((frame_len, width), f32), ((8, frame_len), f32)]
 
-    def with_second_sum(scalars, weights, attended, norms, grads, weights_v):
-        part = combined_of(wired(grads, 0, plain_groups))
-        pairs = [(i, i ^ near) for i in range(frames // 2, frames)]
-        other = lax.ppermute(part.astype(f16), "frame", pairs).astype(f32)
-        part = combined_of(part[None], other[None])
-        total = wired(part, near, plain_groups)
+    def applied(weights, total, scalars, attended, norms, weights_v):
         return call(
             late_kernel,
             results,
@@ -490,16 +501,35 @@
             flops=4 * 10**9,
         )
 
-    def with_first_sum(scalars, weights, attended, norms, grads, weights_v):
-        return call(
-            early_kernel,
-            results,
+    def with_second_sum(
+        scalars, total, attended, attended_t, norms, values_v, values_t, other_frame, weights_v
+    ):
+        weights, grads = call(
+            second_kernel,
+            [((rows, dim), f32), ((near // heads, piece + 8, dim), f32)],
             scalars,
-            weights,
+            total,
             attended,
-            norms,
+            attended_t,
+            values_v,
+            values_t,
+            other_frame,
+            weights_v,
             scalars=1,
-            flops=10**9,
+            flops=4 * 10**9,
+        )
+        part = combined_of(wired(grads, 0, same_core))
+        pairs = [(i, i ^ near) for i in range(frames // 2, frames)]
+        other = lax.ppermute(part.astype(f16), "frame", pairs).astype(f32)
+        part = combined_of(part[None], other[None])
+        total = wired(part, near, plain_groups)
+        return applied(weights, total, scalars, attended, norms, weights_v)
+
+    def with_first_sum(
+        scalars, total, attended, attended_t, norms, values_v, values_t, other_frame, weights_v
+    ):
+        return applied(
+            weights_v.reshape(rows, dim), total, scalars, attended, norms, weights_v
         )
 
     combined, square = lax.cond(
@@ -507,10 +537,13 @@
         with_second_sum,
         with_first_sum,
         scalars,
-        weights,
+        total,
         attended,
+        attended_t,
         norms,
-        grads,
+        values_v,
+        values_t,
+        other_frame,
         weights_v,
     )
     columns = lax.axis_size("head")

time: 107 us -> 105 us (0.981)
  blocking collectives: 72.6 us -> 66.9 us
  starting transfers between devices: 8.16 us -> 10.1 us
  waiting for transfers between devices: 8.93 us -> 10.5 us
    all_to_all x4, blocking collectives: 58.2 us -> 52.4 us  [exchange(): lax.all_to_all(array, 'frame', split_axis=0, concat_axis=0, tiled=True, a...]
    ppermute x0 -> x1, starting transfers between devices: none -> 1.92 us  [swapped(): lax.ppermute(leaving, 'frame', cores)]
    ppermute x0 -> x1, waiting for transfers between devices: none -> 1.63 us  [swapped(): lax.ppermute(leaving, 'frame', cores)]
  transfers between devices with their start and end apart: 3 -> 4, of which waited for: 3 -> 4; matrix products, arithmetic and copies ran while one was open for 0% -> 0% of each run, Pallas kernels for 4% -> 4%
where the time goes in v7:
time: 105 us
  blocking collectives  66.9 us (64%)
  Pallas kernels  16.5 us (16%)
  waiting for transfers between devices  10.5 us (10%)
  starting transfers between devices  10.1 us (10%)
    all_to_all x4, blocking collectives, exchange(): lax.all_to_all(array, 'frame', split_axis=0, concat_axis=0, tiled=True, a...  52.4 us
    pallas_call x9, Pallas kernels, call(): pl.pallas_call(kernel, out_shape=shapes, in_specs=first + [spec] * (len(a...  16.5 us
    all_to_all x1, blocking collectives, shards(): lax.all_to_all(jnp.broadcast_to(square[:1], (columns, frame_len)), 'head'...  14.5 us
    ppermute x1, waiting for transfers between devices, with_second_sum(): other = lax.ppermute(part.astype(f16), 'frame', pairs).astype(f32)  6.41 us
    ppermute x1, starting transfers between devices, with_second_sum(): other = lax.ppermute(part.astype(f16), 'frame', pairs).astype(f32)  3.23 us
    ppermute x1, starting transfers between devices, shards(): values_prev = lax.ppermute(values, 'frame', route)  3.03 us
  transfers between devices with their start and end apart: 4, of which 4 were waited for; matrix products, arithmetic and copies ran while one was open for 0% of the time, Pallas kernels for 4%

profile of v7, /device:TPU:384, one launch (start us, length us, event | category | flops | bytes accessed | tf_op | source)
XLA Modules:
  0.0 105.1 jit_solution(11318753332330384004)
XLA Ops:
  0.0 1.9 %collective-permute-start.2 = (bf16[512,256]{1,0:T(8,128)(2,1)}, bf16[512,256]{1,0:T(8,128)(2,1)S(1)}, u32[]{:S(2)}, u32[]{:S(2)}) collective-permute-start(bf16[512,256]{1,0:T(8,128)(2,1)} %k_hbm.1), channel_id=1, source_target_pairs={{0,16},{16,32},{32,48},{48,64},{64,80},{80,96},{96,112},{112,128},... | collective-permute-start | bytes 786440 | tf_op jit(solution)/shard_map/ppermute | solution.py:411
  1.9 3.0 %collective-permute-start.3 = (bf16[512,256]{1,0:T(8,128)(2,1)}, bf16[512,256]{1,0:T(8,128)(2,1)S(1)}, u32[]{:S(2)}, u32[]{:S(2)}) collective-permute-start(bf16[512,256]{1,0:T(8,128)(2,1)} %v_hbm.1), channel_id=1, source_target_pairs={{0,16},{16,32},{32,48},{48,64},{64,80},{80,96},{96,112},{112,128},... | collective-permute-start | bytes 786440 | tf_op jit(solution)/shard_map/ppermute | solution.py:412
  5.0 0.1 add_convert_fusion
  5.0 0.0 copy-start.1
  5.1 0.0 copy-start.2
  5.1 2.2 %shard_map.91 = (bf16[512,256]{1,0:T(8,128)(2,1)S(1)}, bf16[512,256]{1,0:T(8,128)(2,1)S(1)}, bf16[512,256]{1,0:T(8,128)(2,1)S(1)}, bf16[2,128,512]{2,1,0:T(8,128...) custom-call(bf16[512,256]{1,0:T(8,128)(2,1)} %q_hbm.1, ...), custom_call_target="tpu_custom_call" | custom-call | flops 2000000000 | bytes 2097152 | tf_op jit(solution)/shard_map/pallas_call | solution.py:364
  7.3 0.0 copy-done.1
  7.3 0.0 copy-done.2
  7.3 0.1 pad_maximum_fusion.1.scalars
  7.4 1.7 %collective-permute-done.2.past_ref = bf16[512,256]{1,0:T(8,128)(2,1)S(1)} collective-permute-done((bf16[512,256]{1,0:T(8,128)(2,1)}, bf16[512,256]{1,0:T(8,128)(2,1)S(1)}, u32[]{:S(2)}, u32[]{:S(2)}) %collective-permute-start.2) | collective-permute-done | bytes 262176 | tf_op jit(solution)/shard_map/ppermute | solution.py:411
  9.1 2.0 %shard_map.92 = (bf16[2,512,512]{2,1,0:T(8,128)(2,1)S(1)}, f32[2,128,512]{2,1,0:T(8,128)S(1)}) custom-call(f32[6]{0:T(128)S(1)} %pad_maximum_fusion.1.scalars, bf16[512,256]{1,0:T(8,128)(2,1)S(1)} %get-tuple-element.76.q_ref, bf16[512,256]{1,0:T(8,128)(2,1)S(1)} %collective-permute-done.2.past_ref, f32[2,512,512]{2,1,0:T(8,128)S(1)} %get-tuple-element.77.prob_ref, ...), custom_call_target="tpu_custom_call" | custom-call | flops 2000000000 | bytes 2097152 | tf_op jit(solution)/shard_map/pallas_call | solution.py:364
  11.1 0.8 collective-permute-done.3.past_ref
  11.9 1.7 %shard_map.93 = (bf16[512,256]{1,0:T(8,128)(2,1)S(1)}, bf16[2,128,512]{2,1,0:T(8,128)(2,1)S(1)}, f32[8,104,128]{2,1,0:T(8,128)S(1)}) custom-call(bf16[2,512,512]{2,1,0:T(8,128)(2,1)S(1)} %get-tuple-element.80.share_ref, f32[2,128,512]{2,1,0:T(8,128)S(1)} %get-tuple-element.81.mixed_ref, bf16[512,256]{1,0:T(8,128)(2,1)S(1)} %collective-permute-done.3.past_ref, ...), custom_call_target="tpu_custom_call" | custom-call | flops 3000000000 | bytes 2097152 | tf_op jit(solution)/shard_map/pallas_call | solution.py:364
  13.6 3.7 %conditional.2 = (f32[104,128]{1,0:T(8,128)S(1)}, bf16[2,512,128]{2,1,0:T(8,128)(2,1)}) conditional(s32[]{:T(128)} %convert_element_type.39, f32[8,104,128]{2,1,0:T(8,128)S(1)} %get-tuple-element.85, (s32[]{:T(128)}, bf16[512,256]{1,0:T(8,128)(2,1)S(1)}, bf16[512,256]{1,0:T(8,128)(2,1)S(1)}) %tuple.19), branch_computations={%region_0.1_spmd, %region_1.2_spmd} | conditional | flops 1179649 | bytes 6111280 | solution.py:485
  13.6 0.1 fusion.1
  13.7 1.9 %collective-permute-start = (bf16[2,512,128]{2,1,0:T(8,128)(2,1)S(1)}, bf16[2,512,128]{2,1,0:T(8,128)(2,1)}, u32[]{:S(2)}, u32[]{:S(2)}) collective-permute-start(bf16[2,512,128]{2,1,0:T(8,128)(2,1)S(1)} %fusion.1), channel_id=1, source_target_pairs={{256,272},{272,256},{288,304},{304,288},{320,336},{336,320},{352,3... | collective-permute-start | bytes 786440 | tf_op jit(solution)/shard_map/cond/branch_1_fun/ppermute | solution.py:479
  15.7 1.6 %collective-permute-done = bf16[2,512,128]{2,1,0:T(8,128)(2,1)} collective-permute-done((bf16[2,512,128]{2,1,0:T(8,128)(2,1)S(1)}, bf16[2,512,128]{2,1,0:T(8,128)(2,1)}, u32[]{:S(2)}, u32[]{:S(2)}) %collective-permute-start) | collective-permute-done | bytes 262176 | tf_op jit(solution)/shard_map/cond/branch_1_fun/ppermute | solution.py:479
  17.3 21.4 %all_to_all.32 = f16[4,104,128]{2,1,0:T(8,128)(2,1)S(1)} all-to-all(f16[4,104,128]{2,1,0:T(8,128)(2,1)S(1)} %broadcast_in_dim.22), channel_id=1, replica_groups={{0,192,320,384},{16,208,336,400},{32,224,352,416},{48,240,368,432},{64,..., dimensions={0} | all-to-all | bytes 212992 | tf_op jit(solution)/shard_map/all_to_all | solution.py:376
  38.8 11.8 %all_to_all.33 = f16[8,104,128]{2,1,0:T(8,128)(2,1)S(1)} all-to-all(f16[8,104,128]{2,1,0:T(8,128)(2,1)S(1)} %broadcast_in_dim.23), channel_id=1, replica_groups={{0,16,32,48,64,80,96,112},{192,208,224,240,128,144,160,176},{320,336,35..., dimensions={0} | all-to-all | bytes 425984 | tf_op jit(solution)/shard_map/all_to_all | solution.py:376
  50.6 0.0 copy-start
  50.6 39.0 %conditional.3 = ((f32[512,256]{1,0:T(8,128)S(1)}, f32[8,512]{1,0:T(8,128)S(1)})) conditional(s32[]{:T(128)} %convert_element_type.39, (f32[6,128,128]{2,1,0:T(8,128)S(1)}, f32[6]{0:T(128)S(1)}, bf16[512,256]{1,0:T(8,128)(2,1)S(1)}, bf16[512,256]{1,0:T(8,128)(2,1)S(1)}, f32[8,104,128]{2,1,0:T(8,128)S(1)}) %tuple.20, (f32[6]{0:T(128)S(1)}, ...), branch_computations={%region_2.3_spmd, %region_3.4_spmd} | conditional | flops 8000252928 | bytes 10891312 | solution.py:535
  50.8 5.1 %branch_1_fun.4 = (f32[768,128]{1,0:T(8,128)S(1)}, f32[4,104,128]{2,1,0:T(8,128)S(1)}) custom-call(f32[6]{0:T(128)S(1)} %get-tuple-element.48.scalars, f32[8,104,128]{2,1,0:T(8,128)S(1)} %get-tuple-element.49.total_ref, bf16[512,256]{1,0:T(8,128)(2,1)S(1)} %get-tuple-element.50.att_ref, bf16[2,128,512]{2,1,0:T(8,128)(2,1)S(1)} %get-tuple-element.51.att_t_ref, ...), custom_call_target="tpu_custom_call" | custom-call | flops 4000000000 | bytes 2097152 | tf_op jit(solution)/shard_map/cond/branch_1_fun/pallas_call | solution.py:364
  55.9 8.2 %all_to_all.30 = f16[4,104,128]{2,1,0:T(8,128)(2,1)S(1)} all-to-all(f16[4,104,128]{2,1,0:T(8,128)(2,1)S(1)} %convert_element_type.13), channel_id=1, replica_groups={{0,32,64,96},{16,48,80,112},{128,160,192,224},{144,176,208,240},{256,28..., dimensions={0} | all-to-all | bytes 212992 | tf_op jit(solution)/shard_map/cond/branch_1_fun/all_to_all | solution.py:376
  64.2 3.2 %collective-permute-start.1 = (f16[104,128]{1,0:T(8,128)(2,1)S(1)}, f16[104,128]{1,0:T(8,128)(2,1)S(1)}, u32[]{:S(2)}, u32[]{:S(2)}) collective-permute-start(f16[104,128]{1,0:T(8,128)(2,1)S(1)} %convert_element_type.31), channel_id=1, source_target_pairs={{256,384},{272,400},{288,416},{304,432},{320,448},{336,464},{352,4... | collective-permute-start | bytes 79880 | tf_op jit(solution)/shard_map/cond/branch_1_fun/ppermute | solution.py:523
  67.5 6.4 %collective-permute-done.1 = f16[104,128]{1,0:T(8,128)(2,1)S(1)} collective-permute-done((f16[104,128]{1,0:T(8,128)(2,1)S(1)}, f16[104,128]{1,0:T(8,128)(2,1)S(1)}, u32[]{:S(2)}, u32[]{:S(2)}) %collective-permute-start.1) | collective-permute-done | bytes 26656 | tf_op jit(solution)/shard_map/cond/branch_1_fun/ppermute | solution.py:523
  74.0 11.1 %all_to_all.31 = f16[8,104,128]{2,1,0:T(8,128)(2,1)S(1)} all-to-all(f16[8,104,128]{2,1,0:T(8,128)(2,1)S(1)} %broadcast_in_dim.5), channel_id=1, replica_groups={{0,16,32,48,64,80,96,112},{128,144,160,176,192,208,224,240},{256,272,28..., dimensions={0} | all-to-all | bytes 425984 | tf_op jit(solution)/shard_map/cond/branch_1_fun/all_to_all | solution.py:376
  85.1 4.4 %branch_1_fun.7 = (f32[512,256]{1,0:T(8,128)S(1)}, f32[8,512]{1,0:T(8,128)S(1)}) custom-call(f32[6]{0:T(128)S(1)} %get-tuple-element.48.scalars, f32[768,128]{1,0:T(8,128)S(1)} %get-tuple-element.56.weight_ref, bf16[512,256]{1,0:T(8,128)(2,1)S(1)} %get-tuple-element.50.att_ref, bf16[512,256]{1,0:T(8,128)(2,1)S(1)} %get-tuple-element.57.norm_ref, ...), custom_call_target="tpu_custom_call" | custom-call | flops 4000000000 | bytes 2097152 | tf_op jit(solution)/shard_map/cond/branch_1_fun/pallas_call | solution.py:364
  89.6 14.5 %all_to_all.34 = f32[16,1,512]{2,1,0:T(1,128)S(1)} all-to-all(f32[16,1,512]{2,1,0:T(1,128)S(1)} %broadcast_in_dim.36), channel_id=1, replica_groups=mesh['frame'=32,'head'=16] {'head'}, dimensions={0} | all-to-all | bytes 65536 | tf_op jit(solution)/shard_map/all_to_all | solution.py:550
  104.1 0.0 copy-done
  104.1 1.0 shard_map.95
  (20 shorter events, 0.3 us)
Async XLA Ops:
  0.0 9.1 %collective-permute-start.2 = (bf16[512,256]{1,0:T(8,128)(2,1)}, bf16[512,256]{1,0:T(8,128)(2,1)S(1)}, u32[]{:S(2)}, u32[]{:S(2)}) collective-permute-start(bf16[512,256]{1,0:T(8,128)(2,1)} %k_hbm.1), channel_id=1, source_target_pairs={{0,16},{16,32},{32,48},{48,64},{64,80},{80,96},{96,112},{112,128},... | collective-permute-start | bytes 786440 | tf_op jit(solution)/shard_map/ppermute | solution.py:411
  1.9 10.0 %collective-permute-start.3 = (bf16[512,256]{1,0:T(8,128)(2,1)}, bf16[512,256]{1,0:T(8,128)(2,1)S(1)}, u32[]{:S(2)}, u32[]{:S(2)}) collective-permute-start(bf16[512,256]{1,0:T(8,128)(2,1)} %v_hbm.1), channel_id=1, source_target_pairs={{0,16},{16,32},{32,48},{48,64},{64,80},{80,96},{96,112},{112,128},... | collective-permute-start | bytes 786440 | tf_op jit(solution)/shard_map/ppermute | solution.py:412
  5.0 2.2 %copy-start.1 = (f32[2]{0:T(128)S(1)}, f32[2]{0:T(128)}, u32[]{:S(2)}) copy-start(f32[2]{0:T(128)} %param.20) | copy-start | bytes 28
  5.1 2.3 %copy-start.2 = (f32[2]{0:T(128)S(1)}, f32[2]{0:T(128)}, u32[]{:S(2)}) copy-start(f32[2]{0:T(128)} %param.19) | copy-start | bytes 28
  13.7 3.6 %collective-permute-start = (bf16[2,512,128]{2,1,0:T(8,128)(2,1)S(1)}, bf16[2,512,128]{2,1,0:T(8,128)(2,1)}, u32[]{:S(2)}, u32[]{:S(2)}) collective-permute-start(bf16[2,512,128]{2,1,0:T(8,128)(2,1)S(1)} %fusion.1), channel_id=1, source_target_pairs={{256,272},{272,256},{288,304},{304,288},{320,336},{336,320},{352,3... | collective-permute-start | bytes 786440 | tf_op jit(solution)/shard_map/cond/branch_1_fun/ppermute | solution.py:479
  50.6 53.5 %copy-start = (f32[256]{0:T(256)S(1)}, f32[256]{0:T(256)}, u32[]{:S(2)}) copy-start(f32[256]{0:T(256)} %param.21) | copy-start | bytes 3076
  64.2 9.7 %collective-permute-start.1 = (f16[104,128]{1,0:T(8,128)(2,1)S(1)}, f16[104,128]{1,0:T(8,128)(2,1)S(1)}, u32[]{:S(2)}, u32[]{:S(2)}) collective-permute-start(f16[104,128]{1,0:T(8,128)(2,1)S(1)} %convert_element_type.31), channel_id=1, source_target_pairs={{256,384},{272,400},{288,416},{304,432},{320,448},{336,464},{352,4... | collective-permute-start | bytes 79880 | tf_op jit(solution)/shard_map/cond/branch_1_fun/ppermute | solution.py:523

commit v8 on v7

--- a/solution.py
+++ b/solution.py
@@ -272,6 +272,12 @@
     out_ref[:, 0:16, :] = jnp.zeros((out_ref.shape[0], 16, out_ref.shape[2]), out_ref.dtype)
 
 
+def one_head(scalars, weights_ref, dim):
+    core = scalars[1].astype(jnp.int32)
+    cols = pl.ds(pl.multiple_of(core * dim, dim), dim)
+    return core, cols, [weights_ref[3 * core + no] for no in range(3)]
+
+
 def second_kernel(
     scalars,
     total_ref,
@@ -285,59 +291,72 @@
     grad_ref,
 ):
     heads, dim, frame_len = turned_ref.shape
-    initial = initial_of(weights_ref)
-    steps = [scalars[2 + head_no] for head_no in range(heads)]
-    weights = renewed(initial, load_scaled(total_ref, heads), initial, steps)
+    core, cols, initial = one_head(scalars, weights_ref, dim)
+    weights = renewed(initial, load_scaled(total_ref, 1), initial, [scalars[2 + core]])
     store_matrices(weight_ref, 0, weights)
+    grads = fast_grads(
+        weights,
+        jnp.concatenate([att_ref[:, cols], other_ref[0]], axis=0),
+        jnp.concatenate([v_ref[:, cols], other_ref[1]], axis=0),
+        jnp.concatenate([att_t_ref[core], other_ref[0].T], axis=1),
+        jnp.concatenate([turned_ref[core], other_ref[1].T], axis=1),
+    )
+    store_scaled(grad_ref, [grads])
+
+
+def fast_rows(weights, rows, scale):
+    gate_w, up_w, down_t = weights
+    gate, upward = gate_and_up(rows, gate_w, up_w)
+    hidden = gate / (1.0 + jnp.exp(-gate)) * upward
+    return (product(parts_of(hidden), parts_of(down_t), across) * scale).astype(bf16)
+
+
+def store_combined(att_ref, fast, comb_ref, square_ref):
+    combined = att_ref[...].astype(f32) + jnp.concatenate(fast, axis=1).astype(f32)
+    comb_ref[...] = combined
+    square = combined * combined
+    ones = jnp.ones((8, square.shape[1]), bf16)
+    high, low = parts_of(square)
+    square_ref[...] = dot(ones, high, across) + dot(ones, low, across)
+
+
+def late_kernel(
+    scalars, weight_ref, norm_ref, other_ref, total_ref, weights_ref, own_ref, away_ref
+):
+    frame_len, dim = own_ref.shape
+    heads = weights_ref.shape[0] // 3
+    core, cols, initial = one_head(scalars, weights_ref, dim)
+    weights = renewed(
+        load_matrices(weight_ref, dim), load_scaled(total_ref, 1), initial, [scalars[2 + core]]
+    )
+    rows = jnp.concatenate([norm_ref[:, cols], other_ref[2]], axis=0)
+    fast = fast_rows(weights, rows, scalars[2 + heads + core])
+    own_ref[...] = fast[:frame_len]
+    away_ref[...] = fast[frame_len:]
+
+
+def merge_kernel(scalars, att_ref, own_ref, back_ref, comb_ref, square_ref):
     first = scalars[1] == 0
-
-    def mine(zero, one):
-        return jnp.where(first, zero, one)
-
-    def rows_of(ref, received):
-        own = mine(ref[:, :dim].astype(f32), ref[:, dim:].astype(f32)).astype(bf16)
-        return jnp.concatenate([own, received], axis=0)
-
-    def columns_of(ref, received):
-        own = mine(ref[0].astype(f32), ref[1].astype(f32)).astype(bf16)
-        return jnp.concatenate([own, received.T], axis=1)
-
-    grads = fast_grads(
-        [mine(weights[no], weights[3 + no]) for no in range(3)],
-        rows_of(att_ref, other_ref[0]),
-        rows_of(v_ref, other_ref[1]),
-        columns_of(att_t_ref, other_ref[0]),
-        columns_of(turned_ref, other_ref[1]),
-    )
-    store_scaled(grad_ref, [grads])
-
-
-def late_kernel(
-    scalars, weight_ref, att_ref, norm_ref, total_ref, weights_ref, comb_ref, square_ref
-):
+    own, back = own_ref[...].astype(f32), back_ref[...].astype(f32)
+    fast = [jnp.where(first, own, back), jnp.where(first, back, own)]
+    store_combined(att_ref, fast, comb_ref, square_ref)
+
+
+def early_kernel(scalars, att_ref, norm_ref, total_ref, weights_ref, comb_ref, square_ref):
     dim = weights_ref.shape[1]
     heads = weights_ref.shape[0] // 3
     initial = initial_of(weights_ref)
     steps = [scalars[2 + head_no] for head_no in range(heads)]
-    weights = renewed(load_matrices(weight_ref, dim), load_scaled(total_ref, heads), initial, steps)
-    apply_weights(weights, scalars, att_ref, norm_ref, comb_ref, square_ref)
-
-
-def apply_weights(weights, scalars, att_ref, norm_ref, comb_ref, square_ref):
-    heads, dim = len(weights) // 3, weights[0].shape[0]
-    for head_no in range(heads):
-        cols = slice(head_no * dim, (head_no + 1) * dim)
-        gate_w, up_w, down_t = weights[3 * head_no : 3 * head_no + 3]
-        gate, upward = gate_and_up(norm_ref[:, cols], gate_w, up_w)
-        hidden = gate / (1.0 + jnp.exp(-gate)) * upward
-        output = product(parts_of(hidden), parts_of(down_t), across)
-        fast_out = (output * scalars[2 + heads + head_no]).astype(bf16)
-        comb_ref[:, cols] = att_ref[:, cols].astype(f32) + fast_out.astype(f32)
-    combined = comb_ref[...]
-    square = combined * combined
-    ones = jnp.ones((8, square.shape[1]), bf16)
-    high, low = parts_of(square)
-    square_ref[...] = dot(ones, high, across) + dot(ones, low, across)
+    weights = renewed(initial, load_scaled(total_ref, heads), initial, steps)
+    fast = [
+        fast_rows(
+            weights[3 * head_no : 3 * head_no + 3],
+            norm_ref[:, head_no * dim : (head_no + 1) * dim],
+            scalars[2 + heads + head_no],
+        )
+        for head_no in range(heads)
+    ]
+    store_combined(att_ref, fast, comb_ref, square_ref)
 
 
 def final_kernel(square_ref, comb_ref, gain_ref, out_ref, *, features):
@@ -471,44 +490,31 @@
 
     late = position >= frames // 2
     cores = [(i, i ^ 1) for i in range(frames // 2, frames)]
-    same_core = [group[core_no::heads] for group in plain_groups for core_no in range(heads)]
-
-    def swapped(grads, attended, values):
-        both = jnp.stack([attended, values])
-        leaving = jnp.where(core == 0, both[:, :, dim:], both[:, :, :dim])
+    def same_core(groups):
+        return [group[core_no::heads] for group in groups for core_no in range(heads)]
+
+    def swapped(grads, attended, values, norms):
+        each = jnp.stack([attended, values, norms])
+        leaving = jnp.where(core == 0, each[:, :, dim:], each[:, :, :dim])
         return jnp.zeros((piece + 8, dim), f32), lax.ppermute(leaving, "frame", cores)
 
-    def summed(grads, attended, values):
+    def summed(grads, attended, values, norms):
         part = combined_of(wired(grads, 0, near_groups))
-        return part, call(unused_kernel, [((2, frame_len, dim), bf16)])[0]
-
-    part, other_frame = lax.cond(late, swapped, summed, grads, attended, values_v)
+        return part, call(unused_kernel, [((3, frame_len, dim), bf16)])[0]
+
+    part, other_frame = lax.cond(late, swapped, summed, grads, attended, values_v, norms)
     part = combined_of(wired(part, 4, far_groups)[:2])
-    total = wired(part, near, near_groups)
     results = [((frame_len, width), f32), ((8, frame_len), f32)]
-
-    def applied(weights, total, scalars, attended, norms, weights_v):
-        return call(
-            late_kernel,
-            results,
-            scalars,
-            weights,
-            attended,
-            norms,
-            total,
-            weights_v,
-            scalars=1,
-            flops=4 * 10**9,
-        )
+    quarter = near // heads
 
     def with_second_sum(
-        scalars, total, attended, attended_t, norms, values_v, values_t, other_frame, weights_v
+        scalars, part, attended, attended_t, norms, values_v, values_t, other_frame, weights_v
     ):
         weights, grads = call(
             second_kernel,
-            [((rows, dim), f32), ((near // heads, piece + 8, dim), f32)],
+            [((3 * dim, dim), f32), ((quarter, piece + 8, dim), f32)],
             scalars,
-            total,
+            wired(part, quarter, same_core(near_groups)),
             attended,
             attended_t,
             values_v,
@@ -518,18 +524,38 @@
             scalars=1,
             flops=4 * 10**9,
         )
-        part = combined_of(wired(grads, 0, same_core))
+        part = combined_of(wired(grads, 0, same_core(plain_groups)))
         pairs = [(i, i ^ near) for i in range(frames // 2, frames)]
         other = lax.ppermute(part.astype(f16), "frame", pairs).astype(f32)
         part = combined_of(part[None], other[None])
-        total = wired(part, near, plain_groups)
-        return applied(weights, total, scalars, attended, norms, weights_v)
+        own, away = call(
+            late_kernel,
+            [((frame_len, dim), bf16)] * 2,
+            scalars,
+            weights,
+            norms,
+            other_frame,
+            wired(part, quarter, same_core(plain_groups)),
+            weights_v,
+            scalars=1,
+            flops=4 * 10**9,
+        )
+        back = lax.ppermute(away, "frame", cores)
+        return call(merge_kernel, results, scalars, attended, own, back, scalars=1, flops=10**8)
 
     def with_first_sum(
-        scalars, total, attended, attended_t, norms, values_v, values_t, other_frame, weights_v
+        scalars, part, attended, attended_t, norms, values_v, values_t, other_frame, weights_v
     ):
-        return applied(
-            weights_v.reshape(rows, dim), total, scalars, attended, norms, weights_v
+        return call(
+            early_kernel,
+            results,
+            scalars,
+            attended,
+            norms,
+            wired(part, near, near_groups),
+            weights_v,
+            scalars=1,
+            flops=4 * 10**9,
         )
 
     combined, square = lax.cond(
@@ -537,7 +563,7 @@
         with_second_sum,
         with_first_sum,
         scalars,
-        total,
+        part,
         attended,
         attended_t,
         norms,

time: 105 us -> 104 us (level)
  the two profiles are of different devices: /device:TPU:384 before, /device:TPU:416 now
where the time goes in v8:
time: 104 us
  blocking collectives  62.1 us (60%)
  Pallas kernels  16.5 us (16%)
  starting transfers between devices  12.2 us (12%)
  waiting for transfers between devices  11.7 us (11%)
    all_to_all x4, blocking collectives, exchange(): lax.all_to_all(array, 'frame', split_axis=0, concat_axis=0, tiled=True, a...  47.7 us
    pallas_call x10, Pallas kernels, call(): pl.pallas_call(kernel, out_shape=shapes, in_specs=first + [spec] * (len(a...  16.5 us
    all_to_all x1, blocking collectives, shards(): lax.all_to_all(jnp.broadcast_to(square[:1], (columns, frame_len)), 'head'...  14.4 us
    ppermute x1, waiting for transfers between devices, with_second_sum(): other = lax.ppermute(part.astype(f16), 'frame', pairs).astype(f32)  7.32 us
    ppermute x1, starting transfers between devices, with_second_sum(): other = lax.ppermute(part.astype(f16), 'frame', pairs).astype(f32)  3.46 us
    ppermute x1, starting transfers between devices, shards(): values_prev = lax.ppermute(values, 'frame', route)  3.03 us
  transfers between devices with their start and end apart: 5, of which 5 were waited for; matrix products, arithmetic and copies ran while one was open for 0% of the time, Pallas kernels for 4%

profile of v8, /device:TPU:416, one launch (start us, length us, event | category | flops | bytes accessed | tf_op | source)
XLA Modules:
  0.0 103.6 jit_solution(15198232560810808683)
XLA Ops:
  0.0 1.9 %collective-permute-start.3 = (bf16[512,256]{1,0:T(8,128)(2,1)}, bf16[512,256]{1,0:T(8,128)(2,1)S(1)}, u32[]{:S(2)}, u32[]{:S(2)}) collective-permute-start(bf16[512,256]{1,0:T(8,128)(2,1)} %k_hbm.1), channel_id=1, source_target_pairs={{0,16},{16,32},{32,48},{48,64},{64,80},{80,96},{96,112},{112,128},... | collective-permute-start | bytes 786440 | tf_op jit(solution)/shard_map/ppermute | solution.py:430
  1.9 3.0 %collective-permute-start.4 = (bf16[512,256]{1,0:T(8,128)(2,1)}, bf16[512,256]{1,0:T(8,128)(2,1)S(1)}, u32[]{:S(2)}, u32[]{:S(2)}) collective-permute-start(bf16[512,256]{1,0:T(8,128)(2,1)} %v_hbm.1), channel_id=1, source_target_pairs={{0,16},{16,32},{32,48},{48,64},{64,80},{80,96},{96,112},{112,128},... | collective-permute-start | bytes 786440 | tf_op jit(solution)/shard_map/ppermute | solution.py:431
  5.0 0.1 add_convert_fusion
  5.0 0.0 copy-start.1
  5.1 0.0 copy-start.2
  5.1 2.2 %shard_map.91 = (bf16[512,256]{1,0:T(8,128)(2,1)S(1)}, bf16[512,256]{1,0:T(8,128)(2,1)S(1)}, bf16[512,256]{1,0:T(8,128)(2,1)S(1)}, bf16[2,128,512]{2,1,0:T(8,128...) custom-call(bf16[512,256]{1,0:T(8,128)(2,1)} %q_hbm.1, ...), custom_call_target="tpu_custom_call" | custom-call | flops 2000000000 | bytes 2097152 | tf_op jit(solution)/shard_map/pallas_call | solution.py:383
  7.3 0.0 copy-done.1
  7.3 0.0 copy-done.2
  7.3 0.1 pad_maximum_fusion.1.scalars
  7.4 0.5 collective-permute-done.3.past_ref
  7.9 2.0 %shard_map.92 = (bf16[2,512,512]{2,1,0:T(8,128)(2,1)S(1)}, f32[2,128,512]{2,1,0:T(8,128)S(1)}) custom-call(f32[6]{0:T(128)S(1)} %pad_maximum_fusion.1.scalars, bf16[512,256]{1,0:T(8,128)(2,1)S(1)} %get-tuple-element.80.q_ref, bf16[512,256]{1,0:T(8,128)(2,1)S(1)} %collective-permute-done.3.past_ref, f32[2,512,512]{2,1,0:T(8,128)S(1)} %get-tuple-element.81.prob_ref, ...), custom_call_target="tpu_custom_call" | custom-call | flops 2000000000 | bytes 2097152 | tf_op jit(solution)/shard_map/pallas_call | solution.py:383
  9.9 0.8 collective-permute-done.4.past_ref
  10.7 1.7 %shard_map.93 = (bf16[512,256]{1,0:T(8,128)(2,1)S(1)}, bf16[2,128,512]{2,1,0:T(8,128)(2,1)S(1)}, f32[8,104,128]{2,1,0:T(8,128)S(1)}) custom-call(bf16[2,512,512]{2,1,0:T(8,128)(2,1)S(1)} %get-tuple-element.84.share_ref, f32[2,128,512]{2,1,0:T(8,128)S(1)} %get-tuple-element.85.mixed_ref, bf16[512,256]{1,0:T(8,128)(2,1)S(1)} %collective-permute-done.4.past_ref, ...), custom_call_target="tpu_custom_call" | custom-call | flops 3000000000 | bytes 2097152 | tf_op jit(solution)/shard_map/pallas_call | solution.py:383
  12.4 3.9 %conditional.2 = (f32[104,128]{1,0:T(8,128)S(1)}, bf16[3,512,128]{2,1,0:T(8,128)(2,1)}) conditional(s32[]{:T(128)} %convert_element_type.45, f32[8,104,128]{2,1,0:T(8,128)S(1)} %get-tuple-element.88, (s32[]{:T(128)}, bf16[512,256]{1,0:T(8,128)(2,1)S(1)}, bf16[512,256]{1,0:T(8,128)(2,1)S(1)}, bf16[512,256]{1,0:T(8,128)(2,1)S(1)}) %tuple.19), branch_computations={%region_0.1_spmd, %region_1.2_spmd} | conditional | flops 983041 | bytes 6111280 | solution.py:505
  12.4 0.1 pad_maximum_fusion
  12.5 0.1 slice_select_fusion
  12.6 1.9 %collective-permute-start = (bf16[3,512,128]{2,1,0:T(8,128)(2,1)S(1)}, bf16[3,512,128]{2,1,0:T(8,128)(2,1)}, u32[]{:S(2)}, u32[]{:S(2)}) collective-permute-start(bf16[3,512,128]{2,1,0:T(8,128)(2,1)S(1)} %slice_select_fusion), channel_id=1, source_target_pairs={{256,272},{272,256},{288,304},{304,288},{320,336},{336,320},{352,3... | collective-permute-start | bytes 1179656 | tf_op jit(solution)/shard_map/cond/branch_1_fun/ppermute | solution.py:499
  14.5 1.8 %collective-permute-done = bf16[3,512,128]{2,1,0:T(8,128)(2,1)} collective-permute-done((bf16[3,512,128]{2,1,0:T(8,128)(2,1)S(1)}, bf16[3,512,128]{2,1,0:T(8,128)(2,1)}, u32[]{:S(2)}, u32[]{:S(2)}) %collective-permute-start) | collective-permute-done | bytes 393248 | tf_op jit(solution)/shard_map/cond/branch_1_fun/ppermute | solution.py:499
  16.4 23.3 %all_to_all.37 = f16[4,104,128]{2,1,0:T(8,128)(2,1)S(1)} all-to-all(f16[4,104,128]{2,1,0:T(8,128)(2,1)S(1)} %broadcast_in_dim.32), channel_id=1, replica_groups={{0,192,320,384},{16,208,336,400},{32,224,352,416},{48,240,368,432},{64,..., dimensions={0} | all-to-all | bytes 212992 | tf_op jit(solution)/shard_map/all_to_all | solution.py:395
  39.7 0.0 copy-start
  39.7 48.4 %conditional.3 = ((f32[512,256]{1,0:T(8,128)S(1)}, f32[8,512]{1,0:T(8,128)S(1)})) conditional(s32[]{:T(128)} %convert_element_type.45, (f32[104,128]{1,0:T(8,128)S(1)}, f32[6]{0:T(128)S(1)}, bf16[512,256]{1,0:T(8,128)(2,1)S(1)}, bf16[512,256]{1,0:T(8,128)(2,1)S(1)}, f32[6,128,128]{2,1,0:T(8,128)S(1)}) %tuple.20, (f32[104,128]{1,0:T(8,128)S(1)}, ...), branch_computations={%region_2.3_spmd, %region_3.4_spmd} | conditional | flops 8100265984 | bytes 13619288 | solution.py:561
  39.8 8.1 %all_to_all.34 = f16[4,104,128]{2,1,0:T(8,128)(2,1)S(1)} all-to-all(f16[4,104,128]{2,1,0:T(8,128)(2,1)S(1)} %broadcast_in_dim.6), channel_id=1, replica_groups={{0,32,64,96},{16,48,80,112},{192,224,128,160},{208,240,144,176},{320,35..., dimensions={0} | all-to-all | bytes 212992 | tf_op jit(solution)/shard_map/cond/branch_1_fun/all_to_all | solution.py:395
  47.9 4.5 %branch_1_fun.5 = (f32[384,128]{1,0:T(8,128)S(1)}, f32[4,104,128]{2,1,0:T(8,128)S(1)}) custom-call(f32[6]{0:T(128)S(1)} %get-tuple-element.51.scalars, f32[4,104,128]{2,1,0:T(8,128)S(1)} %convert_element_type.36.total_ref, bf16[512,256]{1,0:T(8,128)(2,1)S(1)} %get-tuple-element.52.att_ref, bf16[2,128,512]{2,1,0:T(8,128)(2,1)S(1)} %get-tuple-element.54.att_t_ref, ...), custom_call_target="tpu_custom_call" | custom-call | flops 4000000000 | bytes 2097152 | tf_op jit(solution)/shard_map/cond/branch_1_fun/pallas_call | solution.py:383
  52.4 8.3 %all_to_all.35 = f16[4,104,128]{2,1,0:T(8,128)(2,1)S(1)} all-to-all(f16[4,104,128]{2,1,0:T(8,128)(2,1)S(1)} %convert_element_type.37), channel_id=1, replica_groups={{0,32,64,96},{16,48,80,112},{128,160,192,224},{144,176,208,240},{256,28..., dimensions={0} | all-to-all | bytes 212992 | tf_op jit(solution)/shard_map/cond/branch_1_fun/all_to_all | solution.py:395
  60.8 3.5 %collective-permute-start.1 = (f16[104,128]{1,0:T(8,128)(2,1)S(1)}, f16[104,128]{1,0:T(8,128)(2,1)S(1)}, u32[]{:S(2)}, u32[]{:S(2)}) collective-permute-start(f16[104,128]{1,0:T(8,128)(2,1)S(1)} %convert_element_type.39), channel_id=1, source_target_pairs={{256,384},{272,400},{288,416},{304,432},{320,448},{336,464},{352,4... | collective-permute-start | bytes 79880 | tf_op jit(solution)/shard_map/cond/branch_1_fun/ppermute | solution.py:529
  64.3 7.3 %collective-permute-done.1 = f16[104,128]{1,0:T(8,128)(2,1)S(1)} collective-permute-done((f16[104,128]{1,0:T(8,128)(2,1)S(1)}, f16[104,128]{1,0:T(8,128)(2,1)S(1)}, u32[]{:S(2)}, u32[]{:S(2)}) %collective-permute-start.1) | collective-permute-done | bytes 26656 | tf_op jit(solution)/shard_map/cond/branch_1_fun/ppermute | solution.py:529
  71.7 8.1 %all_to_all.36 = f16[4,104,128]{2,1,0:T(8,128)(2,1)S(1)} all-to-all(f16[4,104,128]{2,1,0:T(8,128)(2,1)S(1)} %broadcast_in_dim.18), channel_id=1, replica_groups={{0,32,64,96},{16,48,80,112},{128,160,192,224},{144,176,208,240},{256,28..., dimensions={0} | all-to-all | bytes 212992 | tf_op jit(solution)/shard_map/cond/branch_1_fun/all_to_all | solution.py:395
  79.7 4.1 %branch_1_fun.8 = (bf16[512,128]{1,0:T(8,128)(2,1)S(1)}, bf16[512,128]{1,0:T(8,128)(2,1)S(1)}) custom-call(f32[6]{0:T(128)S(1)} %get-tuple-element.51.scalars, f32[384,128]{1,0:T(8,128)S(1)} %get-tuple-element.59.weight_ref, bf16[512,256]{1,0:T(8,128)(2,1)S(1)} %get-tuple-element.60.norm_ref, bf16[3,512,128]{2,1,0:T(8,128)(2,1)} %get-tuple-element.57.other_ref, ...), custom_call_target="tpu_custom_call" | custom-call | flops 4000000000 | bytes 2097152 | tf_op jit(solution)/shard_map/cond/branch_1_fun/pallas_call | solution.py:383
  83.9 1.9 %collective-permute-start.2 = (bf16[512,128]{1,0:T(8,128)(2,1)S(1)}, bf16[512,128]{1,0:T(8,128)(2,1)S(1)}, u32[]{:S(2)}, u32[]{:S(2)}) collective-permute-start(bf16[512,128]{1,0:T(8,128)(2,1)S(1)} %get-tuple-element.63), channel_id=1, source_target_pairs={{256,272},{272,256},{288,304},{304,288},{320,336},{336,320},{352,3... | collective-permute-start | bytes 393224 | tf_op jit(solution)/shard_map/cond/branch_1_fun/ppermute | solution.py:543
  85.8 1.3 %collective-permute-done.2.back_ref = bf16[512,128]{1,0:T(8,128)(2,1)S(1)} collective-permute-done((bf16[512,128]{1,0:T(8,128)(2,1)S(1)}, bf16[512,128]{1,0:T(8,128)(2,1)S(1)}, u32[]{:S(2)}, u32[]{:S(2)}) %collective-permute-start.2) | collective-permute-done | bytes 131104 | tf_op jit(solution)/shard_map/cond/branch_1_fun/ppermute | solution.py:543
  87.1 0.9 branch_1_fun.9
  88.1 14.4 %all_to_all.38 = f32[16,1,512]{2,1,0:T(1,128)S(1)} all-to-all(f32[16,1,512]{2,1,0:T(1,128)S(1)} %broadcast_in_dim.33), channel_id=1, replica_groups=mesh['frame'=32,'head'=16] {'head'}, dimensions={0} | all-to-all | bytes 65536 | tf_op jit(solution)/shard_map/all_to_all | solution.py:576
  102.6 0.0 copy-done
  102.6 1.0 shard_map.95
  (20 shorter events, 0.3 us)
Async XLA Ops:
  0.0 7.9 %collective-permute-start.3 = (bf16[512,256]{1,0:T(8,128)(2,1)}, bf16[512,256]{1,0:T(8,128)(2,1)S(1)}, u32[]{:S(2)}, u32[]{:S(2)}) collective-permute-start(bf16[512,256]{1,0:T(8,128)(2,1)} %k_hbm.1), channel_id=1, source_target_pairs={{0,16},{16,32},{32,48},{48,64},{64,80},{80,96},{96,112},{112,128},... | collective-permute-start | bytes 786440 | tf_op jit(solution)/shard_map/ppermute | solution.py:430
  1.9 8.8 %collective-permute-start.4 = (bf16[512,256]{1,0:T(8,128)(2,1)}, bf16[512,256]{1,0:T(8,128)(2,1)S(1)}, u32[]{:S(2)}, u32[]{:S(2)}) collective-permute-start(bf16[512,256]{1,0:T(8,128)(2,1)} %v_hbm.1), channel_id=1, source_target_pairs={{0,16},{16,32},{32,48},{48,64},{64,80},{80,96},{96,112},{112,128},... | collective-permute-start | bytes 786440 | tf_op jit(solution)/shard_map/ppermute | solution.py:431
  5.0 2.2 %copy-start.1 = (f32[2]{0:T(128)S(1)}, f32[2]{0:T(128)}, u32[]{:S(2)}) copy-start(f32[2]{0:T(128)} %param.20) | copy-start | bytes 28
  5.1 2.3 %copy-start.2 = (f32[2]{0:T(128)S(1)}, f32[2]{0:T(128)}, u32[]{:S(2)}) copy-start(f32[2]{0:T(128)} %param.19) | copy-start | bytes 28
  12.6 3.7 %collective-permute-start = (bf16[3,512,128]{2,1,0:T(8,128)(2,1)S(1)}, bf16[3,512,128]{2,1,0:T(8,128)(2,1)}, u32[]{:S(2)}, u32[]{:S(2)}) collective-permute-start(bf16[3,512,128]{2,1,0:T(8,128)(2,1)S(1)} %slice_select_fusion), channel_id=1, source_target_pairs={{256,272},{272,256},{288,304},{304,288},{320,336},{336,320},{352,3... | collective-permute-start | bytes 1179656 | tf_op jit(solution)/shard_map/cond/branch_1_fun/ppermute | solution.py:499
  39.7 62.9 %copy-start = (f32[256]{0:T(256)S(1)}, f32[256]{0:T(256)}, u32[]{:S(2)}) copy-start(f32[256]{0:T(256)} %param.21) | copy-start | bytes 3076
  60.8 10.8 %collective-permute-start.1 = (f16[104,128]{1,0:T(8,128)(2,1)S(1)}, f16[104,128]{1,0:T(8,128)(2,1)S(1)}, u32[]{:S(2)}, u32[]{:S(2)}) collective-permute-start(f16[104,128]{1,0:T(8,128)(2,1)S(1)} %convert_element_type.39), channel_id=1, source_target_pairs={{256,384},{272,400},{288,416},{304,432},{320,448},{336,464},{352,4... | collective-permute-start | bytes 79880 | tf_op jit(solution)/shard_map/cond/branch_1_fun/ppermute | solution.py:529
  83.9 3.2 %collective-permute-start.2 = (bf16[512,128]{1,0:T(8,128)(2,1)S(1)}, bf16[512,128]{1,0:T(8,128)(2,1)S(1)}, u32[]{:S(2)}, u32[]{:S(2)}) collective-permute-start(bf16[512,128]{1,0:T(8,128)(2,1)S(1)} %get-tuple-element.63), channel_id=1, source_target_pairs={{256,272},{272,256},{288,304},{304,288},{320,336},{336,320},{352,3... | collective-permute-start | bytes 393224 | tf_op jit(solution)/shard_map/cond/branch_1_fun/ppermute | solution.py:543

commit v9 on v8

--- a/solution.py
+++ b/solution.py
@@ -503,13 +503,27 @@
         return part, call(unused_kernel, [((3, frame_len, dim), bf16)])[0]
 
     part, other_frame = lax.cond(late, swapped, summed, grads, attended, values_v, norms)
-    part = combined_of(wired(part, 4, far_groups)[:2])
+    longer = [pair for a, b, c, d in far_groups for pair in ((b, d), (a, c))]
+    shorter = [pair for a, b, c, d in far_groups for pair in ((b, c), (a, d))]
+    halves = [pair for a, b, _, _ in far_groups for pair in ((a, b), (b, a))]
+    leaving = part.astype(f16)
+    far_parts = [lax.ppermute(leaving, "frame", route) for route in (longer, shorter)]
     results = [((frame_len, width), f32), ((8, frame_len), f32)]
     quarter = near // heads
 
     def with_second_sum(
-        scalars, part, attended, attended_t, norms, values_v, values_t, other_frame, weights_v
+        scalars,
+        part,
+        far_parts,
+        attended,
+        attended_t,
+        norms,
+        values_v,
+        values_t,
+        other_frame,
+        weights_v,
     ):
+        part = combined_of(*[far_part.astype(f32)[None] for far_part in far_parts])
         weights, grads = call(
             second_kernel,
             [((3 * dim, dim), f32), ((quarter, piece + 8, dim), f32)],
@@ -544,8 +558,19 @@
         return call(merge_kernel, results, scalars, attended, own, back, scalars=1, flops=10**8)
 
     def with_first_sum(
-        scalars, part, attended, attended_t, norms, values_v, values_t, other_frame, weights_v
+        scalars,
+        part,
+        far_parts,
+        attended,
+        attended_t,
+        norms,
+        values_v,
+        values_t,
+        other_frame,
+        weights_v,
     ):
+        other = lax.ppermute(part.astype(f16), "frame", halves).astype(f32)
+        part = combined_of(part[None], other[None])
         return call(
             early_kernel,
             results,
@@ -564,6 +589,7 @@
         with_first_sum,
         scalars,
         part,
+        far_parts,
         attended,
         attended_t,
         norms,

time: 104 us -> 97.6 us (0.938)
  blocking collectives: 62.1 us -> 39 us
  waiting for transfers between devices: 11.7 us -> 25.2 us
  starting transfers between devices: 12.2 us -> 15.5 us
    all_to_all x4 -> x3, blocking collectives: 47.7 us -> 24.6 us  [exchange(): lax.all_to_all(array, 'frame', split_axis=0, concat_axis=0, tiled=True, a...]
    ppermute x0 -> x2, waiting for transfers between devices: none -> 15.2 us  [shards(): lax.ppermute(leaving, 'frame', route)]
    ppermute x0 -> x2, starting transfers between devices: none -> 2.58 us  [shards(): lax.ppermute(leaving, 'frame', route)]
    ppermute x1, waiting for transfers between devices: 7.32 us -> 5.55 us  [with_second_sum(): other = lax.ppermute(part.astype(f16), 'frame', pairs).astype(f32)]
  transfers between devices with their start and end apart: 5 -> 7, of which waited for: 5 -> 6; matrix products, arithmetic and copies ran while one was open for 0% -> 0% of each run, Pallas kernels for 4% -> 4%
where the time goes in v9:
time: 97.6 us; the launch traced here: 97.1 us
  blocking collectives  39 us (40%)
  waiting for transfers between devices  25.2 us (26%)
  Pallas kernels  16.6 us (17%)
  starting transfers between devices  15.5 us (16%)
    all_to_all x3, blocking collectives, exchange(): lax.all_to_all(array, 'frame', split_axis=0, concat_axis=0, tiled=True, a...  24.6 us
    pallas_call x10, Pallas kernels, call(): pl.pallas_call(kernel, out_shape=shapes, in_specs=first + [spec] * (len(a...  16.6 us
    ppermute x2, waiting for transfers between devices, shards(): lax.ppermute(leaving, 'frame', route)  15.2 us
    all_to_all x1, blocking collectives, shards(): lax.all_to_all(jnp.broadcast_to(square[:1], (columns, frame_len)), 'head'...  14.5 us
    ppermute x1, waiting for transfers between devices, with_second_sum(): other = lax.ppermute(part.astype(f16), 'frame', pairs).astype(f32)  5.55 us
    ppermute x1, starting transfers between devices, with_second_sum(): other = lax.ppermute(part.astype(f16), 'frame', pairs).astype(f32)  4.09 us
    ppermute x1, starting transfers between devices, shards(): values_prev = lax.ppermute(values, 'frame', route)  3.03 us
    ppermute x2, starting transfers between devices, shards(): lax.ppermute(leaving, 'frame', route)  2.58 us
  transfers between devices with their start and end apart: 7, of which 6 were waited for; matrix products, arithmetic and copies ran while one was open for 0% of the time, Pallas kernels for 4%

profile of v9, /device:TPU:416, one launch (start us, length us, event | category | flops | bytes accessed | tf_op | source)
XLA Modules:
  0.0 97.1 jit_solution(11582976232144014402)
XLA Ops:
  0.0 1.9 %collective-permute-start.4 = (bf16[512,256]{1,0:T(8,128)(2,1)}, bf16[512,256]{1,0:T(8,128)(2,1)S(1)}, u32[]{:S(2)}, u32[]{:S(2)}) collective-permute-start(bf16[512,256]{1,0:T(8,128)(2,1)} %k_hbm.1), channel_id=1, source_target_pairs={{0,16},{16,32},{32,48},{48,64},{64,80},{80,96},{96,112},{112,128},... | collective-permute-start | bytes 786440 | tf_op jit(solution)/shard_map/ppermute | solution.py:430
  1.9 3.0 %collective-permute-start.5 = (bf16[512,256]{1,0:T(8,128)(2,1)}, bf16[512,256]{1,0:T(8,128)(2,1)S(1)}, u32[]{:S(2)}, u32[]{:S(2)}) collective-permute-start(bf16[512,256]{1,0:T(8,128)(2,1)} %v_hbm.1), channel_id=1, source_target_pairs={{0,16},{16,32},{32,48},{48,64},{64,80},{80,96},{96,112},{112,128},... | collective-permute-start | bytes 786440 | tf_op jit(solution)/shard_map/ppermute | solution.py:431
  5.0 0.1 add_convert_fusion
  5.0 0.0 copy-start.1
  5.1 0.0 copy-start.2
  5.1 2.2 %shard_map.91 = (bf16[512,256]{1,0:T(8,128)(2,1)S(1)}, bf16[512,256]{1,0:T(8,128)(2,1)S(1)}, bf16[512,256]{1,0:T(8,128)(2,1)S(1)}, bf16[2,128,512]{2,1,0:T(8,128...) custom-call(bf16[512,256]{1,0:T(8,128)(2,1)} %q_hbm.1, ...), custom_call_target="tpu_custom_call" | custom-call | flops 2000000000 | bytes 2097152 | tf_op jit(solution)/shard_map/pallas_call | solution.py:383
  7.3 0.0 copy-done.1
  7.3 0.0 copy-done.2
  7.3 0.1 pad_maximum_fusion.1.scalars
  7.4 0.5 collective-permute-done.4.past_ref
  7.9 2.0 %shard_map.92 = (bf16[2,512,512]{2,1,0:T(8,128)(2,1)S(1)}, f32[2,128,512]{2,1,0:T(8,128)S(1)}) custom-call(f32[6]{0:T(128)S(1)} %pad_maximum_fusion.1.scalars, bf16[512,256]{1,0:T(8,128)(2,1)S(1)} %get-tuple-element.85.q_ref, bf16[512,256]{1,0:T(8,128)(2,1)S(1)} %collective-permute-done.4.past_ref, f32[2,512,512]{2,1,0:T(8,128)S(1)} %get-tuple-element.86.prob_ref, ...), custom_call_target="tpu_custom_call" | custom-call | flops 2000000000 | bytes 2097152 | tf_op jit(solution)/shard_map/pallas_call | solution.py:383
  9.9 0.8 collective-permute-done.5.past_ref
  10.7 1.7 %shard_map.93 = (bf16[512,256]{1,0:T(8,128)(2,1)S(1)}, bf16[2,128,512]{2,1,0:T(8,128)(2,1)S(1)}, f32[8,104,128]{2,1,0:T(8,128)S(1)}) custom-call(bf16[2,512,512]{2,1,0:T(8,128)(2,1)S(1)} %get-tuple-element.89.share_ref, f32[2,128,512]{2,1,0:T(8,128)S(1)} %get-tuple-element.90.mixed_ref, bf16[512,256]{1,0:T(8,128)(2,1)S(1)} %collective-permute-done.5.past_ref, ...), custom_call_target="tpu_custom_call" | custom-call | flops 3000000000 | bytes 2097152 | tf_op jit(solution)/shard_map/pallas_call | solution.py:383
  12.4 3.9 %conditional.2 = (f32[104,128]{1,0:T(8,128)S(1)}, bf16[3,512,128]{2,1,0:T(8,128)(2,1)}, f16[104,128]{1,0:T(8,128)(2,1)S(1)}) conditional(s32[]{:T(128)} %convert_element_type.53, f32[8,104,128]{2,1,0:T(8,128)S(1)} %get-tuple-element.93, (s32[]{:T(128)}, bf16[512,256]{1,0:T(8,128)(2,1)S(1)}, bf16[512,256]{1,0:T(8,128)(2,1)S(1)}, ...), branch_computations={%region_0.1_spmd, %region_1.2_spmd} | conditional | flops 983041 | bytes 6191160 | solution.py:505
  12.5 0.1 pad_maximum_fusion
  12.6 0.1 slice_select_fusion
  12.6 1.9 %collective-permute-start = (bf16[3,512,128]{2,1,0:T(8,128)(2,1)S(1)}, bf16[3,512,128]{2,1,0:T(8,128)(2,1)}, u32[]{:S(2)}, u32[]{:S(2)}) collective-permute-start(bf16[3,512,128]{2,1,0:T(8,128)(2,1)S(1)} %slice_select_fusion), channel_id=1, source_target_pairs={{256,272},{272,256},{288,304},{304,288},{320,336},{336,320},{352,3... | collective-permute-start | bytes 1179656 | tf_op jit(solution)/shard_map/cond/branch_1_fun/ppermute | solution.py:499
  14.5 1.8 %collective-permute-done = bf16[3,512,128]{2,1,0:T(8,128)(2,1)} collective-permute-done((bf16[3,512,128]{2,1,0:T(8,128)(2,1)S(1)}, bf16[3,512,128]{2,1,0:T(8,128)(2,1)}, u32[]{:S(2)}, u32[]{:S(2)}) %collective-permute-start) | collective-permute-done | bytes 393248 | tf_op jit(solution)/shard_map/cond/branch_1_fun/ppermute | solution.py:499
  16.4 1.3 %collective-permute-start.6 = (f16[104,128]{1,0:T(8,128)(2,1)S(1)}, f16[104,128]{1,0:T(8,128)(2,1)S(1)}, u32[]{:S(2)}, u32[]{:S(2)}) collective-permute-start(f16[104,128]{1,0:T(8,128)(2,1)S(1)} %get-tuple-element.97), channel_id=1, source_target_pairs={{192,384},{0,320},{208,400},{16,336},{224,416},{32,352},{240,432},... | collective-permute-start | bytes 79880 | tf_op jit(solution)/shard_map/ppermute | solution.py:510
  17.7 1.3 %collective-permute-start.7 = (f16[104,128]{1,0:T(8,128)(2,1)S(1)}, f16[104,128]{1,0:T(8,128)(2,1)S(1)}, u32[]{:S(2)}, u32[]{:S(2)}) collective-permute-start(f16[104,128]{1,0:T(8,128)(2,1)S(1)} %get-tuple-element.97), channel_id=1, source_target_pairs={{192,320},{0,384},{208,336},{16,400},{224,352},{32,416},{240,368},... | collective-permute-start | bytes 79880 | tf_op jit(solution)/shard_map/ppermute | solution.py:510
  19.0 15.2 %collective-permute-done.6 = f16[104,128]{1,0:T(8,128)(2,1)S(1)} collective-permute-done((f16[104,128]{1,0:T(8,128)(2,1)S(1)}, f16[104,128]{1,0:T(8,128)(2,1)S(1)}, u32[]{:S(2)}, u32[]{:S(2)}) %collective-permute-start.6) | collective-permute-done | bytes 26656 | tf_op jit(solution)/shard_map/ppermute | solution.py:510
  34.2 0.0 collective-permute-done.7
  34.2 0.0 copy-start
  34.2 47.4 %conditional.3 = ((f32[512,256]{1,0:T(8,128)S(1)}, f32[8,512]{1,0:T(8,128)S(1)})) conditional(s32[]{:T(128)} %convert_element_type.53, (f32[104,128]{1,0:T(8,128)S(1)}, f32[6]{0:T(128)S(1)}, bf16[512,256]{1,0:T(8,128)(2,1)S(1)}, bf16[512,256]{1,0:T(8,128)(2,1)S(1)}, f32[6,128,128]{2,1,0:T(8,128)S(1)}) %tuple.22, (f16[104,128]{1,0:T(8,128)(2,1)S(1)}, ...), branch_computations={%region_2.3_spmd, %region_3.4_spmd} | conditional | flops 8100292608 | bytes 15876184 | solution.py:586
  34.3 8.1 %all_to_all.29 = f16[4,104,128]{2,1,0:T(8,128)(2,1)S(1)} all-to-all(f16[4,104,128]{2,1,0:T(8,128)(2,1)S(1)} %broadcast_in_dim.45), channel_id=1, replica_groups={{0,32,64,96},{16,48,80,112},{192,224,128,160},{208,240,144,176},{320,35..., dimensions={0} | all-to-all | bytes 212992 | tf_op jit(solution)/shard_map/cond/branch_1_fun/all_to_all | solution.py:395
  42.4 4.6 %branch_1_fun.7 = (f32[384,128]{1,0:T(8,128)S(1)}, f32[4,104,128]{2,1,0:T(8,128)S(1)}) custom-call(f32[6]{0:T(128)S(1)} %get-tuple-element.54.scalars, f32[4,104,128]{2,1,0:T(8,128)S(1)} %convert_element_type.45.total_ref, bf16[512,256]{1,0:T(8,128)(2,1)S(1)} %get-tuple-element.55.att_ref, bf16[2,128,512]{2,1,0:T(8,128)(2,1)S(1)} %get-tuple-element.58.att_t_ref, ...), custom_call_target="tpu_custom_call" | custom-call | flops 4000000000 | bytes 2097152 | tf_op jit(solution)/shard_map/cond/branch_1_fun/pallas_call | solution.py:383
  46.9 8.2 %all_to_all.30 = f16[4,104,128]{2,1,0:T(8,128)(2,1)S(1)} all-to-all(f16[4,104,128]{2,1,0:T(8,128)(2,1)S(1)} %convert_element_type.46), channel_id=1, replica_groups={{0,32,64,96},{16,48,80,112},{128,160,192,224},{144,176,208,240},{256,28..., dimensions={0} | all-to-all | bytes 212992 | tf_op jit(solution)/shard_map/cond/branch_1_fun/all_to_all | solution.py:395
  55.2 4.1 %collective-permute-start.2 = (f16[104,128]{1,0:T(8,128)(2,1)S(1)}, f16[104,128]{1,0:T(8,128)(2,1)S(1)}, u32[]{:S(2)}, u32[]{:S(2)}) collective-permute-start(f16[104,128]{1,0:T(8,128)(2,1)S(1)} %convert_element_type.48), channel_id=1, source_target_pairs={{256,384},{272,400},{288,416},{304,432},{320,448},{336,464},{352,4... | collective-permute-start | bytes 79880 | tf_op jit(solution)/shard_map/cond/branch_1_fun/ppermute | solution.py:543
  59.3 5.5 %collective-permute-done.2 = f16[104,128]{1,0:T(8,128)(2,1)S(1)} collective-permute-done((f16[104,128]{1,0:T(8,128)(2,1)S(1)}, f16[104,128]{1,0:T(8,128)(2,1)S(1)}, u32[]{:S(2)}, u32[]{:S(2)}) %collective-permute-start.2) | collective-permute-done | bytes 26656 | tf_op jit(solution)/shard_map/cond/branch_1_fun/ppermute | solution.py:543
  65.0 8.3 %all_to_all.31 = f16[4,104,128]{2,1,0:T(8,128)(2,1)S(1)} all-to-all(f16[4,104,128]{2,1,0:T(8,128)(2,1)S(1)} %broadcast_in_dim.49), channel_id=1, replica_groups={{0,32,64,96},{16,48,80,112},{128,160,192,224},{144,176,208,240},{256,28..., dimensions={0} | all-to-all | bytes 212992 | tf_op jit(solution)/shard_map/cond/branch_1_fun/all_to_all | solution.py:395
  73.3 4.1 %branch_1_fun.10 = (bf16[512,128]{1,0:T(8,128)(2,1)S(1)}, bf16[512,128]{1,0:T(8,128)(2,1)S(1)}) custom-call(f32[6]{0:T(128)S(1)} %get-tuple-element.54.scalars, f32[384,128]{1,0:T(8,128)S(1)} %get-tuple-element.63.weight_ref, bf16[512,256]{1,0:T(8,128)(2,1)S(1)} %get-tuple-element.64.norm_ref, bf16[3,512,128]{2,1,0:T(8,128)(2,1)} %get-tuple-element.61.other_ref, ...), custom_call_target="tpu_custom_call" | custom-call | flops 4000000000 | bytes 2097152 | tf_op jit(solution)/shard_map/cond/branch_1_fun/pallas_call | solution.py:383
  77.4 1.9 %collective-permute-start.3 = (bf16[512,128]{1,0:T(8,128)(2,1)S(1)}, bf16[512,128]{1,0:T(8,128)(2,1)S(1)}, u32[]{:S(2)}, u32[]{:S(2)}) collective-permute-start(bf16[512,128]{1,0:T(8,128)(2,1)S(1)} %get-tuple-element.67), channel_id=1, source_target_pairs={{256,272},{272,256},{288,304},{304,288},{320,336},{336,320},{352,3... | collective-permute-start | bytes 393224 | tf_op jit(solution)/shard_map/cond/branch_1_fun/ppermute | solution.py:557
  79.3 1.3 %collective-permute-done.3.back_ref = bf16[512,128]{1,0:T(8,128)(2,1)S(1)} collective-permute-done((bf16[512,128]{1,0:T(8,128)(2,1)S(1)}, bf16[512,128]{1,0:T(8,128)(2,1)S(1)}, u32[]{:S(2)}, u32[]{:S(2)}) %collective-permute-start.3) | collective-permute-done | bytes 131104 | tf_op jit(solution)/shard_map/cond/branch_1_fun/ppermute | solution.py:557
  80.6 0.9 branch_1_fun.11
  81.7 14.5 %all_to_all.32 = f32[16,1,512]{2,1,0:T(1,128)S(1)} all-to-all(f32[16,1,512]{2,1,0:T(1,128)S(1)} %broadcast_in_dim.52), channel_id=1, replica_groups=mesh['frame'=32,'head'=16] {'head'}, dimensions={0} | all-to-all | bytes 65536 | tf_op jit(solution)/shard_map/all_to_all | solution.py:602
  96.1 0.0 copy-done
  96.1 1.0 %shard_map.94 = bf16[512,256]{1,0:T(8,128)(2,1)} custom-call(f32[16,512]{1,0:T(8,128)S(1)} %bitcast.25, f32[512,256]{1,0:T(8,128)S(1)} %get-tuple-element.101.refs_1_, f32[1,256]{1,0:T(1,128)S(1)} %bitcast.26), custom_call_target="tpu_custom_call" | custom-call | bytes 2097152 | tf_op jit(solution)/shard_map/pallas_call | solution.py:383
  (19 shorter events, 0.2 us)
Async XLA Ops:
  0.0 7.9 %collective-permute-start.4 = (bf16[512,256]{1,0:T(8,128)(2,1)}, bf16[512,256]{1,0:T(8,128)(2,1)S(1)}, u32[]{:S(2)}, u32[]{:S(2)}) collective-permute-start(bf16[512,256]{1,0:T(8,128)(2,1)} %k_hbm.1), channel_id=1, source_target_pairs={{0,16},{16,32},{32,48},{48,64},{64,80},{80,96},{96,112},{112,128},... | collective-permute-start | bytes 786440 | tf_op jit(solution)/shard_map/ppermute | solution.py:430
  1.9 8.8 %collective-permute-start.5 = (bf16[512,256]{1,0:T(8,128)(2,1)}, bf16[512,256]{1,0:T(8,128)(2,1)S(1)}, u32[]{:S(2)}, u32[]{:S(2)}) collective-permute-start(bf16[512,256]{1,0:T(8,128)(2,1)} %v_hbm.1), channel_id=1, source_target_pairs={{0,16},{16,32},{32,48},{48,64},{64,80},{80,96},{96,112},{112,128},... | collective-permute-start | bytes 786440 | tf_op jit(solution)/shard_map/ppermute | solution.py:431
  5.0 2.2 %copy-start.1 = (f32[2]{0:T(128)S(1)}, f32[2]{0:T(128)}, u32[]{:S(2)}) copy-start(f32[2]{0:T(128)} %param.20) | copy-start | bytes 28
  5.1 2.2 %copy-start.2 = (f32[2]{0:T(128)S(1)}, f32[2]{0:T(128)}, u32[]{:S(2)}) copy-start(f32[2]{0:T(128)} %param.19) | copy-start | bytes 28
  12.6 3.7 %collective-permute-start = (bf16[3,512,128]{2,1,0:T(8,128)(2,1)S(1)}, bf16[3,512,128]{2,1,0:T(8,128)(2,1)}, u32[]{:S(2)}, u32[]{:S(2)}) collective-permute-start(bf16[3,512,128]{2,1,0:T(8,128)(2,1)S(1)} %slice_select_fusion), channel_id=1, source_target_pairs={{256,272},{272,256},{288,304},{304,288},{320,336},{336,320},{352,3... | collective-permute-start | bytes 1179656 | tf_op jit(solution)/shard_map/cond/branch_1_fun/ppermute | solution.py:499
  16.4 17.8 %collective-permute-start.6 = (f16[104,128]{1,0:T(8,128)(2,1)S(1)}, f16[104,128]{1,0:T(8,128)(2,1)S(1)}, u32[]{:S(2)}, u32[]{:S(2)}) collective-permute-start(f16[104,128]{1,0:T(8,128)(2,1)S(1)} %get-tuple-element.97), channel_id=1, source_target_pairs={{192,384},{0,320},{208,400},{16,336},{224,416},{32,352},{240,432},... | collective-permute-start | bytes 79880 | tf_op jit(solution)/shard_map/ppermute | solution.py:510
  17.7 16.5 %collective-permute-start.7 = (f16[104,128]{1,0:T(8,128)(2,1)S(1)}, f16[104,128]{1,0:T(8,128)(2,1)S(1)}, u32[]{:S(2)}, u32[]{:S(2)}) collective-permute-start(f16[104,128]{1,0:T(8,128)(2,1)S(1)} %get-tuple-element.97), channel_id=1, source_target_pairs={{192,320},{0,384},{208,336},{16,400},{224,352},{32,416},{240,368},... | collective-permute-start | bytes 79880 | tf_op jit(solution)/shard_map/ppermute | solution.py:510
  34.2 61.9 %copy-start = (f32[256]{0:T(256)S(1)}, f32[256]{0:T(256)}, u32[]{:S(2)}) copy-start(f32[256]{0:T(256)} %param.21) | copy-start | bytes 3076
  55.2 9.7 %collective-permute-start.2 = (f16[104,128]{1,0:T(8,128)(2,1)S(1)}, f16[104,128]{1,0:T(8,128)(2,1)S(1)}, u32[]{:S(2)}, u32[]{:S(2)}) collective-permute-start(f16[104,128]{1,0:T(8,128)(2,1)S(1)} %convert_element_type.48), channel_id=1, source_target_pairs={{256,384},{272,400},{288,416},{304,432},{320,448},{336,464},{352,4... | collective-permute-start | bytes 79880 | tf_op jit(solution)/shard_map/cond/branch_1_fun/ppermute | solution.py:543
  77.4 3.2 %collective-permute-start.3 = (bf16[512,128]{1,0:T(8,128)(2,1)S(1)}, bf16[512,128]{1,0:T(8,128)(2,1)S(1)}, u32[]{:S(2)}, u32[]{:S(2)}) collective-permute-start(bf16[512,128]{1,0:T(8,128)(2,1)S(1)} %get-tuple-element.67), channel_id=1, source_target_pairs={{256,272},{272,256},{288,304},{304,288},{320,336},{336,320},{352,3... | collective-permute-start | bytes 393224 | tf_op jit(solution)/shard_map/cond/branch_1_fun/ppermute | solution.py:557

commit v10 on v9

--- a/solution.py
+++ b/solution.py
@@ -507,7 +507,7 @@
     shorter = [pair for a, b, c, d in far_groups for pair in ((b, c), (a, d))]
     halves = [pair for a, b, _, _ in far_groups for pair in ((a, b), (b, a))]
     leaving = part.astype(f16)
-    far_parts = [lax.ppermute(leaving, "frame", route) for route in (longer, shorter)]
+    far_parts = [lax.ppermute(leaving, "frame", route) for route in (shorter, longer)]
     results = [((frame_len, width), f32), ((8, frame_len), f32)]
     quarter = near // heads
 

time: 97.6 us -> 96.4 us (0.988)
  waiting for transfers between devices: 25.2 us -> 23.4 us
    ppermute x2, waiting for transfers between devices: 15.2 us -> 14.1 us  [shards(): lax.ppermute(leaving, 'frame', route)]
  transfers between devices with their start and end apart: 7 -> 7, of which waited for: 6 -> 7; matrix products, arithmetic and copies ran while one was open for 0% -> 0% of each run, Pallas kernels for 4% -> 4%
where the time goes in v10:
time: 96.4 us; the launch traced here: 95.9 us
  blocking collectives  38.9 us (40%)
  waiting for transfers between devices  23.4 us (24%)
  Pallas kernels  16.6 us (17%)
  starting transfers between devices  16.2 us (17%)
    all_to_all x3, blocking collectives, exchange(): lax.all_to_all(array, 'frame', split_axis=0, concat_axis=0, tiled=True, a...  24.4 us
    pallas_call x10, Pallas kernels, call(): pl.pallas_call(kernel, out_shape=shapes, in_specs=first + [spec] * (len(a...  16.6 us
    all_to_all x1, blocking collectives, shards(): lax.all_to_all(jnp.broadcast_to(square[:1], (columns, frame_len)), 'head'...  14.4 us
    ppermute x2, waiting for transfers between devices, shards(): lax.ppermute(leaving, 'frame', route)  14.1 us
    ppermute x1, waiting for transfers between devices, with_second_sum(): other = lax.ppermute(part.astype(f16), 'frame', pairs).astype(f32)  4.9 us
    ppermute x1, starting transfers between devices, with_second_sum(): other = lax.ppermute(part.astype(f16), 'frame', pairs).astype(f32)  4.84 us
    ppermute x1, starting transfers between devices, shards(): values_prev = lax.ppermute(values, 'frame', route)  3.03 us
    ppermute x2, starting transfers between devices, shards(): lax.ppermute(leaving, 'frame', route)  2.58 us
  transfers between devices with their start and end apart: 7, of which 7 were waited for; matrix products, arithmetic and copies ran while one was open for 0% of the time, Pallas kernels for 4%

profile of v10, /device:TPU:416, one launch (start us, length us, event | category | flops | bytes accessed | tf_op | source)
XLA Modules:
  0.0 95.9 jit_solution(12592627320619256169)
XLA Ops:
  0.0 1.9 %collective-permute-start.4 = (bf16[512,256]{1,0:T(8,128)(2,1)}, bf16[512,256]{1,0:T(8,128)(2,1)S(1)}, u32[]{:S(2)}, u32[]{:S(2)}) collective-permute-start(bf16[512,256]{1,0:T(8,128)(2,1)} %k_hbm.1), channel_id=1, source_target_pairs={{0,16},{16,32},{32,48},{48,64},{64,80},{80,96},{96,112},{112,128},... | collective-permute-start | bytes 786440 | tf_op jit(solution)/shard_map/ppermute | solution.py:430
  1.9 3.0 %collective-permute-start.5 = (bf16[512,256]{1,0:T(8,128)(2,1)}, bf16[512,256]{1,0:T(8,128)(2,1)S(1)}, u32[]{:S(2)}, u32[]{:S(2)}) collective-permute-start(bf16[512,256]{1,0:T(8,128)(2,1)} %v_hbm.1), channel_id=1, source_target_pairs={{0,16},{16,32},{32,48},{48,64},{64,80},{80,96},{96,112},{112,128},... | collective-permute-start | bytes 786440 | tf_op jit(solution)/shard_map/ppermute | solution.py:431
  5.0 0.1 add_convert_fusion
  5.0 0.0 copy-start.1
  5.1 0.0 copy-start.2
  5.1 2.2 %shard_map.91 = (bf16[512,256]{1,0:T(8,128)(2,1)S(1)}, bf16[512,256]{1,0:T(8,128)(2,1)S(1)}, bf16[512,256]{1,0:T(8,128)(2,1)S(1)}, bf16[2,128,512]{2,1,0:T(8,128...) custom-call(bf16[512,256]{1,0:T(8,128)(2,1)} %q_hbm.1, ...), custom_call_target="tpu_custom_call" | custom-call | flops 2000000000 | bytes 2097152 | tf_op jit(solution)/shard_map/pallas_call | solution.py:383
  7.3 0.0 copy-done.1
  7.3 0.0 copy-done.2
  7.3 0.1 pad_maximum_fusion.1.scalars
  7.4 0.5 collective-permute-done.4.past_ref
  7.9 2.0 %shard_map.92 = (bf16[2,512,512]{2,1,0:T(8,128)(2,1)S(1)}, f32[2,128,512]{2,1,0:T(8,128)S(1)}) custom-call(f32[6]{0:T(128)S(1)} %pad_maximum_fusion.1.scalars, bf16[512,256]{1,0:T(8,128)(2,1)S(1)} %get-tuple-element.85.q_ref, bf16[512,256]{1,0:T(8,128)(2,1)S(1)} %collective-permute-done.4.past_ref, f32[2,512,512]{2,1,0:T(8,128)S(1)} %get-tuple-element.86.prob_ref, ...), custom_call_target="tpu_custom_call" | custom-call | flops 2000000000 | bytes 2097152 | tf_op jit(solution)/shard_map/pallas_call | solution.py:383
  9.9 0.8 collective-permute-done.5.past_ref
  10.7 1.7 %shard_map.93 = (bf16[512,256]{1,0:T(8,128)(2,1)S(1)}, bf16[2,128,512]{2,1,0:T(8,128)(2,1)S(1)}, f32[8,104,128]{2,1,0:T(8,128)S(1)}) custom-call(bf16[2,512,512]{2,1,0:T(8,128)(2,1)S(1)} %get-tuple-element.89.share_ref, f32[2,128,512]{2,1,0:T(8,128)S(1)} %get-tuple-element.90.mixed_ref, bf16[512,256]{1,0:T(8,128)(2,1)S(1)} %collective-permute-done.5.past_ref, ...), custom_call_target="tpu_custom_call" | custom-call | flops 3000000000 | bytes 2097152 | tf_op jit(solution)/shard_map/pallas_call | solution.py:383
  12.4 3.9 %conditional.2 = (f32[104,128]{1,0:T(8,128)S(1)}, bf16[3,512,128]{2,1,0:T(8,128)(2,1)}, f16[104,128]{1,0:T(8,128)(2,1)S(1)}) conditional(s32[]{:T(128)} %convert_element_type.53, f32[8,104,128]{2,1,0:T(8,128)S(1)} %get-tuple-element.93, (s32[]{:T(128)}, bf16[512,256]{1,0:T(8,128)(2,1)S(1)}, bf16[512,256]{1,0:T(8,128)(2,1)S(1)}, ...), branch_computations={%region_0.1_spmd, %region_1.2_spmd} | conditional | flops 983041 | bytes 6191160 | solution.py:505
  12.5 0.1 pad_maximum_fusion
  12.6 0.1 slice_select_fusion
  12.6 1.9 %collective-permute-start = (bf16[3,512,128]{2,1,0:T(8,128)(2,1)S(1)}, bf16[3,512,128]{2,1,0:T(8,128)(2,1)}, u32[]{:S(2)}, u32[]{:S(2)}) collective-permute-start(bf16[3,512,128]{2,1,0:T(8,128)(2,1)S(1)} %slice_select_fusion), channel_id=1, source_target_pairs={{256,272},{272,256},{288,304},{304,288},{320,336},{336,320},{352,3... | collective-permute-start | bytes 1179656 | tf_op jit(solution)/shard_map/cond/branch_1_fun/ppermute | solution.py:499
  14.5 1.8 %collective-permute-done = bf16[3,512,128]{2,1,0:T(8,128)(2,1)} collective-permute-done((bf16[3,512,128]{2,1,0:T(8,128)(2,1)S(1)}, bf16[3,512,128]{2,1,0:T(8,128)(2,1)}, u32[]{:S(2)}, u32[]{:S(2)}) %collective-permute-start) | collective-permute-done | bytes 393248 | tf_op jit(solution)/shard_map/cond/branch_1_fun/ppermute | solution.py:499
  16.4 1.3 %collective-permute-start.6 = (f16[104,128]{1,0:T(8,128)(2,1)S(1)}, f16[104,128]{1,0:T(8,128)(2,1)S(1)}, u32[]{:S(2)}, u32[]{:S(2)}) collective-permute-start(f16[104,128]{1,0:T(8,128)(2,1)S(1)} %get-tuple-element.97), channel_id=1, source_target_pairs={{192,320},{0,384},{208,336},{16,400},{224,352},{32,416},{240,368},... | collective-permute-start | bytes 79880 | tf_op jit(solution)/shard_map/ppermute | solution.py:510
  17.7 1.3 %collective-permute-start.7 = (f16[104,128]{1,0:T(8,128)(2,1)S(1)}, f16[104,128]{1,0:T(8,128)(2,1)S(1)}, u32[]{:S(2)}, u32[]{:S(2)}) collective-permute-start(f16[104,128]{1,0:T(8,128)(2,1)S(1)} %get-tuple-element.97), channel_id=1, source_target_pairs={{192,384},{0,320},{208,400},{16,336},{224,416},{32,352},{240,432},... | collective-permute-start | bytes 79880 | tf_op jit(solution)/shard_map/ppermute | solution.py:510
  19.0 7.3 %collective-permute-done.6 = f16[104,128]{1,0:T(8,128)(2,1)S(1)} collective-permute-done((f16[104,128]{1,0:T(8,128)(2,1)S(1)}, f16[104,128]{1,0:T(8,128)(2,1)S(1)}, u32[]{:S(2)}, u32[]{:S(2)}) %collective-permute-start.6) | collective-permute-done | bytes 26656 | tf_op jit(solution)/shard_map/ppermute | solution.py:510
  26.2 6.8 %collective-permute-done.7 = f16[104,128]{1,0:T(8,128)(2,1)S(1)} collective-permute-done((f16[104,128]{1,0:T(8,128)(2,1)S(1)}, f16[104,128]{1,0:T(8,128)(2,1)S(1)}, u32[]{:S(2)}, u32[]{:S(2)}) %collective-permute-start.7) | collective-permute-done | bytes 26656 | tf_op jit(solution)/shard_map/ppermute | solution.py:510
  33.0 0.0 copy-start
  33.0 47.4 %conditional.3 = ((f32[512,256]{1,0:T(8,128)S(1)}, f32[8,512]{1,0:T(8,128)S(1)})) conditional(s32[]{:T(128)} %convert_element_type.53, (f32[104,128]{1,0:T(8,128)S(1)}, f32[6]{0:T(128)S(1)}, bf16[512,256]{1,0:T(8,128)(2,1)S(1)}, bf16[512,256]{1,0:T(8,128)(2,1)S(1)}, f32[6,128,128]{2,1,0:T(8,128)S(1)}) %tuple.22, (f16[104,128]{1,0:T(8,128)(2,1)S(1)}, ...), branch_computations={%region_2.3_spmd, %region_3.4_spmd} | conditional | flops 8100292608 | bytes 15876184 | solution.py:586
  33.1 8.1 %all_to_all.29 = f16[4,104,128]{2,1,0:T(8,128)(2,1)S(1)} all-to-all(f16[4,104,128]{2,1,0:T(8,128)(2,1)S(1)} %broadcast_in_dim.45), channel_id=1, replica_groups={{0,32,64,96},{16,48,80,112},{192,224,128,160},{208,240,144,176},{320,35..., dimensions={0} | all-to-all | bytes 212992 | tf_op jit(solution)/shard_map/cond/branch_1_fun/all_to_all | solution.py:395
  41.2 4.6 %branch_1_fun.7 = (f32[384,128]{1,0:T(8,128)S(1)}, f32[4,104,128]{2,1,0:T(8,128)S(1)}) custom-call(f32[6]{0:T(128)S(1)} %get-tuple-element.54.scalars, f32[4,104,128]{2,1,0:T(8,128)S(1)} %convert_element_type.45.total_ref, bf16[512,256]{1,0:T(8,128)(2,1)S(1)} %get-tuple-element.55.att_ref, bf16[2,128,512]{2,1,0:T(8,128)(2,1)S(1)} %get-tuple-element.58.att_t_ref, ...), custom_call_target="tpu_custom_call" | custom-call | flops 4000000000 | bytes 2097152 | tf_op jit(solution)/shard_map/cond/branch_1_fun/pallas_call | solution.py:383
  45.8 8.2 %all_to_all.30 = f16[4,104,128]{2,1,0:T(8,128)(2,1)S(1)} all-to-all(f16[4,104,128]{2,1,0:T(8,128)(2,1)S(1)} %convert_element_type.46), channel_id=1, replica_groups={{0,32,64,96},{16,48,80,112},{128,160,192,224},{144,176,208,240},{256,28..., dimensions={0} | all-to-all | bytes 212992 | tf_op jit(solution)/shard_map/cond/branch_1_fun/all_to_all | solution.py:395
  54.1 4.8 %collective-permute-start.2 = (f16[104,128]{1,0:T(8,128)(2,1)S(1)}, f16[104,128]{1,0:T(8,128)(2,1)S(1)}, u32[]{:S(2)}, u32[]{:S(2)}) collective-permute-start(f16[104,128]{1,0:T(8,128)(2,1)S(1)} %convert_element_type.48), channel_id=1, source_target_pairs={{256,384},{272,400},{288,416},{304,432},{320,448},{336,464},{352,4... | collective-permute-start | bytes 79880 | tf_op jit(solution)/shard_map/cond/branch_1_fun/ppermute | solution.py:543
  59.0 4.9 %collective-permute-done.2 = f16[104,128]{1,0:T(8,128)(2,1)S(1)} collective-permute-done((f16[104,128]{1,0:T(8,128)(2,1)S(1)}, f16[104,128]{1,0:T(8,128)(2,1)S(1)}, u32[]{:S(2)}, u32[]{:S(2)}) %collective-permute-start.2) | collective-permute-done | bytes 26656 | tf_op jit(solution)/shard_map/cond/branch_1_fun/ppermute | solution.py:543
  63.9 8.1 %all_to_all.31 = f16[4,104,128]{2,1,0:T(8,128)(2,1)S(1)} all-to-all(f16[4,104,128]{2,1,0:T(8,128)(2,1)S(1)} %broadcast_in_dim.49), channel_id=1, replica_groups={{0,32,64,96},{16,48,80,112},{128,160,192,224},{144,176,208,240},{256,28..., dimensions={0} | all-to-all | bytes 212992 | tf_op jit(solution)/shard_map/cond/branch_1_fun/all_to_all | solution.py:395
  72.1 4.1 %branch_1_fun.10 = (bf16[512,128]{1,0:T(8,128)(2,1)S(1)}, bf16[512,128]{1,0:T(8,128)(2,1)S(1)}) custom-call(f32[6]{0:T(128)S(1)} %get-tuple-element.54.scalars, f32[384,128]{1,0:T(8,128)S(1)} %get-tuple-element.63.weight_ref, bf16[512,256]{1,0:T(8,128)(2,1)S(1)} %get-tuple-element.64.norm_ref, bf16[3,512,128]{2,1,0:T(8,128)(2,1)} %get-tuple-element.61.other_ref, ...), custom_call_target="tpu_custom_call" | custom-call | flops 4000000000 | bytes 2097152 | tf_op jit(solution)/shard_map/cond/branch_1_fun/pallas_call | solution.py:383
  76.2 1.9 %collective-permute-start.3 = (bf16[512,128]{1,0:T(8,128)(2,1)S(1)}, bf16[512,128]{1,0:T(8,128)(2,1)S(1)}, u32[]{:S(2)}, u32[]{:S(2)}) collective-permute-start(bf16[512,128]{1,0:T(8,128)(2,1)S(1)} %get-tuple-element.67), channel_id=1, source_target_pairs={{256,272},{272,256},{288,304},{304,288},{320,336},{336,320},{352,3... | collective-permute-start | bytes 393224 | tf_op jit(solution)/shard_map/cond/branch_1_fun/ppermute | solution.py:557
  78.1 1.3 %collective-permute-done.3.back_ref = bf16[512,128]{1,0:T(8,128)(2,1)S(1)} collective-permute-done((bf16[512,128]{1,0:T(8,128)(2,1)S(1)}, bf16[512,128]{1,0:T(8,128)(2,1)S(1)}, u32[]{:S(2)}, u32[]{:S(2)}) %collective-permute-start.3) | collective-permute-done | bytes 131104 | tf_op jit(solution)/shard_map/cond/branch_1_fun/ppermute | solution.py:557
  79.5 0.9 branch_1_fun.11
  80.5 14.4 %all_to_all.32 = f32[16,1,512]{2,1,0:T(1,128)S(1)} all-to-all(f32[16,1,512]{2,1,0:T(1,128)S(1)} %broadcast_in_dim.52), channel_id=1, replica_groups=mesh['frame'=32,'head'=16] {'head'}, dimensions={0} | all-to-all | bytes 65536 | tf_op jit(solution)/shard_map/all_to_all | solution.py:602
  94.9 0.0 copy-done
  94.9 1.0 %shard_map.94 = bf16[512,256]{1,0:T(8,128)(2,1)} custom-call(f32[16,512]{1,0:T(8,128)S(1)} %bitcast.25, f32[512,256]{1,0:T(8,128)S(1)} %get-tuple-element.101.refs_1_, f32[1,256]{1,0:T(1,128)S(1)} %bitcast.26), custom_call_target="tpu_custom_call" | custom-call | bytes 2097152 | tf_op jit(solution)/shard_map/pallas_call | solution.py:383
  (19 shorter events, 0.2 us)
Async XLA Ops:
  0.0 7.9 %collective-permute-start.4 = (bf16[512,256]{1,0:T(8,128)(2,1)}, bf16[512,256]{1,0:T(8,128)(2,1)S(1)}, u32[]{:S(2)}, u32[]{:S(2)}) collective-permute-start(bf16[512,256]{1,0:T(8,128)(2,1)} %k_hbm.1), channel_id=1, source_target_pairs={{0,16},{16,32},{32,48},{48,64},{64,80},{80,96},{96,112},{112,128},... | collective-permute-start | bytes 786440 | tf_op jit(solution)/shard_map/ppermute | solution.py:430
  1.9 8.8 %collective-permute-start.5 = (bf16[512,256]{1,0:T(8,128)(2,1)}, bf16[512,256]{1,0:T(8,128)(2,1)S(1)}, u32[]{:S(2)}, u32[]{:S(2)}) collective-permute-start(bf16[512,256]{1,0:T(8,128)(2,1)} %v_hbm.1), channel_id=1, source_target_pairs={{0,16},{16,32},{32,48},{48,64},{64,80},{80,96},{96,112},{112,128},... | collective-permute-start | bytes 786440 | tf_op jit(solution)/shard_map/ppermute | solution.py:431
  5.0 2.2 %copy-start.1 = (f32[2]{0:T(128)S(1)}, f32[2]{0:T(128)}, u32[]{:S(2)}) copy-start(f32[2]{0:T(128)} %param.20) | copy-start | bytes 28
  5.1 2.2 %copy-start.2 = (f32[2]{0:T(128)S(1)}, f32[2]{0:T(128)}, u32[]{:S(2)}) copy-start(f32[2]{0:T(128)} %param.19) | copy-start | bytes 28
  12.6 3.7 %collective-permute-start = (bf16[3,512,128]{2,1,0:T(8,128)(2,1)S(1)}, bf16[3,512,128]{2,1,0:T(8,128)(2,1)}, u32[]{:S(2)}, u32[]{:S(2)}) collective-permute-start(bf16[3,512,128]{2,1,0:T(8,128)(2,1)S(1)} %slice_select_fusion), channel_id=1, source_target_pairs={{256,272},{272,256},{288,304},{304,288},{320,336},{336,320},{352,3... | collective-permute-start | bytes 1179656 | tf_op jit(solution)/shard_map/cond/branch_1_fun/ppermute | solution.py:499
  16.4 9.9 %collective-permute-start.6 = (f16[104,128]{1,0:T(8,128)(2,1)S(1)}, f16[104,128]{1,0:T(8,128)(2,1)S(1)}, u32[]{:S(2)}, u32[]{:S(2)}) collective-permute-start(f16[104,128]{1,0:T(8,128)(2,1)S(1)} %get-tuple-element.97), channel_id=1, source_target_pairs={{192,320},{0,384},{208,336},{16,400},{224,352},{32,416},{240,368},... | collective-permute-start | bytes 79880 | tf_op jit(solution)/shard_map/ppermute | solution.py:510
  17.7 15.4 %collective-permute-start.7 = (f16[104,128]{1,0:T(8,128)(2,1)S(1)}, f16[104,128]{1,0:T(8,128)(2,1)S(1)}, u32[]{:S(2)}, u32[]{:S(2)}) collective-permute-start(f16[104,128]{1,0:T(8,128)(2,1)S(1)} %get-tuple-element.97), channel_id=1, source_target_pairs={{192,384},{0,320},{208,400},{16,336},{224,416},{32,352},{240,432},... | collective-permute-start | bytes 79880 | tf_op jit(solution)/shard_map/ppermute | solution.py:510
  33.0 61.9 %copy-start = (f32[256]{0:T(256)S(1)}, f32[256]{0:T(256)}, u32[]{:S(2)}) copy-start(f32[256]{0:T(256)} %param.21) | copy-start | bytes 3076
  54.1 9.8 %collective-permute-start.2 = (f16[104,128]{1,0:T(8,128)(2,1)S(1)}, f16[104,128]{1,0:T(8,128)(2,1)S(1)}, u32[]{:S(2)}, u32[]{:S(2)}) collective-permute-start(f16[104,128]{1,0:T(8,128)(2,1)S(1)} %convert_element_type.48), channel_id=1, source_target_pairs={{256,384},{272,400},{288,416},{304,432},{320,448},{336,464},{352,4... | collective-permute-start | bytes 79880 | tf_op jit(solution)/shard_map/cond/branch_1_fun/ppermute | solution.py:543
  76.2 3.2 %collective-permute-start.3 = (bf16[512,128]{1,0:T(8,128)(2,1)S(1)}, bf16[512,128]{1,0:T(8,128)(2,1)S(1)}, u32[]{:S(2)}, u32[]{:S(2)}) collective-permute-start(bf16[512,128]{1,0:T(8,128)(2,1)S(1)} %get-tuple-element.67), channel_id=1, source_target_pairs={{256,272},{272,256},{288,304},{304,288},{320,336},{336,320},{352,3... | collective-permute-start | bytes 393224 | tf_op jit(solution)/shard_map/cond/branch_1_fun/ppermute | solution.py:557
